TPU v7x, 32 devices: a whole 2x2x4 slice. The times are simulated.
32 devices in a mesh: pipe: 4 (over y, x), seq: 8 (over z, core).
Axes of the slice: x: 2, y: 2, z: 4, core: 2. Of those that a mesh axis runs over, the one named last changes fastest.
Arguments:
- query_rows: bfloat16 [4, 1024, 1536], P('pipe', 'seq'), may hold values from -6 to 6
- key_rows: bfloat16 [4, 1024, 1536], P('pipe', 'seq'), may hold values from -6 to 6
- value_rows: bfloat16 [4, 1024, 1536], P('pipe', 'seq'), may hold values from -6 to 6
- query_weight: bfloat16 [4, 1536, 1536], P('pipe'), may hold values from -0.15625 to 0.15625
- key_weight: bfloat16 [4, 1536, 1536], P('pipe'), may hold values from -0.15625 to 0.15625
- value_weight: bfloat16 [4, 1536, 1536], P('pipe'), may hold values from -0.15625 to 0.15625
- out_weight: bfloat16 [4, 1536, 1536], P('pipe'), may hold values from -0.15625 to 0.15625
- upstream: bfloat16 [1024, 1536], P('seq'), may hold values from -6 to 6
- window: int32 [8, 12, 2], replicated, may hold values from 0 to 1, as said below
Outputs:
- gradients: bfloat16 [4, 1024, 1536], P('pipe', 'seq')
Inputs may be any that keep to these rules, and one draw needn't show every extreme that they name: window[i, h, 0] is 0 where i % 4 == 3, and window[i, h, 1] is 0 where i % 4 == 2.
All inputs are finite; a program needn't handle non-finite values.
Results may differ from a plain program's by a relative error of at most 0.02.
Values may be sent and summed in bfloat16 or wider, within the bound.
No kernel may reach another device: no remote copies, remote signals or barrier semaphores. Data moves between devices by JAX's collectives and lax.ppermute only.
A program may use at most 128 MiB of HBM per device.

v0:
```python
import functools

import jax
import jax.numpy as jnp
from jax import lax
from jax.experimental import pallas as pl
from jax.experimental.pallas import tpu as pltpu
from jax.sharding import PartitionSpec as P

HEAD_DIM = 128
TILE = 128
MIB = 1 << 20


def dot_nt(a, b):
    return lax.dot_general(a, b, (((1,), (1,)), ((), ())), preferred_element_type=jnp.float32)


def dot_nn(a, b):
    return lax.dot_general(a, b, (((1,), (0,)), ((), ())), preferred_element_type=jnp.float32)


def pair_cols(g):
    return pl.ds(g * 2 * HEAD_DIM, 2 * HEAD_DIM)


def put_diagonal(target, g, value):
    target[g, pl.ds(0, TILE), pl.ds(0, HEAD_DIM)] = value[:, :HEAD_DIM]
    target[g, pl.ds(TILE, TILE), pl.ds(HEAD_DIM, HEAD_DIM)] = value[:, HEAD_DIM:]


def prep_kernel(
    wo_hbm,
    wk_hbm,
    wv_hbm,
    wq_hbm,
    q_hbm,
    k_hbm,
    v_hbm,
    x_hbm,
    window,
    wot,
    wkt,
    wvt,
    wqt,
    q,
    k,
    v,
    x,
    qbd,
    keep,
    raw,
    flags,
    sems,
):
    groups = 4
    rows = raw.shape[1] // groups
    small = [
        pltpu.make_async_copy(src, dst, sems.at[n])
        for n, (src, dst) in enumerate(((q_hbm, q), (k_hbm, k), (v_hbm, v), (x_hbm, x)))
    ]
    sources = (wo_hbm, wk_hbm, wv_hbm, wq_hbm)

    def large(n, g):
        part = pl.ds(g * rows, rows)
        return pltpu.make_async_copy(
            sources[n].at[part], raw.at[n, part], sems.at[4 + n * groups + g]
        )

    window_copy = pltpu.make_async_copy(window, flags, sems.at[20])
    window_copy.start()
    for copy in small:
        copy.start()
    for n in range(len(sources)):
        for g in range(groups):
            large(n, g).start()
    qbd[...] = jnp.zeros_like(qbd)
    for copy in small:
        copy.wait()
    for g in range(qbd.shape[0]):
        put_diagonal(qbd, g, q[:, pair_cols(g)])
    for n, dst in enumerate((wot, wkt, wvt, wqt)):

        @pl.loop(0, groups)
        def _(g, n=n, dst=dst):
            start = pl.multiple_of(g * rows, rows)
            large(n, g).wait()
            for r in range(0, rows, TILE):
                part = pl.ds(start + r, TILE)
                dst[:, part] = raw[n, part, :].T
    window_copy.wait()
    tile = lax.axis_index("seq")
    odd = lax.rem(tile, 2)
    lane = lax.broadcasted_iota(jnp.int32, keep.shape[2:], 1)
    for b, side in enumerate((1 - odd, odd)):
        for g in range(keep.shape[1]):
            keep[b, g] = jnp.where(
                lane < TILE, flags[tile, side, 2 * g], flags[tile, side, 2 * g + 1]
            )


def prob_kernel(scaling, keep, qbd, k0, k1, k2, after, pt_ref, kt_ref, scores):
    pairs = pt_ref.shape[0]
    for g in range(pairs):
        cols = pair_cols(g)
        keys = jnp.concatenate([k0[:, cols], k1[:, cols], k2[:, cols]], axis=0)
        scores[g] = dot_nt(keys, qbd[g])
        for b, k_ref in enumerate((k0, k1, k2)):
            for n in range(2):
                h = 2 * g + n
                part = k_ref[:, pl.ds(h * HEAD_DIM, HEAD_DIM)]
                kt_ref[h, :, pl.ds(b * TILE, TILE)] = part.T
    for g in range(pairs):
        parts = []
        for b in range(3):
            s = scaling * scores[g, pl.ds(b * TILE, TILE)]
            if b > 0:
                s = jnp.where(keep[b - 1, g, 0:1] > 0, s, -jnp.inf)
            parts.append(s)
        top = jnp.maximum(jnp.maximum(parts[0], parts[1]), parts[2])
        top = jnp.max(top, axis=0, keepdims=True)
        weights = [jnp.exp(s - top) for s in parts]
        total = jnp.sum(weights[0] + weights[1] + weights[2], axis=0, keepdims=True)
        scale = 1.0 / total
        for b, w in enumerate(weights):
            pt_ref[g, pl.ds(b * TILE, TILE), :] = (w * scale).astype(jnp.bfloat16)


def out_kernel(pt, q, v0, v1, v2, after, pon_ref, pof_ref):
    for g in range(pt.shape[0]):
        pon_ref[g, :TILE] = pt[g, TILE : 2 * TILE]
        pof_ref[g, :TILE] = pt[g, 2 * TILE :]
        for n in range(2):
            cols = pl.ds((2 * g + n) * HEAD_DIM, HEAD_DIM)
            lanes = pl.ds(n * HEAD_DIM, HEAD_DIM)
            values = jnp.concatenate([v0[:, cols], v1[:, cols], v2[:, cols]], axis=0)
            out = dot_nn(pt[g, :, lanes].T, values).astype(jnp.bfloat16)
            pon_ref[g, pl.ds(TILE, TILE), lanes] = out
            pof_ref[g, pl.ds(TILE, TILE), lanes] = out
        queries = q[:, pair_cols(g)]
        pon_ref[g, 2 * TILE :] = queries
        pof_ref[g, 2 * TILE :] = queries


def turn_kernel(po, qbd):
    qbd[...] = jnp.zeros_like(qbd)
    for g in range(qbd.shape[0]):
        put_diagonal(qbd, g, po[g, 2 * TILE :])


def mark_kernel(*refs):
    refs[-1][...] = jnp.zeros_like(refs[-1])


def begin_kernel(xa_ref, wot, after, acc_ref, copy_ref):
    x = xa_ref[...]
    copy_ref[...] = x
    acc_ref[...] = dot_nn(x, wot[: x.shape[1], :])


def fill_diagonal(bd, wot, x, acc_ref):
    bd[...] = jnp.zeros_like(bd)
    start = wot.shape[0] - x.shape[1]
    for g in range(bd.shape[0]):
        cols = pair_cols(g)
        d_out = dot_nn(x, wot[start:, cols])
        if acc_ref is not None:
            d_out = acc_ref[:, cols] + d_out
        put_diagonal(bd, g, d_out.astype(jnp.bfloat16))


def own_attention(scaling, bd, pt, v0, v1, v2, dp, ds_ref):
    for g in range(pt.shape[0]):
        cols = pair_cols(g)
        values = jnp.concatenate([v0[:, cols], v1[:, cols], v2[:, cols]], axis=0)
        dp[g] = dot_nt(values, bd[g])
    for g in range(pt.shape[0]):
        pf = pt[g].astype(jnp.float32)
        delta = jnp.sum(pf * dp[g], axis=0, keepdims=True)
        ds_ref[g] = (pf * ((dp[g] - delta) * scaling)).astype(jnp.bfloat16)


def put_dq(ds, kt, turned, dq):
    for h in range(kt.shape[0]):
        turned[h] = dot_nn(kt[h], ds[h // 2, :, pl.ds((h % 2) * TILE, TILE)])
    for h in range(kt.shape[0]):
        dq[:, pl.ds(h * HEAD_DIM, HEAD_DIM)] = turned[h].T.astype(jnp.bfloat16)


def project_pair(dk, dv, wkt, wvt, part):
    return dot_nn(dk[...], wkt[:, part]) + dot_nn(dv[...], wvt[:, part])


def first_far_kernel(
    last, scaling, x, wot, qbd, pt, v0, v1, v2, wkt, wvt, after, far_ref, ds_ref, bd, dk, dv, dp
):
    @pl.when(lax.axis_index("pipe") == last)
    def _():
        fill_diagonal(bd, wot, x[...], None)
        own_attention(scaling, bd, pt, v0, v1, v2, dp, ds_ref)
        for g in range(pt.shape[0]):
            cols = pair_cols(g)
            dv[:, cols] = dot_nn(pt[g, 2 * TILE :], bd[g]).astype(jnp.bfloat16)
            dk[:, cols] = dot_nn(ds_ref[g, 2 * TILE :], qbd[g]).astype(jnp.bfloat16)
        far_ref[...] = project_pair(dk, dv, wkt, wvt, slice(None)).astype(jnp.bfloat16)


def first_near_kernel(last, ds_ref, bd, qbd, pt, wkt, wvt, near_ref, dk, dv):
    @pl.when(lax.axis_index("pipe") == last)
    def _():
        for g in range(pt.shape[0]):
            cols = pair_cols(g)
            dv[:, cols] = dot_nn(pt[g, TILE : 2 * TILE], bd[g]).astype(jnp.bfloat16)
            dk[:, cols] = dot_nn(ds_ref[g, TILE : 2 * TILE], qbd[g]).astype(jnp.bfloat16)
        near_ref[...] = project_pair(dk, dv, wkt, wvt, slice(None)).astype(jnp.bfloat16)


def first_own_kernel(
    last, x, ds_ref, bd, qbd, pt, kt, wqt, wkt, wvt, after, base_ref, dq, dk, dv, turned
):
    @pl.when(lax.axis_index("pipe") == last)
    def _():
        for g in range(pt.shape[0]):
            cols = pair_cols(g)
            dv[:, cols] = dot_nn(pt[g, :TILE], bd[g]).astype(jnp.bfloat16)
            dk[:, cols] = dot_nn(ds_ref[g, :TILE], qbd[g]).astype(jnp.bfloat16)
        put_dq(ds_ref, kt, turned, dq)
        base = project_pair(dk, dv, wkt, wvt, slice(None)) + dot_nn(dq[...], wqt[...])
        base_ref[...] = base + x[...].astype(jnp.float32)


def first_sum_kernel(base, near, far, after, suma_ref, sumb_ref):
    total = base[...] + near[...].astype(jnp.float32) + far[...].astype(jnp.float32)
    total = total.astype(jnp.bfloat16)
    split = suma_ref.shape[1]
    suma_ref[...] = total[:, :split]
    sumb_ref[...] = total[:, split:]


def halo_attention(scaling, bd, po, v, both, ds_ref):
    for g in range(po.shape[0]):
        values = jnp.concatenate([v[:, pair_cols(g)], po[g, TILE : 2 * TILE]], axis=0)
        both[g] = dot_nt(values, bd[g])
    row = lax.broadcasted_iota(jnp.int32, (TILE, 2 * TILE), 0)
    col = lax.broadcasted_iota(jnp.int32, (TILE, 2 * TILE), 1)
    same = (row == col) | (row + TILE == col)
    for g in range(po.shape[0]):
        delta = jnp.sum(jnp.where(same, both[g, TILE:], 0.0), axis=0, keepdims=True)
        ds = po[g, :TILE].astype(jnp.float32) * ((both[g, :TILE] - delta) * scaling)
        ds_ref[g] = ds.astype(jnp.bfloat16)


def own_kernel(
    scaling,
    acc,
    xa,
    xb,
    wot,
    qbd,
    pt,
    kt,
    v0,
    v1,
    v2,
    wqt,
    dq,
    dk_ref,
    dv_ref,
    base_ref,
    bd,
    dp,
    ds,
    turned,
):
    fill_diagonal(bd, wot, xb[...], acc)
    own_attention(scaling, bd, pt, v0, v1, v2, dp, ds)
    for g in range(pt.shape[0]):
        cols = pair_cols(g)
        dv_ref[:, cols] = dot_nn(pt[g, :TILE], bd[g])
        dk_ref[:, cols] = dot_nn(ds[g, :TILE], qbd[g])
    put_dq(ds, kt, turned, dq)
    base_ref[...] = xa[...].astype(jnp.float32) + dot_nn(dq[...], wqt[:, : xa.shape[1]])


def near_kernel(
    scaling,
    xfa,
    xa,
    xb,
    wot,
    qbd,
    po,
    v,
    dk_in,
    dv_in,
    after,
    acc_ref,
    dk_ref,
    dv_ref,
    bd,
    both,
    ds,
):
    x = jnp.concatenate([xa[...], xb[...]], axis=1)
    fill_diagonal(bd, wot, x, None)
    halo_attention(scaling, bd, po, v, both, ds)
    for g in range(po.shape[0]):
        cols = pair_cols(g)
        dv_ref[:, cols] = dv_in[:, cols] + dot_nn(po[g, :TILE], bd[g])
        dk_ref[:, cols] = dk_in[:, cols] + dot_nn(ds[g], qbd[g])
    acc_ref[...] = dot_nn(xfa[...], wot[: xfa.shape[1], :])


def far_kernel(
    scaling,
    acc,
    xb,
    wot,
    qbd,
    po,
    v,
    dk_in,
    dv_in,
    base,
    wkt,
    wvt,
    sum_ref,
    dk_ref,
    dv_ref,
    bd,
    both,
    ds,
):
    fill_diagonal(bd, wot, xb[...], acc)
    halo_attention(scaling, bd, po, v, both, ds)
    for g in range(po.shape[0]):
        cols = pair_cols(g)
        dv = dv_in[:, cols] + dot_nn(po[g, :TILE], bd[g])
        dk = dk_in[:, cols] + dot_nn(ds[g], qbd[g])
        dv_ref[:, cols] = dv.astype(jnp.bfloat16)
        dk_ref[:, cols] = dk.astype(jnp.bfloat16)
    part = pl.ds(0, sum_ref.shape[1])
    total = base[...] + project_pair(dk_ref, dv_ref, wkt, wvt, part)
    sum_ref[...] = total.astype(jnp.bfloat16)


def last_columns(dk, dv, dq, own_x, wqt, wkt, wvt):
    rest = own_x.shape[1]
    part = pl.ds(wqt.shape[1] - rest, rest)
    total = own_x[...].astype(jnp.float32) + dot_nn(dq[...], wqt[:, part])
    total = total + project_pair(dk, dv, wkt, wvt, part)
    return total.astype(jnp.bfloat16)


def rest_kernel(dk, dv, dq, own_x, wqt, wkt, wvt, sum_ref):
    sum_ref[...] = last_columns(dk, dv, dq, own_x, wqt, wkt, wvt)


def finish_kernel(dk, dv, dq, own_x, wqt, wkt, wvt, *refs):
    done_refs, out_ref = refs[:-1], refs[-1]
    position = lax.axis_index("pipe")
    split = done_refs[0].shape[1]
    out_ref[:, :split] = done_refs[-1][...]
    out_ref[:, split:] = last_columns(dk, dv, dq, own_x, wqt, wkt, wvt)
    count = len(done_refs) // 2
    for step in range(count):

        @pl.when(position == count - step)
        def _():
            out_ref[:, :split] = done_refs[2 * step][...]
            out_ref[:, split:] = done_refs[2 * step + 1][...]


def body(
    query_rows,
    key_rows,
    value_rows,
    query_weight,
    key_weight,
    value_weight,
    out_weight,
    upstream,
    window,
):
    sections = lax.axis_size("pipe")
    seq_size = lax.axis_size("seq")
    rows, width = query_rows.shape[1:]
    model = out_weight.shape[2]
    split = model // 2
    heads = width // HEAD_DIM
    pairs = heads // 2
    scaling = HEAD_DIM ** (-0.5)
    near_pairs = [(i, i ^ 1) for i in range(seq_size)]
    far_pairs = [(i, i + 1) for i in range(1, seq_size - 1, 2)]
    far_pairs = far_pairs + [(j, i) for i, j in far_pairs]

    def near(value):
        return lax.ppermute(value, "seq", near_pairs)

    def far(value):
        return lax.ppermute(value, "seq", far_pairs)

    def far_within(value, columns):
        moves = [(c * seq_size + i, c * seq_size + j) for c in columns for i, j in far_pairs]
        return lax.ppermute(value, ("pipe", "seq"), moves)

    def hop(value, source):
        return lax.ppermute(value, "pipe", [(source, source - 1)])

    vmem = pl.BlockSpec(memory_space=pltpu.VMEM)
    anywhere = pl.BlockSpec(memory_space=pl.ANY)
    bf16, f32 = jnp.bfloat16, jnp.float32
    weight = pltpu.VMEM((model, width), bf16)
    block = (pairs, 2 * TILE, 2 * HEAD_DIM)
    tile = pltpu.VMEM((rows, width), bf16)
    wide = pltpu.VMEM((rows, width), f32)
    whole = jax.ShapeDtypeStruct((rows, model), bf16)
    piece_a = jax.ShapeDtypeStruct((rows, split), bf16)
    piece_b = jax.ShapeDtypeStruct((rows, model - split), bf16)
    dp_scratch = pltpu.VMEM((pairs, 3 * TILE, 2 * TILE), f32)
    turned_scratch = pltpu.VMEM((heads, HEAD_DIM, TILE), f32)
    halo_scratch = [
        pltpu.VMEM(block, bf16),
        pltpu.VMEM(block, f32),
        pltpu.VMEM((pairs, TILE, 2 * TILE), bf16),
    ]
    diagonal = pltpu.VMEM(block, bf16)

    def call(kernel, name, ins, outs, scratch=(), limit=12, cost=0):
        single = not isinstance(outs, list)
        estimate = pl.CostEstimate(flops=cost, bytes_accessed=0, transcendentals=0)
        return pl.pallas_call(
            kernel,
            in_specs=ins,
            out_specs=vmem if single else [vmem] * len(outs),
            out_shape=outs,
            scratch_shapes=list(scratch),
            compiler_params=pltpu.CompilerParams(vmem_limit_bytes=limit * MIB),
            cost_estimate=estimate if cost else None,
            name=name,
        )

    def mark(*values, cost=10**10):
        token = pltpu.VMEM((8, 128), f32)
        return call(mark_kernel, "mark", [anywhere] * len(values), token, cost=cost)(*values)

    k2 = far(key_rows[0])
    v2 = far(value_rows[0])
    k1 = near(key_rows[0])
    wot, wkt, wvt, wqt, q, k, v, x, qbd, keep = call(
        prep_kernel,
        "prep",
        [anywhere] * 9,
        [
            weight,
            weight,
            weight,
            weight,
            tile,
            tile,
            tile,
            tile,
            diagonal,
            pltpu.VMEM((2, pairs, 8, 2 * TILE), jnp.int32),
        ],
        [
            pltpu.VMEM((4, model, width), bf16),
            pltpu.SMEM((window.shape[0], 2, heads), jnp.int32),
            pltpu.SemaphoreType.DMA((21,)),
        ],
        36,
    )(
        out_weight[0],
        key_weight[0],
        value_weight[0],
        query_weight[0],
        query_rows[0],
        key_rows[0],
        value_rows[0],
        upstream,
        jnp.transpose(window, (0, 2, 1)),
    )
    v1 = near(v)
    pt, kt = call(
        functools.partial(prob_kernel, scaling),
        "prob",
        [vmem] * 5 + [anywhere],
        [
            pltpu.VMEM((pairs, 3 * TILE, 2 * rows), bf16),
            pltpu.VMEM((heads, HEAD_DIM, 3 * TILE), bf16),
        ],
        [dp_scratch],
    )(keep, qbd, k, k1, k2, mark(k1, k2))

    to_far, ds, bd = call(
        functools.partial(first_far_kernel, sections - 1, scaling),
        "first_far",
        [vmem] * 9 + [anywhere],
        [whole, pltpu.VMEM((pairs, 3 * TILE, 2 * rows), bf16), diagonal],
        [tile, tile, dp_scratch],
    )(x, wot, qbd, pt, v, v1, v2, wkt, wvt, mark(v2, pt))
    from_far = far(to_far)
    to_near = call(
        functools.partial(first_near_kernel, sections - 1), "first_near", [vmem] * 6, whole, [tile, tile])(
        ds, bd, qbd, pt, wkt, wvt
    )
    from_near = near(to_near)
    packet = pltpu.VMEM((pairs, 3 * TILE, 2 * HEAD_DIM), bf16)
    po_to_near, po_to_far = call(out_kernel, "out", [vmem] * 5 + [anywhere], [packet, packet])(
        pt, q, v, v1, v2, to_near
    )
    pof = far_within(po_to_far, range(sections - 1))
    pon = near(po_to_near)
    turn = call(turn_kernel, "turn", [vmem], diagonal)
    qbdn, qbdf = turn(pon), turn(pof)
    base = call(
        functools.partial(first_own_kernel, sections - 1),
        "first_own",
        [vmem] * 9 + [anywhere],
        wide,
        [tile, tile, tile, turned_scratch],
    )(x, ds, bd, qbd, pt, kt, wqt, wkt, wvt, po_to_far)
    done_a, done_b = call(
        first_sum_kernel, "first_sum", [vmem] * 3 + [anywhere], [piece_a, piece_b]
    )(base, from_near, from_far, mark(from_far))
    done = [done_a, done_b]

    for step in range(1, sections):
        source = sections - step
        xa = hop(done_a, source)
        xb = hop(done_b, source)
        acc, xa_copy = call(
            begin_kernel, "begin", [vmem] * 2 + [anywhere], [wide, piece_a]
        )(xa, wot, qbdn)
        xfa, xfb = far(xa_copy), far(xb)
        xna, xnb = near(xa_copy), near(xb)
        dq, dk, dv, base = call(
            functools.partial(own_kernel, scaling),
            "own",
            [vmem] * 11,
            [tile, wide, wide, pltpu.VMEM((rows, split), f32)],
            [
                pltpu.VMEM(block, bf16),
                dp_scratch,
                pltpu.VMEM((pairs, 3 * TILE, 2 * TILE), bf16),
                turned_scratch,
            ],
        )(acc, xa, xb, wot, qbd, pt, kt, v, v1, v2, wqt)
        acc, dk, dv = call(
            functools.partial(near_kernel, scaling),
            "near",
            [vmem] * 9 + [anywhere],
            [wide, wide, wide],
            halo_scratch,
        )(xfa, xna, xnb, wot, qbdn, pon, v, dk, dv, mark(xfa, xna, cost=10**8))
        done_a, dk, dv = call(
            functools.partial(far_kernel, scaling),
            "far",
            [vmem] * 11,
            [piece_a, tile, tile],
            halo_scratch,
        )(acc, xfb, wot, qbdf, pof, v, dk, dv, base, wkt, wvt)
        rest_in = (dk, dv, dq, xb, wqt, wkt, wvt)
        if step < sections - 1:
            done_b = call(rest_kernel, "rest", [vmem] * 7, piece_b)(*rest_in)
            done += [done_a, done_b]
    out = call(
        finish_kernel,
        "finish",
        [vmem] * (8 + len(done)),
        jax.ShapeDtypeStruct((rows, model), bf16),
    )(*rest_in, *done, done_a)
    return out[None]


def solution(mesh):
    in_specs = (
        P("pipe", "seq", None),
        P("pipe", "seq", None),
        P("pipe", "seq", None),
        P("pipe", None, None),
        P("pipe", None, None),
        P("pipe", None, None),
        P("pipe", None, None),
        P("seq", None),
        P(),
    )
    out_specs = P("pipe", "seq", None)
    return jax.shard_map(body, mesh=mesh, in_specs=in_specs, out_specs=out_specs, check_vma=False)
```

profile of v0, /device:TPU:1, one launch (start us, length us, event | category | flops | bytes accessed | tf_op | source)
XLA Modules:
  0.0 95.0 jit_solution(15908350898902942176)
XLA Ops:
  0.1 4.5 %collective-permute-start.1 = (bf16[128,1536]{1,0:T(8,128)(2,1)}, bf16[128,1536]{1,0:T(8,128)(2,1)S(1)}, u32[]{:S(2)}, u32[]{:S(2)}) collective-permute-start(bf16[128,1536]{1,0:T(8,128)(2,1)} %bitcast.15), channel_id=1, source_target_pairs={{1,2},{3,4},{5,6},{2,1},{4,3},{6,5},{9,10},{11,12},{13,14},{10,9},... | collective-permute-start | bytes 1179656 | tf_op jit(solution)/shard_map/ppermute | solution.py:401
  4.6 1.9 %collective-permute-start.3 = (bf16[128,1536]{1,0:T(8,128)(2,1)}, bf16[128,1536]{1,0:T(8,128)(2,1)S(1)}, u32[]{:S(2)}, u32[]{:S(2)}) collective-permute-start(bf16[128,1536]{1,0:T(8,128)(2,1)} %bitcast.17), channel_id=1, source_target_pairs={{1,2},{3,4},{5,6},{2,1},{4,3},{6,5},{9,10},{11,12},{13,14},{10,9},... | collective-permute-start | bytes 1179656 | tf_op jit(solution)/shard_map/ppermute | solution.py:401
  6.5 7.7 %prep.1 = (bf16[1536,1536]{1,0:T(8,128)(2,1)S(1)}, bf16[1536,1536]{1,0:T(8,128)(2,1)S(1)}, bf16[1536,1536]{1,0:T(8,128)(2,1)S(1)}, bf16[1536,1536]{1,0:T(8,128)(...) custom-call(bf16[1536,1536]{1,0:T(8,128)(2,1)} %bitcast.9, ...), custom_call_target="tpu_custom_call" | custom-call | tf_op jit(solution)/shard_map/prep/pallas_call | solution.py:450
  16.1 3.8 %collective-permute-start.5 = (bf16[128,1536]{1,0:T(8,128)(2,1)S(1)}, bf16[128,1536]{1,0:T(8,128)(2,1)S(1)}, u32[]{:S(2)}, u32[]{:S(2)}) collective-permute-start(bf16[128,1536]{1,0:T(8,128)(2,1)S(1)} %get-tuple-element.75), channel_id=1, source_target_pairs={{1,2},{3,4},{5,6},{2,1},{4,3},{6,5},{9,10},{11,12},{13,14},{10,9},... | collective-permute-start | bytes 1179656 | tf_op jit(solution)/shard_map/ppermute | solution.py:401
  21.0 3.2 %collective-permute-start.13 = (bf16[6,384,256]{2,1,0:T(8,128)(2,1)S(1)}, bf16[6,384,256]{2,1,0:T(8,128)(2,1)S(1)}, u32[]{:S(2)}, u32[]{:S(2)}) collective-permute-start(bf16[6,384,256]{2,1,0:T(8,128)(2,1)S(1)} %get-tuple-element.74.after), channel_id=1, source_target_pairs={{1,2},{3,4},{5,6},{2,1},{4,3},{6,5},{9,10},{11,12},{13,14},{10,9},... | collective-permute-start | bytes 3538952 | tf_op jit(solution)/shard_map/ppermute | solution.py:405
  27.4 3.6 %collective-permute-start.8 = (bf16[128,768]{1,0:T(8,128)(2,1)S(1)}, bf16[128,768]{1,0:T(8,128)(2,1)S(1)}, u32[]{:S(2)}, u32[]{:S(2)}) collective-permute-start(bf16[128,768]{1,0:T(8,128)(2,1)S(1)} %get-tuple-element.78), channel_id=1, source_target_pairs={{1,2},{3,4},{5,6},{2,1},{4,3},{6,5},{9,10},{11,12},{13,14},{10,9},... | collective-permute-start | bytes 589832 | tf_op jit(solution)/shard_map/ppermute | solution.py:401
  31.6 3.3 %collective-permute-start.12 = (bf16[128,768]{1,0:T(8,128)(2,1)S(1)}, bf16[128,768]{1,0:T(8,128)(2,1)S(1)}, u32[]{:S(2)}, u32[]{:S(2)}) collective-permute-start(bf16[128,768]{1,0:T(8,128)(2,1)S(1)} %collective-permute-done.10.xb.own_x), channel_id=1, source_target_pairs={{1,2},{3,4},{5,6},{2,1},{4,3},{6,5},{9,10},{11,12},{13,14},{10,9},... | collective-permute-start | bytes 589832 | tf_op jit(solution)/shard_map/ppermute | solution.py:401
  35.0 2.3 %own.3 = (bf16[128,1536]{1,0:T(8,128)(2,1)S(1)}, f32[128,1536]{1,0:T(8,128)S(1)}, f32[128,1536]{1,0:T(8,128)S(1)}, f32[128,768]{1,0:T(8,128)S(1)}) custom-call(f32[128,1536]{1,0:T(8,128)S(1)} %get-tuple-element.80.acc, bf16[128,768]{1,0:T(8,128)(2,1)S(1)} %collective-permute-done.6.xa_ref.xa, bf16[128,768]{1,0:T(8,128)(2,1)S(1)} %collective-permute-done.10.xb.own_x, ...), custom_call_target="tpu_custom_call" | custom-call | tf_op jit(solution)/shard_map/own/pallas_call | solution.py:537
  38.6 2.0 %collective-permute-done.8.refs_0_.xfa = bf16[128,768]{1,0:T(8,128)(2,1)S(1)} collective-permute-done((bf16[128,768]{1,0:T(8,128)(2,1)S(1)}, bf16[128,768]{1,0:T(8,128)(2,1)S(1)}, u32[]{:S(2)}, u32[]{:S(2)}) %collective-permute-start.8) | collective-permute-done | bytes 196640 | tf_op jit(solution)/shard_map/ppermute | solution.py:401
  40.6 1.6 %near.3 = (f32[128,1536]{1,0:T(8,128)S(1)}, f32[128,1536]{1,0:T(8,128)S(1)}, f32[128,1536]{1,0:T(8,128)S(1)}) custom-call(bf16[128,768]{1,0:T(8,128)(2,1)S(1)} %collective-permute-done.8.refs_0_.xfa, bf16[128,768]{1,0:T(8,128)(2,1)S(1)} %collective-permute-done.9.refs_1_.xa, bf16[128,768]{1,0:T(8,128)(2,1)S(1)} %collective-permute-done.11.xb, ...), custom_call_target="tpu_custom_call" | custom-call | tf_op jit(solution)/shard_map/near/pallas_call | solution.py:549
  42.7 1.7 %far.3 = (bf16[128,768]{1,0:T(8,128)(2,1)S(1)}, bf16[128,1536]{1,0:T(8,128)(2,1)S(1)}, bf16[128,1536]{1,0:T(8,128)(2,1)S(1)}) custom-call(f32[128,1536]{1,0:T(8,128)S(1)} %get-tuple-element.83.acc, bf16[128,768]{1,0:T(8,128)(2,1)S(1)} %collective-permute-done.12.xb, bf16[1536,1536]{1,0:T(8,128)(2,1)S(1)} %get-tuple-element.61.wot, ...), custom_call_target="tpu_custom_call" | custom-call | tf_op jit(solution)/shard_map/far/pallas_call | solution.py:556
  47.3 3.2 %collective-permute-start.15 = (bf16[128,768]{1,0:T(8,128)(2,1)S(1)}, bf16[128,768]{1,0:T(8,128)(2,1)S(1)}, u32[]{:S(2)}, u32[]{:S(2)}) collective-permute-start(bf16[128,768]{1,0:T(8,128)(2,1)S(1)} %get-tuple-element.88), channel_id=1, source_target_pairs={{1,2},{3,4},{5,6},{2,1},{4,3},{6,5},{9,10},{11,12},{13,14},{10,9},... | collective-permute-start | bytes 589832 | tf_op jit(solution)/shard_map/ppermute | solution.py:401
  51.1 3.1 %collective-permute-start.19 = (bf16[128,768]{1,0:T(8,128)(2,1)S(1)}, bf16[128,768]{1,0:T(8,128)(2,1)S(1)}, u32[]{:S(2)}, u32[]{:S(2)}) collective-permute-start(bf16[128,768]{1,0:T(8,128)(2,1)S(1)} %collective-permute-done.17.xb.own_x), channel_id=1, source_target_pairs={{1,2},{3,4},{5,6},{2,1},{4,3},{6,5},{9,10},{11,12},{13,14},{10,9},... | collective-permute-start | bytes 589832 | tf_op jit(solution)/shard_map/ppermute | solution.py:401
  54.2 2.4 %own.4 = (bf16[128,1536]{1,0:T(8,128)(2,1)S(1)}, f32[128,1536]{1,0:T(8,128)S(1)}, f32[128,1536]{1,0:T(8,128)S(1)}, f32[128,768]{1,0:T(8,128)S(1)}) custom-call(f32[128,1536]{1,0:T(8,128)S(1)} %get-tuple-element.92.acc, bf16[128,768]{1,0:T(8,128)(2,1)S(1)} %collective-permute-done.14.xa_ref.xa, bf16[128,768]{1,0:T(8,128)(2,1)S(1)} %collective-permute-done.17.xb.own_x, ...), custom_call_target="tpu_custom_call" | custom-call | tf_op jit(solution)/shard_map/own/pallas_call | solution.py:537
  56.6 1.6 %near.4 = (f32[128,1536]{1,0:T(8,128)S(1)}, f32[128,1536]{1,0:T(8,128)S(1)}, f32[128,1536]{1,0:T(8,128)S(1)}) custom-call(bf16[128,768]{1,0:T(8,128)(2,1)S(1)} %collective-permute-done.15.refs_0_.xfa, bf16[128,768]{1,0:T(8,128)(2,1)S(1)} %collective-permute-done.16.refs_1_.xa, bf16[128,768]{1,0:T(8,128)(2,1)S(1)} %collective-permute-done.18.xb, ...), custom_call_target="tpu_custom_call" | custom-call | tf_op jit(solution)/shard_map/near/pallas_call | solution.py:549
  58.2 1.7 %far.4 = (bf16[128,768]{1,0:T(8,128)(2,1)S(1)}, bf16[128,1536]{1,0:T(8,128)(2,1)S(1)}, bf16[128,1536]{1,0:T(8,128)(2,1)S(1)}) custom-call(f32[128,1536]{1,0:T(8,128)S(1)} %get-tuple-element.95.acc, bf16[128,768]{1,0:T(8,128)(2,1)S(1)} %collective-permute-done.19.xb, bf16[1536,1536]{1,0:T(8,128)(2,1)S(1)} %get-tuple-element.61.wot, ...), custom_call_target="tpu_custom_call" | custom-call | tf_op jit(solution)/shard_map/far/pallas_call | solution.py:556
  59.9 1.5 %collective-permute-start.20 = (bf16[128,768]{1,0:T(8,128)(2,1)S(1)}, bf16[128,768]{1,0:T(8,128)(2,1)S(1)}, u32[]{:S(2)}, u32[]{:S(2)}) collective-permute-start(bf16[128,768]{1,0:T(8,128)(2,1)S(1)} %get-tuple-element.99.refs_4_), channel_id=1, source_target_pairs={{8,0},{9,1},{10,2},{11,3},{12,4},{13,5},{14,6},{15,7}} | collective-permute-start | bytes 589832 | tf_op jit(solution)/shard_map/ppermute | solution.py:408
  63.8 15.8 %collective-permute-done.20.xa_ref.xa = bf16[128,768]{1,0:T(8,128)(2,1)S(1)} collective-permute-done((bf16[128,768]{1,0:T(8,128)(2,1)S(1)}, bf16[128,768]{1,0:T(8,128)(2,1)S(1)}, u32[]{:S(2)}, u32[]{:S(2)}) %collective-permute-start.20) | collective-permute-done | bytes 196640 | tf_op jit(solution)/shard_map/ppermute | solution.py:408
  80.1 3.8 %collective-permute-start.21 = (bf16[128,768]{1,0:T(8,128)(2,1)S(1)}, bf16[128,768]{1,0:T(8,128)(2,1)S(1)}, u32[]{:S(2)}, u32[]{:S(2)}) collective-permute-start(bf16[128,768]{1,0:T(8,128)(2,1)S(1)} %get-tuple-element.100), channel_id=1, source_target_pairs={{1,2},{3,4},{5,6},{2,1},{4,3},{6,5},{9,10},{11,12},{13,14},{10,9},... | collective-permute-start | bytes 589832 | tf_op jit(solution)/shard_map/ppermute | solution.py:401
  84.5 2.8 %collective-permute-start.25 = (bf16[128,768]{1,0:T(8,128)(2,1)S(1)}, bf16[128,768]{1,0:T(8,128)(2,1)S(1)}, u32[]{:S(2)}, u32[]{:S(2)}) collective-permute-start(bf16[128,768]{1,0:T(8,128)(2,1)S(1)} %collective-permute-done.23.xb.own_x), channel_id=1, source_target_pairs={{1,2},{3,4},{5,6},{2,1},{4,3},{6,5},{9,10},{11,12},{13,14},{10,9},... | collective-permute-start | bytes 589832 | tf_op jit(solution)/shard_map/ppermute | solution.py:401
  87.3 2.4 %own.5 = (bf16[128,1536]{1,0:T(8,128)(2,1)S(1)}, f32[128,1536]{1,0:T(8,128)S(1)}, f32[128,1536]{1,0:T(8,128)S(1)}, f32[128,768]{1,0:T(8,128)S(1)}) custom-call(f32[128,1536]{1,0:T(8,128)S(1)} %get-tuple-element.104.acc, bf16[128,768]{1,0:T(8,128)(2,1)S(1)} %collective-permute-done.20.xa_ref.xa, bf16[128,768]{1,0:T(8,128)(2,1)S(1)} %collective-permute-done.23.xb.own_x, ...), custom_call_target="tpu_custom_call" | custom-call | tf_op jit(solution)/shard_map/own/pallas_call | solution.py:537
  89.8 1.6 %near.5 = (f32[128,1536]{1,0:T(8,128)S(1)}, f32[128,1536]{1,0:T(8,128)S(1)}, f32[128,1536]{1,0:T(8,128)S(1)}) custom-call(bf16[128,768]{1,0:T(8,128)(2,1)S(1)} %collective-permute-done.21.refs_0_.xfa, bf16[128,768]{1,0:T(8,128)(2,1)S(1)} %collective-permute-done.22.refs_1_.xa, bf16[128,768]{1,0:T(8,128)(2,1)S(1)} %collective-permute-done.24.xb, ...), custom_call_target="tpu_custom_call" | custom-call | tf_op jit(solution)/shard_map/near/pallas_call | solution.py:549
  91.5 1.7 %far.5 = (bf16[128,768]{1,0:T(8,128)(2,1)S(1)}, bf16[128,1536]{1,0:T(8,128)(2,1)S(1)}, bf16[128,1536]{1,0:T(8,128)(2,1)S(1)}) custom-call(f32[128,1536]{1,0:T(8,128)S(1)} %get-tuple-element.107.acc, bf16[128,768]{1,0:T(8,128)(2,1)S(1)} %collective-permute-done.25.xb, bf16[1536,1536]{1,0:T(8,128)(2,1)S(1)} %get-tuple-element.61.wot, ...), custom_call_target="tpu_custom_call" | custom-call | tf_op jit(solution)/shard_map/far/pallas_call | solution.py:556
  93.2 1.9 %finish.1 = bf16[128,1536]{1,0:T(8,128)(2,1)} custom-call(bf16[128,1536]{1,0:T(8,128)(2,1)S(1)} %get-tuple-element.111.dk, bf16[128,1536]{1,0:T(8,128)(2,1)S(1)} %get-tuple-element.112.dv, bf16[128,1536]{1,0:T(8,128)(2,1)S(1)} %get-tuple-element.113.dq, bf16[128,768]{1,0:T(8,128)(2,1)S(1)} %collective-permute-done.23.xb.own_x, ...), custom_call_target="tpu_custom_call" | custom-call | tf_op jit(solution)/shard_map/finish/pallas_call | solution.py:567
  (58 shorter events, 15.4 us)
Async XLA Ops:
  0.0 14.3 %collective-permute-start = (bf16[128,1536]{1,0:T(8,128)(2,1)}, bf16[128,1536]{1,0:T(8,128)(2,1)S(1)}, u32[]{:S(2)}, u32[]{:S(2)}) collective-permute-start(bf16[128,1536]{1,0:T(8,128)(2,1)} %bitcast.14), channel_id=1, source_target_pairs={{0,1},{1,0},{2,3},{3,2},{4,5},{5,4},{6,7},{7,6},{8,9},{9,8},{10,11... | collective-permute-start | bytes 1179656 | tf_op jit(solution)/shard_map/ppermute | solution.py:398
  0.1 14.3 %collective-permute-start.1 = (bf16[128,1536]{1,0:T(8,128)(2,1)}, bf16[128,1536]{1,0:T(8,128)(2,1)S(1)}, u32[]{:S(2)}, u32[]{:S(2)}) collective-permute-start(bf16[128,1536]{1,0:T(8,128)(2,1)} %bitcast.15), channel_id=1, source_target_pairs={{1,2},{3,4},{5,6},{2,1},{4,3},{6,5},{9,10},{11,12},{13,14},{10,9},... | collective-permute-start | bytes 1179656 | tf_op jit(solution)/shard_map/ppermute | solution.py:401
  4.6 11.0 %collective-permute-start.3 = (bf16[128,1536]{1,0:T(8,128)(2,1)}, bf16[128,1536]{1,0:T(8,128)(2,1)S(1)}, u32[]{:S(2)}, u32[]{:S(2)}) collective-permute-start(bf16[128,1536]{1,0:T(8,128)(2,1)} %bitcast.17), channel_id=1, source_target_pairs={{1,2},{3,4},{5,6},{2,1},{4,3},{6,5},{9,10},{11,12},{13,14},{10,9},... | collective-permute-start | bytes 1179656 | tf_op jit(solution)/shard_map/ppermute | solution.py:401
  16.1 9.2 %collective-permute-start.5 = (bf16[128,1536]{1,0:T(8,128)(2,1)S(1)}, bf16[128,1536]{1,0:T(8,128)(2,1)S(1)}, u32[]{:S(2)}, u32[]{:S(2)}) collective-permute-start(bf16[128,1536]{1,0:T(8,128)(2,1)S(1)} %get-tuple-element.75), channel_id=1, source_target_pairs={{1,2},{3,4},{5,6},{2,1},{4,3},{6,5},{9,10},{11,12},{13,14},{10,9},... | collective-permute-start | bytes 1179656 | tf_op jit(solution)/shard_map/ppermute | solution.py:401
  20.4 6.4 %collective-permute-start.7 = (bf16[6,384,256]{2,1,0:T(8,128)(2,1)S(1)}, bf16[6,384,256]{2,1,0:T(8,128)(2,1)S(1)}, u32[]{:S(2)}, u32[]{:S(2)}) collective-permute-start(bf16[6,384,256]{2,1,0:T(8,128)(2,1)S(1)} %get-tuple-element.77), channel_id=1, source_target_pairs={{0,1},{1,0},{2,3},{3,2},{4,5},{5,4},{6,7},{7,6},{8,9},{9,8},{10,11... | collective-permute-start | bytes 3538952 | tf_op jit(solution)/shard_map/ppermute | solution.py:398
  20.5 4.8 %collective-permute-start.4 = (bf16[128,1536]{1,0:T(8,128)(2,1)S(1)}, bf16[128,1536]{1,0:T(8,128)(2,1)S(1)}, u32[]{:S(2)}, u32[]{:S(2)}) collective-permute-start(bf16[128,1536]{1,0:T(8,128)(2,1)S(1)} %first_near.1.after), channel_id=1, source_target_pairs={{0,1},{1,0},{2,3},{3,2},{4,5},{5,4},{6,7},{7,6},{8,9},{9,8},{10,11... | collective-permute-start | bytes 1179656 | tf_op jit(solution)/shard_map/ppermute | solution.py:398
  21.0 17.5 %collective-permute-start.13 = (bf16[6,384,256]{2,1,0:T(8,128)(2,1)S(1)}, bf16[6,384,256]{2,1,0:T(8,128)(2,1)S(1)}, u32[]{:S(2)}, u32[]{:S(2)}) collective-permute-start(bf16[6,384,256]{2,1,0:T(8,128)(2,1)S(1)} %get-tuple-element.74.after), channel_id=1, source_target_pairs={{1,2},{3,4},{5,6},{2,1},{4,3},{6,5},{9,10},{11,12},{13,14},{10,9},... | collective-permute-start | bytes 3538952 | tf_op jit(solution)/shard_map/ppermute | solution.py:405
  26.1 5.0 %collective-permute-start.10 = (bf16[128,768]{1,0:T(8,128)(2,1)S(1)}, bf16[128,768]{1,0:T(8,128)(2,1)S(1)}, u32[]{:S(2)}, u32[]{:S(2)}) collective-permute-start(bf16[128,768]{1,0:T(8,128)(2,1)S(1)} %get-tuple-element.79.refs_1_), channel_id=1, source_target_pairs={{24,16},{25,17},{26,18},{27,19},{28,20},{29,21},{30,22},{31,23}} | collective-permute-start | bytes 589832 | tf_op jit(solution)/shard_map/ppermute | solution.py:408
  27.4 13.2 %collective-permute-start.8 = (bf16[128,768]{1,0:T(8,128)(2,1)S(1)}, bf16[128,768]{1,0:T(8,128)(2,1)S(1)}, u32[]{:S(2)}, u32[]{:S(2)}) collective-permute-start(bf16[128,768]{1,0:T(8,128)(2,1)S(1)} %get-tuple-element.78), channel_id=1, source_target_pairs={{1,2},{3,4},{5,6},{2,1},{4,3},{6,5},{9,10},{11,12},{13,14},{10,9},... | collective-permute-start | bytes 589832 | tf_op jit(solution)/shard_map/ppermute | solution.py:401
  31.0 9.5 %collective-permute-start.9 = (bf16[128,768]{1,0:T(8,128)(2,1)S(1)}, bf16[128,768]{1,0:T(8,128)(2,1)S(1)}, u32[]{:S(2)}, u32[]{:S(2)}) collective-permute-start(bf16[128,768]{1,0:T(8,128)(2,1)S(1)} %get-tuple-element.78), channel_id=1, source_target_pairs={{0,1},{1,0},{2,3},{3,2},{4,5},{5,4},{6,7},{7,6},{8,9},{9,8},{10,11... | collective-permute-start | bytes 589832 | tf_op jit(solution)/shard_map/ppermute | solution.py:398
  31.1 9.5 %collective-permute-start.11 = (bf16[128,768]{1,0:T(8,128)(2,1)S(1)}, bf16[128,768]{1,0:T(8,128)(2,1)S(1)}, u32[]{:S(2)}, u32[]{:S(2)}) collective-permute-start(bf16[128,768]{1,0:T(8,128)(2,1)S(1)} %collective-permute-done.10.xb.own_x), channel_id=1, source_target_pairs={{0,1},{1,0},{2,3},{3,2},{4,5},{5,4},{6,7},{7,6},{8,9},{9,8},{10,11... | collective-permute-start | bytes 589832 | tf_op jit(solution)/shard_map/ppermute | solution.py:398
  31.6 11.1 %collective-permute-start.12 = (bf16[128,768]{1,0:T(8,128)(2,1)S(1)}, bf16[128,768]{1,0:T(8,128)(2,1)S(1)}, u32[]{:S(2)}, u32[]{:S(2)}) collective-permute-start(bf16[128,768]{1,0:T(8,128)(2,1)S(1)} %collective-permute-done.10.xb.own_x), channel_id=1, source_target_pairs={{1,2},{3,4},{5,6},{2,1},{4,3},{6,5},{9,10},{11,12},{13,14},{10,9},... | collective-permute-start | bytes 589832 | tf_op jit(solution)/shard_map/ppermute | solution.py:401
  44.4 2.5 %collective-permute-start.14 = (bf16[128,768]{1,0:T(8,128)(2,1)S(1)}, bf16[128,768]{1,0:T(8,128)(2,1)S(1)}, u32[]{:S(2)}, u32[]{:S(2)}) collective-permute-start(bf16[128,768]{1,0:T(8,128)(2,1)S(1)} %get-tuple-element.87.refs_2_), channel_id=1, source_target_pairs={{16,8},{17,9},{18,10},{19,11},{20,12},{21,13},{22,14},{23,15}} | collective-permute-start | bytes 589832 | tf_op jit(solution)/shard_map/ppermute | solution.py:408
  46.1 4.4 %collective-permute-start.17 = (bf16[128,768]{1,0:T(8,128)(2,1)S(1)}, bf16[128,768]{1,0:T(8,128)(2,1)S(1)}, u32[]{:S(2)}, u32[]{:S(2)}) collective-permute-start(bf16[128,768]{1,0:T(8,128)(2,1)S(1)} %rest.2.refs_3_), channel_id=1, source_target_pairs={{16,8},{17,9},{18,10},{19,11},{20,12},{21,13},{22,14},{23,15}} | collective-permute-start | bytes 589832 | tf_op jit(solution)/shard_map/ppermute | solution.py:408
  47.3 9.2 %collective-permute-start.15 = (bf16[128,768]{1,0:T(8,128)(2,1)S(1)}, bf16[128,768]{1,0:T(8,128)(2,1)S(1)}, u32[]{:S(2)}, u32[]{:S(2)}) collective-permute-start(bf16[128,768]{1,0:T(8,128)(2,1)S(1)} %get-tuple-element.88), channel_id=1, source_target_pairs={{1,2},{3,4},{5,6},{2,1},{4,3},{6,5},{9,10},{11,12},{13,14},{10,9},... | collective-permute-start | bytes 589832 | tf_op jit(solution)/shard_map/ppermute | solution.py:401
  50.5 6.0 %collective-permute-start.16 = (bf16[128,768]{1,0:T(8,128)(2,1)S(1)}, bf16[128,768]{1,0:T(8,128)(2,1)S(1)}, u32[]{:S(2)}, u32[]{:S(2)}) collective-permute-start(bf16[128,768]{1,0:T(8,128)(2,1)S(1)} %get-tuple-element.88), channel_id=1, source_target_pairs={{0,1},{1,0},{2,3},{3,2},{4,5},{5,4},{6,7},{7,6},{8,9},{9,8},{10,11... | collective-permute-start | bytes 589832 | tf_op jit(solution)/shard_map/ppermute | solution.py:398
  50.6 6.0 %collective-permute-start.18 = (bf16[128,768]{1,0:T(8,128)(2,1)S(1)}, bf16[128,768]{1,0:T(8,128)(2,1)S(1)}, u32[]{:S(2)}, u32[]{:S(2)}) collective-permute-start(bf16[128,768]{1,0:T(8,128)(2,1)S(1)} %collective-permute-done.17.xb.own_x), channel_id=1, source_target_pairs={{0,1},{1,0},{2,3},{3,2},{4,5},{5,4},{6,7},{7,6},{8,9},{9,8},{10,11... | collective-permute-start | bytes 589832 | tf_op jit(solution)/shard_map/ppermute | solution.py:398
  51.1 7.1 %collective-permute-start.19 = (bf16[128,768]{1,0:T(8,128)(2,1)S(1)}, bf16[128,768]{1,0:T(8,128)(2,1)S(1)}, u32[]{:S(2)}, u32[]{:S(2)}) collective-permute-start(bf16[128,768]{1,0:T(8,128)(2,1)S(1)} %collective-permute-done.17.xb.own_x), channel_id=1, source_target_pairs={{1,2},{3,4},{5,6},{2,1},{4,3},{6,5},{9,10},{11,12},{13,14},{10,9},... | collective-permute-start | bytes 589832 | tf_op jit(solution)/shard_map/ppermute | solution.py:401
  59.9 19.7 %collective-permute-start.20 = (bf16[128,768]{1,0:T(8,128)(2,1)S(1)}, bf16[128,768]{1,0:T(8,128)(2,1)S(1)}, u32[]{:S(2)}, u32[]{:S(2)}) collective-permute-start(bf16[128,768]{1,0:T(8,128)(2,1)S(1)} %get-tuple-element.99.refs_4_), channel_id=1, source_target_pairs={{8,0},{9,1},{10,2},{11,3},{12,4},{13,5},{14,6},{15,7}} | collective-permute-start | bytes 589832 | tf_op jit(solution)/shard_map/ppermute | solution.py:408
  62.5 21.5 %collective-permute-start.23 = (bf16[128,768]{1,0:T(8,128)(2,1)S(1)}, bf16[128,768]{1,0:T(8,128)(2,1)S(1)}, u32[]{:S(2)}, u32[]{:S(2)}) collective-permute-start(bf16[128,768]{1,0:T(8,128)(2,1)S(1)} %rest.3.refs_5_), channel_id=1, source_target_pairs={{8,0},{9,1},{10,2},{11,3},{12,4},{13,5},{14,6},{15,7}} | collective-permute-start | bytes 589832 | tf_op jit(solution)/shard_map/ppermute | solution.py:408
  80.1 9.6 %collective-permute-start.21 = (bf16[128,768]{1,0:T(8,128)(2,1)S(1)}, bf16[128,768]{1,0:T(8,128)(2,1)S(1)}, u32[]{:S(2)}, u32[]{:S(2)}) collective-permute-start(bf16[128,768]{1,0:T(8,128)(2,1)S(1)} %get-tuple-element.100), channel_id=1, source_target_pairs={{1,2},{3,4},{5,6},{2,1},{4,3},{6,5},{9,10},{11,12},{13,14},{10,9},... | collective-permute-start | bytes 589832 | tf_op jit(solution)/shard_map/ppermute | solution.py:401
  83.9 5.8 %collective-permute-start.22 = (bf16[128,768]{1,0:T(8,128)(2,1)S(1)}, bf16[128,768]{1,0:T(8,128)(2,1)S(1)}, u32[]{:S(2)}, u32[]{:S(2)}) collective-permute-start(bf16[128,768]{1,0:T(8,128)(2,1)S(1)} %get-tuple-element.100), channel_id=1, source_target_pairs={{0,1},{1,0},{2,3},{3,2},{4,5},{5,4},{6,7},{7,6},{8,9},{9,8},{10,11... | collective-permute-start | bytes 589832 | tf_op jit(solution)/shard_map/ppermute | solution.py:398
  84.0 5.7 %collective-permute-start.24 = (bf16[128,768]{1,0:T(8,128)(2,1)S(1)}, bf16[128,768]{1,0:T(8,128)(2,1)S(1)}, u32[]{:S(2)}, u32[]{:S(2)}) collective-permute-start(bf16[128,768]{1,0:T(8,128)(2,1)S(1)} %collective-permute-done.23.xb.own_x), channel_id=1, source_target_pairs={{0,1},{1,0},{2,3},{3,2},{4,5},{5,4},{6,7},{7,6},{8,9},{9,8},{10,11... | collective-permute-start | bytes 589832 | tf_op jit(solution)/shard_map/ppermute | solution.py:398
  84.5 7.0 %collective-permute-start.25 = (bf16[128,768]{1,0:T(8,128)(2,1)S(1)}, bf16[128,768]{1,0:T(8,128)(2,1)S(1)}, u32[]{:S(2)}, u32[]{:S(2)}) collective-permute-start(bf16[128,768]{1,0:T(8,128)(2,1)S(1)} %collective-permute-done.23.xb.own_x), channel_id=1, source_target_pairs={{1,2},{3,4},{5,6},{2,1},{4,3},{6,5},{9,10},{11,12},{13,14},{10,9},... | collective-permute-start | bytes 589832 | tf_op jit(solution)/shard_map/ppermute | solution.py:401
  (2 other events, 3.3 us)
where the time goes:
time: 95.4 us; the launch traced here: 95 us
  starting transfers between devices  41.1 us (43%)
  Pallas kernels  32.4 us (34%)
  waiting for transfers between devices  21 us (22%)
    ppermute x9, starting transfers between devices, far(): return lax.ppermute(value, 'seq', far_pairs)  30.1 us
    ppermute x6, waiting for transfers between devices, hop(): return lax.ppermute(value, 'pipe', [(source, source - 1)])  15.8 us
    pallas_call x1, Pallas kernels, body(): call(prep_kernel, 'prep', [anywhere] * 9, [weight, weight, weight, weight...  7.73 us
    pallas_call x3, Pallas kernels, body(): call(functools.partial(own_kernel, scaling), 'own', [vmem] * 11, [tile, w...  7.09 us
    ppermute x6, starting transfers between devices, hop(): return lax.ppermute(value, 'pipe', [(source, source - 1)])  5.5 us
    pallas_call x3, Pallas kernels, body(): call(functools.partial(far_kernel, scaling), 'far', [vmem] * 11, [piece_a...  5.03 us
    pallas_call x3, Pallas kernels, body(): call(functools.partial(near_kernel, scaling), 'near', [vmem] * 9 + [anywh...  4.91 us
    ppermute x9, waiting for transfers between devices, far(): return lax.ppermute(value, 'seq', far_pairs)  3.65 us
  transfers between devices with their start and end apart: 26, of which 7 were waited for; matrix products, arithmetic and copies ran while one was open for 0% of the time, Pallas kernels for 27%

commit v1 on v0

--- a/solution.py
+++ b/solution.py
@@ -99,7 +99,7 @@
             )
 
 
-def prob_kernel(scaling, keep, qbd, k0, k1, k2, after, pt_ref, kt_ref, scores):
+def prob_kernel(scaling, keep, qbd, k0, k1, k2, pt_ref, kt_ref, scores):
     pairs = pt_ref.shape[0]
     for g in range(pairs):
         cols = pair_cols(g)
@@ -148,14 +148,26 @@
         put_diagonal(qbd, g, po[g, 2 * TILE :])
 
 
+def inside(value):
+    tile = lax.axis_index("seq")
+    edge = (tile == 0) | (tile == lax.axis_size("seq") - 1)
+    return jnp.where(edge, jnp.zeros_like(value), value)
+
+
+def clean_kernel(value, before, out_ref):
+    out_ref[...] = inside(value[...])
+
+
 def mark_kernel(*refs):
     refs[-1][...] = jnp.zeros_like(refs[-1])
 
 
-def begin_kernel(xa_ref, wot, after, acc_ref, copy_ref):
-    x = xa_ref[...]
-    copy_ref[...] = x
-    acc_ref[...] = dot_nn(x, wot[: x.shape[1], :])
+def begin_kernel(column, xa_ref, wot, after, acc_ref, copy_ref):
+    @pl.when(lax.axis_index("pipe") == column)
+    def _():
+        x = xa_ref[...]
+        copy_ref[...] = x
+        acc_ref[...] = dot_nn(x, wot[: x.shape[1], :])
 
 
 def fill_diagonal(bd, wot, x, acc_ref):
@@ -192,7 +204,7 @@
 
 
 def first_far_kernel(
-    last, scaling, x, wot, qbd, pt, v0, v1, v2, wkt, wvt, after, far_ref, ds_ref, bd, dk, dv, dp
+    last, scaling, x, wot, qbd, pt, v0, v1, v2, wkt, wvt, far_ref, ds_ref, bd, dk, dv, dp
 ):
     @pl.when(lax.axis_index("pipe") == last)
     def _():
@@ -230,7 +242,7 @@
 
 
 def first_sum_kernel(base, near, far, after, suma_ref, sumb_ref):
-    total = base[...] + near[...].astype(jnp.float32) + far[...].astype(jnp.float32)
+    total = base[...] + near[...].astype(jnp.float32) + inside(far[...]).astype(jnp.float32)
     total = total.astype(jnp.bfloat16)
     split = suma_ref.shape[1]
     suma_ref[...] = total[:, :split]
@@ -251,6 +263,7 @@
 
 
 def own_kernel(
+    column,
     scaling,
     acc,
     xa,
@@ -272,17 +285,20 @@
     ds,
     turned,
 ):
-    fill_diagonal(bd, wot, xb[...], acc)
-    own_attention(scaling, bd, pt, v0, v1, v2, dp, ds)
-    for g in range(pt.shape[0]):
-        cols = pair_cols(g)
-        dv_ref[:, cols] = dot_nn(pt[g, :TILE], bd[g])
-        dk_ref[:, cols] = dot_nn(ds[g, :TILE], qbd[g])
-    put_dq(ds, kt, turned, dq)
-    base_ref[...] = xa[...].astype(jnp.float32) + dot_nn(dq[...], wqt[:, : xa.shape[1]])
+    @pl.when(lax.axis_index("pipe") == column)
+    def _():
+        fill_diagonal(bd, wot, xb[...], acc)
+        own_attention(scaling, bd, pt, v0, v1, v2, dp, ds)
+        for g in range(pt.shape[0]):
+            cols = pair_cols(g)
+            dv_ref[:, cols] = dot_nn(pt[g, :TILE], bd[g])
+            dk_ref[:, cols] = dot_nn(ds[g, :TILE], qbd[g])
+        put_dq(ds, kt, turned, dq)
+        base_ref[...] = xa[...].astype(jnp.float32) + dot_nn(dq[...], wqt[:, : xa.shape[1]])
 
 
 def near_kernel(
+    column,
     scaling,
     xfa,
     xa,
@@ -301,17 +317,20 @@
     both,
     ds,
 ):
-    x = jnp.concatenate([xa[...], xb[...]], axis=1)
-    fill_diagonal(bd, wot, x, None)
-    halo_attention(scaling, bd, po, v, both, ds)
-    for g in range(po.shape[0]):
-        cols = pair_cols(g)
-        dv_ref[:, cols] = dv_in[:, cols] + dot_nn(po[g, :TILE], bd[g])
-        dk_ref[:, cols] = dk_in[:, cols] + dot_nn(ds[g], qbd[g])
-    acc_ref[...] = dot_nn(xfa[...], wot[: xfa.shape[1], :])
+    @pl.when(lax.axis_index("pipe") == column)
+    def _():
+        x = jnp.concatenate([xa[...], xb[...]], axis=1)
+        fill_diagonal(bd, wot, x, None)
+        halo_attention(scaling, bd, po, v, both, ds)
+        for g in range(po.shape[0]):
+            cols = pair_cols(g)
+            dv_ref[:, cols] = dv_in[:, cols] + dot_nn(po[g, :TILE], bd[g])
+            dk_ref[:, cols] = dk_in[:, cols] + dot_nn(ds[g], qbd[g])
+        acc_ref[...] = dot_nn(inside(xfa[...]), wot[: xfa.shape[1], :])
 
 
 def far_kernel(
+    column,
     scaling,
     acc,
     xb,
@@ -331,17 +350,19 @@
     both,
     ds,
 ):
-    fill_diagonal(bd, wot, xb[...], acc)
-    halo_attention(scaling, bd, po, v, both, ds)
-    for g in range(po.shape[0]):
-        cols = pair_cols(g)
-        dv = dv_in[:, cols] + dot_nn(po[g, :TILE], bd[g])
-        dk = dk_in[:, cols] + dot_nn(ds[g], qbd[g])
-        dv_ref[:, cols] = dv.astype(jnp.bfloat16)
-        dk_ref[:, cols] = dk.astype(jnp.bfloat16)
-    part = pl.ds(0, sum_ref.shape[1])
-    total = base[...] + project_pair(dk_ref, dv_ref, wkt, wvt, part)
-    sum_ref[...] = total.astype(jnp.bfloat16)
+    @pl.when(lax.axis_index("pipe") == column)
+    def _():
+        fill_diagonal(bd, wot, inside(xb[...]), acc)
+        halo_attention(scaling, bd, po, v, both, ds)
+        for g in range(po.shape[0]):
+            cols = pair_cols(g)
+            dv = dv_in[:, cols] + dot_nn(po[g, :TILE], bd[g])
+            dk = dk_in[:, cols] + dot_nn(ds[g], qbd[g])
+            dv_ref[:, cols] = dv.astype(jnp.bfloat16)
+            dk_ref[:, cols] = dk.astype(jnp.bfloat16)
+        part = pl.ds(0, sum_ref.shape[1])
+        total = base[...] + project_pair(dk_ref, dv_ref, wkt, wvt, part)
+        sum_ref[...] = total.astype(jnp.bfloat16)
 
 
 def last_columns(dk, dv, dq, own_x, wqt, wkt, wvt):
@@ -352,8 +373,10 @@
     return total.astype(jnp.bfloat16)
 
 
-def rest_kernel(dk, dv, dq, own_x, wqt, wkt, wvt, sum_ref):
-    sum_ref[...] = last_columns(dk, dv, dq, own_x, wqt, wkt, wvt)
+def rest_kernel(column, dk, dv, dq, own_x, wqt, wkt, wvt, sum_ref):
+    @pl.when(lax.axis_index("pipe") == column)
+    def _():
+        sum_ref[...] = last_columns(dk, dv, dq, own_x, wqt, wkt, wvt)
 
 
 def finish_kernel(dk, dv, dq, own_x, wqt, wkt, wvt, *refs):
@@ -397,15 +420,32 @@
     def near(value):
         return lax.ppermute(value, "seq", near_pairs)
 
+    def spread(pairs_of):
+        tiles = range(seq_size)
+        return [
+            (c * seq_size + i, d * seq_size + j)
+            for c in range(sections)
+            for i in tiles
+            for d, j in [pairs_of(c, i)]
+        ]
+
     def far(value):
-        return lax.ppermute(value, "seq", far_pairs)
+        partner = dict(far_pairs)
+
+        def pairs_of(c, i):
+            return (c, partner[i]) if i in partner else ((c + sections // 2) % sections, i)
+
+        return lax.ppermute(value, ("pipe", "seq"), spread(pairs_of))
 
     def far_within(value, columns):
         moves = [(c * seq_size + i, c * seq_size + j) for c in columns for i, j in far_pairs]
         return lax.ppermute(value, ("pipe", "seq"), moves)
 
     def hop(value, source):
-        return lax.ppermute(value, "pipe", [(source, source - 1)])
+        def pairs_of(c, i):
+            return (2 * source - 1 - c) % sections, i
+
+        return lax.ppermute(value, ("pipe", "seq"), spread(pairs_of))
 
     vmem = pl.BlockSpec(memory_space=pltpu.VMEM)
     anywhere = pl.BlockSpec(memory_space=pl.ANY)
@@ -481,24 +521,26 @@
         jnp.transpose(window, (0, 2, 1)),
     )
     v1 = near(v)
+    clean = call(clean_kernel, "clean", [vmem, anywhere], tile, cost=10**10)
     pt, kt = call(
         functools.partial(prob_kernel, scaling),
         "prob",
-        [vmem] * 5 + [anywhere],
+        [vmem] * 5,
         [
             pltpu.VMEM((pairs, 3 * TILE, 2 * rows), bf16),
             pltpu.VMEM((heads, HEAD_DIM, 3 * TILE), bf16),
         ],
         [dp_scratch],
-    )(keep, qbd, k, k1, k2, mark(k1, k2))
-
+    )(keep, qbd, k, k1, clean(k2, k1))
+
+    v2 = clean(v2, pt)
     to_far, ds, bd = call(
         functools.partial(first_far_kernel, sections - 1, scaling),
         "first_far",
-        [vmem] * 9 + [anywhere],
+        [vmem] * 9,
         [whole, pltpu.VMEM((pairs, 3 * TILE, 2 * rows), bf16), diagonal],
         [tile, tile, dp_scratch],
-    )(x, wot, qbd, pt, v, v1, v2, wkt, wvt, mark(v2, pt))
+    )(x, wot, qbd, pt, v, v1, v2, wkt, wvt)
     from_far = far(to_far)
     to_near = call(
         functools.partial(first_near_kernel, sections - 1), "first_near", [vmem] * 6, whole, [tile, tile])(
@@ -530,12 +572,12 @@
         xa = hop(done_a, source)
         xb = hop(done_b, source)
         acc, xa_copy = call(
-            begin_kernel, "begin", [vmem] * 2 + [anywhere], [wide, piece_a]
+            functools.partial(begin_kernel, source - 1), "begin", [vmem] * 2 + [anywhere], [wide, piece_a]
         )(xa, wot, qbdn)
         xfa, xfb = far(xa_copy), far(xb)
         xna, xnb = near(xa_copy), near(xb)
         dq, dk, dv, base = call(
-            functools.partial(own_kernel, scaling),
+            functools.partial(own_kernel, source - 1, scaling),
             "own",
             [vmem] * 11,
             [tile, wide, wide, pltpu.VMEM((rows, split), f32)],
@@ -547,14 +589,14 @@
             ],
         )(acc, xa, xb, wot, qbd, pt, kt, v, v1, v2, wqt)
         acc, dk, dv = call(
-            functools.partial(near_kernel, scaling),
+            functools.partial(near_kernel, source - 1, scaling),
             "near",
             [vmem] * 9 + [anywhere],
             [wide, wide, wide],
             halo_scratch,
         )(xfa, xna, xnb, wot, qbdn, pon, v, dk, dv, mark(xfa, xna, cost=10**8))
         done_a, dk, dv = call(
-            functools.partial(far_kernel, scaling),
+            functools.partial(far_kernel, source - 1, scaling),
             "far",
             [vmem] * 11,
             [piece_a, tile, tile],
@@ -562,7 +604,9 @@
         )(acc, xfb, wot, qbdf, pof, v, dk, dv, base, wkt, wvt)
         rest_in = (dk, dv, dq, xb, wqt, wkt, wvt)
         if step < sections - 1:
-            done_b = call(rest_kernel, "rest", [vmem] * 7, piece_b)(*rest_in)
+            done_b = call(
+                functools.partial(rest_kernel, source - 1), "rest", [vmem] * 7, piece_b
+            )(*rest_in)
             done += [done_a, done_b]
     out = call(
         finish_kernel,

time: 95.4 us -> 81.4 us (0.85)
  Pallas kernels: 32.4 us -> 18.2 us
  waiting for transfers between devices: 21 us -> 25.3 us
  starting transfers between devices: 41.1 us -> 37.2 us
    pallas_call x15 -> x17, Pallas kernels: 21.9 us -> 7.74 us  [the longest x3 2.57 us: body(): call(functools.partial(own_kernel, source - 1, scaling), 'own', [vmem] *...]
    ppermute x15, starting transfers between devices: 35.6 us -> 24.2 us  [the longest x9 12.8 us: far(): return lax.ppermute(value, ('pipe', 'seq'), spread(pairs_of))]
    ppermute x10, starting transfers between devices: 2.38 us -> 10.3 us  [near(): return lax.ppermute(value, 'seq', near_pairs)]
    ppermute x15, waiting for transfers between devices: 19.5 us -> 24.6 us  [the longest x6 12.6 us: hop(): return lax.ppermute(value, ('pipe', 'seq'), spread(pairs_of))]
    ppermute x1, waiting for transfers between devices: 1.15 us -> 0.01 us  [far_within(): return lax.ppermute(value, ('pipe', 'seq'), moves)]
  transfers between devices with their start and end apart: 26 -> 26, of which waited for: 7 -> 12; matrix products, arithmetic and copies ran while one was open for 0% -> 0% of each run, Pallas kernels for 27% -> 18%
where the time goes in v1:
time: 81.4 us; the launch traced here: 80.9 us
  starting transfers between devices  37.2 us (46%)
  waiting for transfers between devices  25.3 us (31%)
  Pallas kernels  18.2 us (22%)
    ppermute x9, starting transfers between devices, far(): return lax.ppermute(value, ('pipe', 'seq'), spread(pairs_of))  12.8 us
    ppermute x6, waiting for transfers between devices, hop(): return lax.ppermute(value, ('pipe', 'seq'), spread(pairs_of))  12.6 us
    ppermute x9, waiting for transfers between devices, far(): return lax.ppermute(value, ('pipe', 'seq'), spread(pairs_of))  12 us
    ppermute x6, starting transfers between devices, hop(): return lax.ppermute(value, ('pipe', 'seq'), spread(pairs_of))  11.4 us
    ppermute x10, starting transfers between devices, near(): return lax.ppermute(value, 'seq', near_pairs)  10.3 us
    pallas_call x1, Pallas kernels, body(): call(prep_kernel, 'prep', [anywhere] * 9, [weight, weight, weight, weight...  7.73 us
    ppermute x1, starting transfers between devices, far_within(): return lax.ppermute(value, ('pipe', 'seq'), moves)  2.67 us
    pallas_call x3, Pallas kernels, body(): call(functools.partial(own_kernel, source - 1, scaling), 'own', [vmem] *...  2.57 us
  transfers between devices with their start and end apart: 26, of which 12 were waited for; matrix products, arithmetic and copies ran while one was open for 0% of the time, Pallas kernels for 18%

profile of v1, /device:TPU:1, one launch (start us, length us, event | category | flops | bytes accessed | tf_op | source)
XLA Modules:
  0.0 80.9 jit_solution(16432055105267463213)
XLA Ops:
  0.1 2.6 %collective-permute-start.1 = (bf16[128,1536]{1,0:T(8,128)(2,1)}, bf16[128,1536]{1,0:T(8,128)(2,1)S(1)}, u32[]{:S(2)}, u32[]{:S(2)}) collective-permute-start(bf16[128,1536]{1,0:T(8,128)(2,1)} %bitcast.15), channel_id=1, source_target_pairs={{0,16},{1,2},{2,1},{3,4},{4,3},{5,6},{6,5},{7,23},{8,24},{9,10},{1... | collective-permute-start | bytes 1179656 | tf_op jit(solution)/shard_map/ppermute | solution.py:438
  2.8 7.7 %prep.1 = (bf16[1536,1536]{1,0:T(8,128)(2,1)S(1)}, bf16[1536,1536]{1,0:T(8,128)(2,1)S(1)}, bf16[1536,1536]{1,0:T(8,128)(2,1)S(1)}, bf16[1536,1536]{1,0:T(8,128)(...) custom-call(bf16[1536,1536]{1,0:T(8,128)(2,1)} %bitcast.9, ...), custom_call_target="tpu_custom_call" | custom-call | tf_op jit(solution)/shard_map/prep/pallas_call | solution.py:490
  12.9 1.6 %collective-permute-start.5 = (bf16[128,1536]{1,0:T(8,128)(2,1)S(1)}, bf16[128,1536]{1,0:T(8,128)(2,1)S(1)}, u32[]{:S(2)}, u32[]{:S(2)}) collective-permute-start(bf16[128,1536]{1,0:T(8,128)(2,1)S(1)} %get-tuple-element.75), channel_id=1, source_target_pairs={{0,16},{1,2},{2,1},{3,4},{4,3},{5,6},{6,5},{7,23},{8,24},{9,10},{1... | collective-permute-start | bytes 1179656 | tf_op jit(solution)/shard_map/ppermute | solution.py:438
  16.1 2.7 %collective-permute-start.13 = (bf16[6,384,256]{2,1,0:T(8,128)(2,1)S(1)}, bf16[6,384,256]{2,1,0:T(8,128)(2,1)S(1)}, u32[]{:S(2)}, u32[]{:S(2)}) collective-permute-start(bf16[6,384,256]{2,1,0:T(8,128)(2,1)S(1)} %get-tuple-element.74.after), channel_id=1, source_target_pairs={{1,2},{3,4},{5,6},{2,1},{4,3},{6,5},{9,10},{11,12},{13,14},{10,9},... | collective-permute-start | bytes 3538952 | tf_op jit(solution)/shard_map/ppermute | solution.py:442
  18.8 1.7 %collective-permute-done.5.refs_0_.far = bf16[128,1536]{1,0:T(8,128)(2,1)S(1)} collective-permute-done((bf16[128,1536]{1,0:T(8,128)(2,1)S(1)}, bf16[128,1536]{1,0:T(8,128)(2,1)S(1)}, u32[]{:S(2)}, u32[]{:S(2)}) %collective-permute-start.5) | collective-permute-done | bytes 393248 | tf_op jit(solution)/shard_map/ppermute | solution.py:438
  20.6 2.8 %collective-permute-start.6 = (bf16[128,768]{1,0:T(8,128)(2,1)S(1)}, bf16[128,768]{1,0:T(8,128)(2,1)S(1)}, u32[]{:S(2)}, u32[]{:S(2)}) collective-permute-start(bf16[128,768]{1,0:T(8,128)(2,1)S(1)} %get-tuple-element.76.refs_0_), channel_id=1, source_target_pairs={{0,8},{1,9},{2,10},{3,11},{4,12},{5,13},{6,14},{7,15},{8,0},{9,1},... | collective-permute-start | bytes 589832 | tf_op jit(solution)/shard_map/ppermute | solution.py:448
  23.6 2.9 %collective-permute-done.6.xa_ref.xa = bf16[128,768]{1,0:T(8,128)(2,1)S(1)} collective-permute-done((bf16[128,768]{1,0:T(8,128)(2,1)S(1)}, bf16[128,768]{1,0:T(8,128)(2,1)S(1)}, u32[]{:S(2)}, u32[]{:S(2)}) %collective-permute-start.6) | collective-permute-done | bytes 196640 | tf_op jit(solution)/shard_map/ppermute | solution.py:448
  26.5 3.7 %collective-permute-start.8 = (bf16[128,768]{1,0:T(8,128)(2,1)S(1)}, bf16[128,768]{1,0:T(8,128)(2,1)S(1)}, u32[]{:S(2)}, u32[]{:S(2)}) collective-permute-start(bf16[128,768]{1,0:T(8,128)(2,1)S(1)} %get-tuple-element.78), channel_id=1, source_target_pairs={{0,16},{1,2},{2,1},{3,4},{4,3},{5,6},{6,5},{7,23},{8,24},{9,10},{1... | collective-permute-start | bytes 589832 | tf_op jit(solution)/shard_map/ppermute | solution.py:438
  30.2 3.9 %collective-permute-start.9 = (bf16[128,768]{1,0:T(8,128)(2,1)S(1)}, bf16[128,768]{1,0:T(8,128)(2,1)S(1)}, u32[]{:S(2)}, u32[]{:S(2)}) collective-permute-start(bf16[128,768]{1,0:T(8,128)(2,1)S(1)} %get-tuple-element.78), channel_id=1, source_target_pairs={{0,1},{1,0},{2,3},{3,2},{4,5},{5,4},{6,7},{7,6},{8,9},{9,8},{10,11... | collective-permute-start | bytes 589832 | tf_op jit(solution)/shard_map/ppermute | solution.py:421
  34.5 1.5 %collective-permute-done.8.refs_0_.xfa = bf16[128,768]{1,0:T(8,128)(2,1)S(1)} collective-permute-done((bf16[128,768]{1,0:T(8,128)(2,1)S(1)}, bf16[128,768]{1,0:T(8,128)(2,1)S(1)}, u32[]{:S(2)}, u32[]{:S(2)}) %collective-permute-start.8) | collective-permute-done | bytes 196640 | tf_op jit(solution)/shard_map/ppermute | solution.py:438
  36.0 3.5 %collective-permute-done.12.xb = bf16[128,768]{1,0:T(8,128)(2,1)S(1)} collective-permute-done((bf16[128,768]{1,0:T(8,128)(2,1)S(1)}, bf16[128,768]{1,0:T(8,128)(2,1)S(1)}, u32[]{:S(2)}, u32[]{:S(2)}) %collective-permute-start.12) | collective-permute-done | bytes 196640 | tf_op jit(solution)/shard_map/ppermute | solution.py:438
  39.5 3.6 %collective-permute-start.14 = (bf16[128,768]{1,0:T(8,128)(2,1)S(1)}, bf16[128,768]{1,0:T(8,128)(2,1)S(1)}, u32[]{:S(2)}, u32[]{:S(2)}) collective-permute-start(bf16[128,768]{1,0:T(8,128)(2,1)S(1)} %get-tuple-element.87.refs_2_), channel_id=1, source_target_pairs={{0,24},{1,25},{2,26},{3,27},{4,28},{5,29},{6,30},{7,31},{8,16},{9,... | collective-permute-start | bytes 589832 | tf_op jit(solution)/shard_map/ppermute | solution.py:448
  43.2 4.9 %collective-permute-done.14.xa_ref.xa = bf16[128,768]{1,0:T(8,128)(2,1)S(1)} collective-permute-done((bf16[128,768]{1,0:T(8,128)(2,1)S(1)}, bf16[128,768]{1,0:T(8,128)(2,1)S(1)}, u32[]{:S(2)}, u32[]{:S(2)}) %collective-permute-start.14) | collective-permute-done | bytes 196640 | tf_op jit(solution)/shard_map/ppermute | solution.py:448
  48.1 1.7 %collective-permute-start.15 = (bf16[128,768]{1,0:T(8,128)(2,1)S(1)}, bf16[128,768]{1,0:T(8,128)(2,1)S(1)}, u32[]{:S(2)}, u32[]{:S(2)}) collective-permute-start(bf16[128,768]{1,0:T(8,128)(2,1)S(1)} %get-tuple-element.88), channel_id=1, source_target_pairs={{0,16},{1,2},{2,1},{3,4},{4,3},{5,6},{6,5},{7,23},{8,24},{9,10},{1... | collective-permute-start | bytes 589832 | tf_op jit(solution)/shard_map/ppermute | solution.py:438
  49.8 3.3 %collective-permute-start.16 = (bf16[128,768]{1,0:T(8,128)(2,1)S(1)}, bf16[128,768]{1,0:T(8,128)(2,1)S(1)}, u32[]{:S(2)}, u32[]{:S(2)}) collective-permute-start(bf16[128,768]{1,0:T(8,128)(2,1)S(1)} %get-tuple-element.88), channel_id=1, source_target_pairs={{0,1},{1,0},{2,3},{3,2},{4,5},{5,4},{6,7},{7,6},{8,9},{9,8},{10,11... | collective-permute-start | bytes 589832 | tf_op jit(solution)/shard_map/ppermute | solution.py:421
  54.5 4.1 %collective-permute-done.19.xb = bf16[128,768]{1,0:T(8,128)(2,1)S(1)} collective-permute-done((bf16[128,768]{1,0:T(8,128)(2,1)S(1)}, bf16[128,768]{1,0:T(8,128)(2,1)S(1)}, u32[]{:S(2)}, u32[]{:S(2)}) %collective-permute-start.19) | collective-permute-done | bytes 196640 | tf_op jit(solution)/shard_map/ppermute | solution.py:438
  58.6 3.4 %collective-permute-start.20 = (bf16[128,768]{1,0:T(8,128)(2,1)S(1)}, bf16[128,768]{1,0:T(8,128)(2,1)S(1)}, u32[]{:S(2)}, u32[]{:S(2)}) collective-permute-start(bf16[128,768]{1,0:T(8,128)(2,1)S(1)} %get-tuple-element.99.refs_4_), channel_id=1, source_target_pairs={{0,8},{1,9},{2,10},{3,11},{4,12},{5,13},{6,14},{7,15},{8,0},{9,1},... | collective-permute-start | bytes 589832 | tf_op jit(solution)/shard_map/ppermute | solution.py:448
  62.0 1.4 %collective-permute-start.23 = (bf16[128,768]{1,0:T(8,128)(2,1)S(1)}, bf16[128,768]{1,0:T(8,128)(2,1)S(1)}, u32[]{:S(2)}, u32[]{:S(2)}) collective-permute-start(bf16[128,768]{1,0:T(8,128)(2,1)S(1)} %rest.3.refs_5_), channel_id=1, source_target_pairs={{0,8},{1,9},{2,10},{3,11},{4,12},{5,13},{6,14},{7,15},{8,0},{9,1},... | collective-permute-start | bytes 589832 | tf_op jit(solution)/shard_map/ppermute | solution.py:448
  63.4 3.5 %collective-permute-done.20.xa_ref.xa = bf16[128,768]{1,0:T(8,128)(2,1)S(1)} collective-permute-done((bf16[128,768]{1,0:T(8,128)(2,1)S(1)}, bf16[128,768]{1,0:T(8,128)(2,1)S(1)}, u32[]{:S(2)}, u32[]{:S(2)}) %collective-permute-start.20) | collective-permute-done | bytes 196640 | tf_op jit(solution)/shard_map/ppermute | solution.py:448
  67.5 1.9 %collective-permute-start.21 = (bf16[128,768]{1,0:T(8,128)(2,1)S(1)}, bf16[128,768]{1,0:T(8,128)(2,1)S(1)}, u32[]{:S(2)}, u32[]{:S(2)}) collective-permute-start(bf16[128,768]{1,0:T(8,128)(2,1)S(1)} %get-tuple-element.100), channel_id=1, source_target_pairs={{0,16},{1,2},{2,1},{3,4},{4,3},{5,6},{6,5},{7,23},{8,24},{9,10},{1... | collective-permute-start | bytes 589832 | tf_op jit(solution)/shard_map/ppermute | solution.py:438
  72.8 2.4 %own.5 = (bf16[128,1536]{1,0:T(8,128)(2,1)S(1)}, f32[128,1536]{1,0:T(8,128)S(1)}, f32[128,1536]{1,0:T(8,128)S(1)}, f32[128,768]{1,0:T(8,128)S(1)}) custom-call(f32[128,1536]{1,0:T(8,128)S(1)} %get-tuple-element.104.acc, bf16[128,768]{1,0:T(8,128)(2,1)S(1)} %collective-permute-done.20.xa_ref.xa, bf16[128,768]{1,0:T(8,128)(2,1)S(1)} %collective-permute-done.23.xb.own_x, ...), custom_call_target="tpu_custom_call" | custom-call | tf_op jit(solution)/shard_map/own/pallas_call | solution.py:579
  75.2 1.6 %near.5 = (f32[128,1536]{1,0:T(8,128)S(1)}, f32[128,1536]{1,0:T(8,128)S(1)}, f32[128,1536]{1,0:T(8,128)S(1)}) custom-call(bf16[128,768]{1,0:T(8,128)(2,1)S(1)} %collective-permute-done.21.refs_0_.xfa, bf16[128,768]{1,0:T(8,128)(2,1)S(1)} %collective-permute-done.22.refs_1_.xa, bf16[128,768]{1,0:T(8,128)(2,1)S(1)} %collective-permute-done.24.xb, ...), custom_call_target="tpu_custom_call" | custom-call | tf_op jit(solution)/shard_map/near/pallas_call | solution.py:591
  77.4 1.7 %far.5 = (bf16[128,768]{1,0:T(8,128)(2,1)S(1)}, bf16[128,1536]{1,0:T(8,128)(2,1)S(1)}, bf16[128,1536]{1,0:T(8,128)(2,1)S(1)}) custom-call(f32[128,1536]{1,0:T(8,128)S(1)} %get-tuple-element.107.acc, bf16[128,768]{1,0:T(8,128)(2,1)S(1)} %collective-permute-done.25.xb, bf16[1536,1536]{1,0:T(8,128)(2,1)S(1)} %get-tuple-element.61.wot, ...), custom_call_target="tpu_custom_call" | custom-call | tf_op jit(solution)/shard_map/far/pallas_call | solution.py:598
  79.1 1.9 %finish.1 = bf16[128,1536]{1,0:T(8,128)(2,1)} custom-call(bf16[128,1536]{1,0:T(8,128)(2,1)S(1)} %get-tuple-element.111.dk, bf16[128,1536]{1,0:T(8,128)(2,1)S(1)} %get-tuple-element.112.dv, bf16[128,1536]{1,0:T(8,128)(2,1)S(1)} %get-tuple-element.113.dq, bf16[128,768]{1,0:T(8,128)(2,1)S(1)} %collective-permute-done.23.xb.own_x, ...), custom_call_target="tpu_custom_call" | custom-call | tf_op jit(solution)/shard_map/finish/pallas_call | solution.py:611
  (58 shorter events, 10.6 us)
Async XLA Ops:
  0.0 10.9 %collective-permute-start = (bf16[128,1536]{1,0:T(8,128)(2,1)}, bf16[128,1536]{1,0:T(8,128)(2,1)S(1)}, u32[]{:S(2)}, u32[]{:S(2)}) collective-permute-start(bf16[128,1536]{1,0:T(8,128)(2,1)} %bitcast.14), channel_id=1, source_target_pairs={{0,1},{1,0},{2,3},{3,2},{4,5},{5,4},{6,7},{7,6},{8,9},{9,8},{10,11... | collective-permute-start | bytes 1179656 | tf_op jit(solution)/shard_map/ppermute | solution.py:421
  0.1 10.8 %collective-permute-start.1 = (bf16[128,1536]{1,0:T(8,128)(2,1)}, bf16[128,1536]{1,0:T(8,128)(2,1)S(1)}, u32[]{:S(2)}, u32[]{:S(2)}) collective-permute-start(bf16[128,1536]{1,0:T(8,128)(2,1)} %bitcast.15), channel_id=1, source_target_pairs={{0,16},{1,2},{2,1},{3,4},{4,3},{5,6},{6,5},{7,23},{8,24},{9,10},{1... | collective-permute-start | bytes 1179656 | tf_op jit(solution)/shard_map/ppermute | solution.py:438
  2.7 10.1 %collective-permute-start.3 = (bf16[128,1536]{1,0:T(8,128)(2,1)}, bf16[128,1536]{1,0:T(8,128)(2,1)S(1)}, u32[]{:S(2)}, u32[]{:S(2)}) collective-permute-start(bf16[128,1536]{1,0:T(8,128)(2,1)} %bitcast.17), channel_id=1, source_target_pairs={{0,16},{1,2},{2,1},{3,4},{4,3},{5,6},{6,5},{7,23},{8,24},{9,10},{1... | collective-permute-start | bytes 1179656 | tf_op jit(solution)/shard_map/ppermute | solution.py:438
  10.5 2.4 %collective-permute-start.2 = (bf16[128,1536]{1,0:T(8,128)(2,1)S(1)}, bf16[128,1536]{1,0:T(8,128)(2,1)S(1)}, u32[]{:S(2)}, u32[]{:S(2)}) collective-permute-start(bf16[128,1536]{1,0:T(8,128)(2,1)S(1)} %get-tuple-element.66.v0.v), channel_id=1, source_target_pairs={{0,1},{1,0},{2,3},{3,2},{4,5},{5,4},{6,7},{7,6},{8,9},{9,8},{10,11... | collective-permute-start | bytes 1179656 | tf_op jit(solution)/shard_map/ppermute | solution.py:421
  12.9 7.6 %collective-permute-start.5 = (bf16[128,1536]{1,0:T(8,128)(2,1)S(1)}, bf16[128,1536]{1,0:T(8,128)(2,1)S(1)}, u32[]{:S(2)}, u32[]{:S(2)}) collective-permute-start(bf16[128,1536]{1,0:T(8,128)(2,1)S(1)} %get-tuple-element.75), channel_id=1, source_target_pairs={{0,16},{1,2},{2,1},{3,4},{4,3},{5,6},{6,5},{7,23},{8,24},{9,10},{1... | collective-permute-start | bytes 1179656 | tf_op jit(solution)/shard_map/ppermute | solution.py:438
  15.0 8.5 %collective-permute-start.7 = (bf16[6,384,256]{2,1,0:T(8,128)(2,1)S(1)}, bf16[6,384,256]{2,1,0:T(8,128)(2,1)S(1)}, u32[]{:S(2)}, u32[]{:S(2)}) collective-permute-start(bf16[6,384,256]{2,1,0:T(8,128)(2,1)S(1)} %get-tuple-element.77), channel_id=1, source_target_pairs={{0,1},{1,0},{2,3},{3,2},{4,5},{5,4},{6,7},{7,6},{8,9},{9,8},{10,11... | collective-permute-start | bytes 3538952 | tf_op jit(solution)/shard_map/ppermute | solution.py:421
  16.0 4.5 %collective-permute-start.4 = (bf16[128,1536]{1,0:T(8,128)(2,1)S(1)}, bf16[128,1536]{1,0:T(8,128)(2,1)S(1)}, u32[]{:S(2)}, u32[]{:S(2)}) collective-permute-start(bf16[128,1536]{1,0:T(8,128)(2,1)S(1)} %first_near.1.after), channel_id=1, source_target_pairs={{0,1},{1,0},{2,3},{3,2},{4,5},{5,4},{6,7},{7,6},{8,9},{9,8},{10,11... | collective-permute-start | bytes 1179656 | tf_op jit(solution)/shard_map/ppermute | solution.py:421
  16.1 18.3 %collective-permute-start.13 = (bf16[6,384,256]{2,1,0:T(8,128)(2,1)S(1)}, bf16[6,384,256]{2,1,0:T(8,128)(2,1)S(1)}, u32[]{:S(2)}, u32[]{:S(2)}) collective-permute-start(bf16[6,384,256]{2,1,0:T(8,128)(2,1)S(1)} %get-tuple-element.74.after), channel_id=1, source_target_pairs={{1,2},{3,4},{5,6},{2,1},{4,3},{6,5},{9,10},{11,12},{13,14},{10,9},... | collective-permute-start | bytes 3538952 | tf_op jit(solution)/shard_map/ppermute | solution.py:442
  20.6 5.9 %collective-permute-start.6 = (bf16[128,768]{1,0:T(8,128)(2,1)S(1)}, bf16[128,768]{1,0:T(8,128)(2,1)S(1)}, u32[]{:S(2)}, u32[]{:S(2)}) collective-permute-start(bf16[128,768]{1,0:T(8,128)(2,1)S(1)} %get-tuple-element.76.refs_0_), channel_id=1, source_target_pairs={{0,8},{1,9},{2,10},{3,11},{4,12},{5,13},{6,14},{7,15},{8,0},{9,1},... | collective-permute-start | bytes 589832 | tf_op jit(solution)/shard_map/ppermute | solution.py:448
  23.4 10.7 %collective-permute-start.10 = (bf16[128,768]{1,0:T(8,128)(2,1)S(1)}, bf16[128,768]{1,0:T(8,128)(2,1)S(1)}, u32[]{:S(2)}, u32[]{:S(2)}) collective-permute-start(bf16[128,768]{1,0:T(8,128)(2,1)S(1)} %get-tuple-element.79.refs_1_), channel_id=1, source_target_pairs={{0,8},{1,9},{2,10},{3,11},{4,12},{5,13},{6,14},{7,15},{8,0},{9,1},... | collective-permute-start | bytes 589832 | tf_op jit(solution)/shard_map/ppermute | solution.py:448
  26.5 9.5 %collective-permute-start.8 = (bf16[128,768]{1,0:T(8,128)(2,1)S(1)}, bf16[128,768]{1,0:T(8,128)(2,1)S(1)}, u32[]{:S(2)}, u32[]{:S(2)}) collective-permute-start(bf16[128,768]{1,0:T(8,128)(2,1)S(1)} %get-tuple-element.78), channel_id=1, source_target_pairs={{0,16},{1,2},{2,1},{3,4},{4,3},{5,6},{6,5},{7,23},{8,24},{9,10},{1... | collective-permute-start | bytes 589832 | tf_op jit(solution)/shard_map/ppermute | solution.py:438
  30.2 5.8 %collective-permute-start.9 = (bf16[128,768]{1,0:T(8,128)(2,1)S(1)}, bf16[128,768]{1,0:T(8,128)(2,1)S(1)}, u32[]{:S(2)}, u32[]{:S(2)}) collective-permute-start(bf16[128,768]{1,0:T(8,128)(2,1)S(1)} %get-tuple-element.78), channel_id=1, source_target_pairs={{0,1},{1,0},{2,3},{3,2},{4,5},{5,4},{6,7},{7,6},{8,9},{9,8},{10,11... | collective-permute-start | bytes 589832 | tf_op jit(solution)/shard_map/ppermute | solution.py:421
  34.2 5.4 %collective-permute-start.12 = (bf16[128,768]{1,0:T(8,128)(2,1)S(1)}, bf16[128,768]{1,0:T(8,128)(2,1)S(1)}, u32[]{:S(2)}, u32[]{:S(2)}) collective-permute-start(bf16[128,768]{1,0:T(8,128)(2,1)S(1)} %collective-permute-done.10.xb.own_x), channel_id=1, source_target_pairs={{0,16},{1,2},{2,1},{3,4},{4,3},{5,6},{6,5},{7,23},{8,24},{9,10},{1... | collective-permute-start | bytes 589832 | tf_op jit(solution)/shard_map/ppermute | solution.py:438
  39.5 8.6 %collective-permute-start.14 = (bf16[128,768]{1,0:T(8,128)(2,1)S(1)}, bf16[128,768]{1,0:T(8,128)(2,1)S(1)}, u32[]{:S(2)}, u32[]{:S(2)}) collective-permute-start(bf16[128,768]{1,0:T(8,128)(2,1)S(1)} %get-tuple-element.87.refs_2_), channel_id=1, source_target_pairs={{0,24},{1,25},{2,26},{3,27},{4,28},{5,29},{6,30},{7,31},{8,16},{9,... | collective-permute-start | bytes 589832 | tf_op jit(solution)/shard_map/ppermute | solution.py:448
  43.2 9.9 %collective-permute-start.17 = (bf16[128,768]{1,0:T(8,128)(2,1)S(1)}, bf16[128,768]{1,0:T(8,128)(2,1)S(1)}, u32[]{:S(2)}, u32[]{:S(2)}) collective-permute-start(bf16[128,768]{1,0:T(8,128)(2,1)S(1)} %rest.2.refs_3_), channel_id=1, source_target_pairs={{0,24},{1,25},{2,26},{3,27},{4,28},{5,29},{6,30},{7,31},{8,16},{9,... | collective-permute-start | bytes 589832 | tf_op jit(solution)/shard_map/ppermute | solution.py:448
  48.1 5.7 %collective-permute-start.15 = (bf16[128,768]{1,0:T(8,128)(2,1)S(1)}, bf16[128,768]{1,0:T(8,128)(2,1)S(1)}, u32[]{:S(2)}, u32[]{:S(2)}) collective-permute-start(bf16[128,768]{1,0:T(8,128)(2,1)S(1)} %get-tuple-element.88), channel_id=1, source_target_pairs={{0,16},{1,2},{2,1},{3,4},{4,3},{5,6},{6,5},{7,23},{8,24},{9,10},{1... | collective-permute-start | bytes 589832 | tf_op jit(solution)/shard_map/ppermute | solution.py:438
  49.8 4.4 %collective-permute-start.16 = (bf16[128,768]{1,0:T(8,128)(2,1)S(1)}, bf16[128,768]{1,0:T(8,128)(2,1)S(1)}, u32[]{:S(2)}, u32[]{:S(2)}) collective-permute-start(bf16[128,768]{1,0:T(8,128)(2,1)S(1)} %get-tuple-element.88), channel_id=1, source_target_pairs={{0,1},{1,0},{2,3},{3,2},{4,5},{5,4},{6,7},{7,6},{8,9},{9,8},{10,11... | collective-permute-start | bytes 589832 | tf_op jit(solution)/shard_map/ppermute | solution.py:421
  53.2 5.4 %collective-permute-start.19 = (bf16[128,768]{1,0:T(8,128)(2,1)S(1)}, bf16[128,768]{1,0:T(8,128)(2,1)S(1)}, u32[]{:S(2)}, u32[]{:S(2)}) collective-permute-start(bf16[128,768]{1,0:T(8,128)(2,1)S(1)} %collective-permute-done.17.xb.own_x), channel_id=1, source_target_pairs={{0,16},{1,2},{2,1},{3,4},{4,3},{5,6},{6,5},{7,23},{8,24},{9,10},{1... | collective-permute-start | bytes 589832 | tf_op jit(solution)/shard_map/ppermute | solution.py:438
  58.6 8.4 %collective-permute-start.20 = (bf16[128,768]{1,0:T(8,128)(2,1)S(1)}, bf16[128,768]{1,0:T(8,128)(2,1)S(1)}, u32[]{:S(2)}, u32[]{:S(2)}) collective-permute-start(bf16[128,768]{1,0:T(8,128)(2,1)S(1)} %get-tuple-element.99.refs_4_), channel_id=1, source_target_pairs={{0,8},{1,9},{2,10},{3,11},{4,12},{5,13},{6,14},{7,15},{8,0},{9,1},... | collective-permute-start | bytes 589832 | tf_op jit(solution)/shard_map/ppermute | solution.py:448
  62.0 9.2 %collective-permute-start.23 = (bf16[128,768]{1,0:T(8,128)(2,1)S(1)}, bf16[128,768]{1,0:T(8,128)(2,1)S(1)}, u32[]{:S(2)}, u32[]{:S(2)}) collective-permute-start(bf16[128,768]{1,0:T(8,128)(2,1)S(1)} %rest.3.refs_5_), channel_id=1, source_target_pairs={{0,8},{1,9},{2,10},{3,11},{4,12},{5,13},{6,14},{7,15},{8,0},{9,1},... | collective-permute-start | bytes 589832 | tf_op jit(solution)/shard_map/ppermute | solution.py:448
  67.5 7.7 %collective-permute-start.21 = (bf16[128,768]{1,0:T(8,128)(2,1)S(1)}, bf16[128,768]{1,0:T(8,128)(2,1)S(1)}, u32[]{:S(2)}, u32[]{:S(2)}) collective-permute-start(bf16[128,768]{1,0:T(8,128)(2,1)S(1)} %get-tuple-element.100), channel_id=1, source_target_pairs={{0,16},{1,2},{2,1},{3,4},{4,3},{5,6},{6,5},{7,23},{8,24},{9,10},{1... | collective-permute-start | bytes 589832 | tf_op jit(solution)/shard_map/ppermute | solution.py:438
  69.4 5.8 %collective-permute-start.22 = (bf16[128,768]{1,0:T(8,128)(2,1)S(1)}, bf16[128,768]{1,0:T(8,128)(2,1)S(1)}, u32[]{:S(2)}, u32[]{:S(2)}) collective-permute-start(bf16[128,768]{1,0:T(8,128)(2,1)S(1)} %get-tuple-element.100), channel_id=1, source_target_pairs={{0,1},{1,0},{2,3},{3,2},{4,5},{5,4},{6,7},{7,6},{8,9},{9,8},{10,11... | collective-permute-start | bytes 589832 | tf_op jit(solution)/shard_map/ppermute | solution.py:421
  71.2 4.0 %collective-permute-start.24 = (bf16[128,768]{1,0:T(8,128)(2,1)S(1)}, bf16[128,768]{1,0:T(8,128)(2,1)S(1)}, u32[]{:S(2)}, u32[]{:S(2)}) collective-permute-start(bf16[128,768]{1,0:T(8,128)(2,1)S(1)} %collective-permute-done.23.xb.own_x), channel_id=1, source_target_pairs={{0,1},{1,0},{2,3},{3,2},{4,5},{5,4},{6,7},{7,6},{8,9},{9,8},{10,11... | collective-permute-start | bytes 589832 | tf_op jit(solution)/shard_map/ppermute | solution.py:421
  72.1 5.3 %collective-permute-start.25 = (bf16[128,768]{1,0:T(8,128)(2,1)S(1)}, bf16[128,768]{1,0:T(8,128)(2,1)S(1)}, u32[]{:S(2)}, u32[]{:S(2)}) collective-permute-start(bf16[128,768]{1,0:T(8,128)(2,1)S(1)} %collective-permute-done.23.xb.own_x), channel_id=1, source_target_pairs={{0,16},{1,2},{2,1},{3,4},{4,3},{5,6},{6,5},{7,23},{8,24},{9,10},{1... | collective-permute-start | bytes 589832 | tf_op jit(solution)/shard_map/ppermute | solution.py:438
  (2 other events, 3.3 us)

commit v2 on v1

--- a/solution.py
+++ b/solution.py
@@ -126,20 +126,22 @@
             pt_ref[g, pl.ds(b * TILE, TILE), :] = (w * scale).astype(jnp.bfloat16)
 
 
-def out_kernel(pt, q, v0, v1, v2, after, pon_ref, pof_ref):
-    for g in range(pt.shape[0]):
-        pon_ref[g, :TILE] = pt[g, TILE : 2 * TILE]
-        pof_ref[g, :TILE] = pt[g, 2 * TILE :]
-        for n in range(2):
-            cols = pl.ds((2 * g + n) * HEAD_DIM, HEAD_DIM)
-            lanes = pl.ds(n * HEAD_DIM, HEAD_DIM)
-            values = jnp.concatenate([v0[:, cols], v1[:, cols], v2[:, cols]], axis=0)
-            out = dot_nn(pt[g, :, lanes].T, values).astype(jnp.bfloat16)
-            pon_ref[g, pl.ds(TILE, TILE), lanes] = out
-            pof_ref[g, pl.ds(TILE, TILE), lanes] = out
-        queries = q[:, pair_cols(g)]
-        pon_ref[g, 2 * TILE :] = queries
-        pof_ref[g, 2 * TILE :] = queries
+def out_kernel(last, pt, q, v0, v1, v2, after, pon_ref, pof_ref):
+    @pl.when(lax.axis_index("pipe") < last)
+    def _():
+        for g in range(pt.shape[0]):
+            pon_ref[g, :TILE] = pt[g, TILE : 2 * TILE]
+            pof_ref[g, :TILE] = pt[g, 2 * TILE :]
+            for n in range(2):
+                cols = pl.ds((2 * g + n) * HEAD_DIM, HEAD_DIM)
+                lanes = pl.ds(n * HEAD_DIM, HEAD_DIM)
+                values = jnp.concatenate([v0[:, cols], v1[:, cols], v2[:, cols]], axis=0)
+                out = dot_nn(pt[g, :, lanes].T, values).astype(jnp.bfloat16)
+                pon_ref[g, pl.ds(TILE, TILE), lanes] = out
+                pof_ref[g, pl.ds(TILE, TILE), lanes] = out
+            queries = q[:, pair_cols(g)]
+            pon_ref[g, 2 * TILE :] = queries
+            pof_ref[g, 2 * TILE :] = queries
 
 
 def turn_kernel(po, qbd):
@@ -154,8 +156,8 @@
     return jnp.where(edge, jnp.zeros_like(value), value)
 
 
-def clean_kernel(value, before, out_ref):
-    out_ref[...] = inside(value[...])
+def clean_kernel(value, *refs):
+    refs[-1][...] = inside(value[...])
 
 
 def mark_kernel(*refs):
@@ -203,12 +205,17 @@
     return dot_nn(dk[...], wkt[:, part]) + dot_nn(dv[...], wvt[:, part])
 
 
+def first_out_kernel(last, x, wot, bd):
+    @pl.when(lax.axis_index("pipe") == last)
+    def _():
+        fill_diagonal(bd, wot, x[...], None)
+
+
 def first_far_kernel(
-    last, scaling, x, wot, qbd, pt, v0, v1, v2, wkt, wvt, far_ref, ds_ref, bd, dk, dv, dp
+    last, scaling, bd, qbd, pt, v0, v1, v2, wkt, wvt, far_ref, ds_ref, dk, dv, dp
 ):
     @pl.when(lax.axis_index("pipe") == last)
     def _():
-        fill_diagonal(bd, wot, x[...], None)
         own_attention(scaling, bd, pt, v0, v1, v2, dp, ds_ref)
         for g in range(pt.shape[0]):
             cols = pair_cols(g)
@@ -521,7 +528,11 @@
         jnp.transpose(window, (0, 2, 1)),
     )
     v1 = near(v)
-    clean = call(clean_kernel, "clean", [vmem, anywhere], tile, cost=10**10)
+
+    def clean(value, *before):
+        ins = [vmem] + [anywhere] * len(before)
+        return call(clean_kernel, "clean", ins, tile, cost=10**10)(value, *before)
+
     pt, kt = call(
         functools.partial(prob_kernel, scaling),
         "prob",
@@ -533,14 +544,17 @@
         [dp_scratch],
     )(keep, qbd, k, k1, clean(k2, k1))
 
-    v2 = clean(v2, pt)
-    to_far, ds, bd = call(
+    bd = call(
+        functools.partial(first_out_kernel, sections - 1), "first_out", [vmem] * 2, diagonal
+    )(x, wot)
+    v2 = clean(v2, pt, bd)
+    to_far, ds = call(
         functools.partial(first_far_kernel, sections - 1, scaling),
         "first_far",
-        [vmem] * 9,
-        [whole, pltpu.VMEM((pairs, 3 * TILE, 2 * rows), bf16), diagonal],
+        [vmem] * 8,
+        [whole, pltpu.VMEM((pairs, 3 * TILE, 2 * rows), bf16)],
         [tile, tile, dp_scratch],
-    )(x, wot, qbd, pt, v, v1, v2, wkt, wvt)
+    )(bd, qbd, pt, v, v1, v2, wkt, wvt)
     from_far = far(to_far)
     to_near = call(
         functools.partial(first_near_kernel, sections - 1), "first_near", [vmem] * 6, whole, [tile, tile])(
@@ -548,9 +562,12 @@
     )
     from_near = near(to_near)
     packet = pltpu.VMEM((pairs, 3 * TILE, 2 * HEAD_DIM), bf16)
-    po_to_near, po_to_far = call(out_kernel, "out", [vmem] * 5 + [anywhere], [packet, packet])(
-        pt, q, v, v1, v2, to_near
-    )
+    po_to_near, po_to_far = call(
+        functools.partial(out_kernel, sections - 1),
+        "out",
+        [vmem] * 5 + [anywhere],
+        [packet, packet],
+    )(pt, q, v, v1, v2, to_near)
     pof = far_within(po_to_far, range(sections - 1))
     pon = near(po_to_near)
     turn = call(turn_kernel, "turn", [vmem], diagonal)

time: 81.4 us -> 81 us (level)
    ppermute x6, starting transfers between devices: 11.4 us -> 10.5 us  [hop(): return lax.ppermute(value, ('pipe', 'seq'), spread(pairs_of))]
where the time goes in v2:
time: 81 us; the launch traced here: 80.5 us
  starting transfers between devices  36.6 us (45%)
  waiting for transfers between devices  25.7 us (32%)
  Pallas kernels  18 us (22%)
    ppermute x9, starting transfers between devices, far(): return lax.ppermute(value, ('pipe', 'seq'), spread(pairs_of))  12.9 us
    ppermute x6, waiting for transfers between devices, hop(): return lax.ppermute(value, ('pipe', 'seq'), spread(pairs_of))  12.9 us
    ppermute x9, waiting for transfers between devices, far(): return lax.ppermute(value, ('pipe', 'seq'), spread(pairs_of))  12 us
    ppermute x6, starting transfers between devices, hop(): return lax.ppermute(value, ('pipe', 'seq'), spread(pairs_of))  10.5 us
    ppermute x10, starting transfers between devices, near(): return lax.ppermute(value, 'seq', near_pairs)  10.4 us
    pallas_call x1, Pallas kernels, body(): call(prep_kernel, 'prep', [anywhere] * 9, [weight, weight, weight, weight...  7.73 us
    ppermute x1, starting transfers between devices, far_within(): return lax.ppermute(value, ('pipe', 'seq'), moves)  2.67 us
    pallas_call x3, Pallas kernels, body(): call(functools.partial(own_kernel, source - 1, scaling), 'own', [vmem] *...  2.39 us
  transfers between devices with their start and end apart: 26, of which 12 were waited for; matrix products, arithmetic and copies ran while one was open for 0% of the time, Pallas kernels for 18%

profile of v2, /device:TPU:1, one launch (start us, length us, event | category | flops | bytes accessed | tf_op | source)
XLA Modules:
  0.0 80.5 jit_solution(6796070355290567544)
XLA Ops:
  0.1 2.6 %collective-permute-start.1 = (bf16[128,1536]{1,0:T(8,128)(2,1)}, bf16[128,1536]{1,0:T(8,128)(2,1)S(1)}, u32[]{:S(2)}, u32[]{:S(2)}) collective-permute-start(bf16[128,1536]{1,0:T(8,128)(2,1)} %bitcast.15), channel_id=1, source_target_pairs={{0,16},{1,2},{2,1},{3,4},{4,3},{5,6},{6,5},{7,23},{8,24},{9,10},{1... | collective-permute-start | bytes 1179656 | tf_op jit(solution)/shard_map/ppermute | solution.py:445
  2.8 7.7 %prep.1 = (bf16[1536,1536]{1,0:T(8,128)(2,1)S(1)}, bf16[1536,1536]{1,0:T(8,128)(2,1)S(1)}, bf16[1536,1536]{1,0:T(8,128)(2,1)S(1)}, bf16[1536,1536]{1,0:T(8,128)(...) custom-call(bf16[1536,1536]{1,0:T(8,128)(2,1)} %bitcast.9, ...), custom_call_target="tpu_custom_call" | custom-call | tf_op jit(solution)/shard_map/prep/pallas_call | solution.py:497
  12.9 1.6 %collective-permute-start.5 = (bf16[128,1536]{1,0:T(8,128)(2,1)S(1)}, bf16[128,1536]{1,0:T(8,128)(2,1)S(1)}, u32[]{:S(2)}, u32[]{:S(2)}) collective-permute-start(bf16[128,1536]{1,0:T(8,128)(2,1)S(1)} %get-tuple-element.73), channel_id=1, source_target_pairs={{0,16},{1,2},{2,1},{3,4},{4,3},{5,6},{6,5},{7,23},{8,24},{9,10},{1... | collective-permute-start | bytes 1179656 | tf_op jit(solution)/shard_map/ppermute | solution.py:445
  16.1 2.7 %collective-permute-start.13 = (bf16[6,384,256]{2,1,0:T(8,128)(2,1)S(1)}, bf16[6,384,256]{2,1,0:T(8,128)(2,1)S(1)}, u32[]{:S(2)}, u32[]{:S(2)}) collective-permute-start(bf16[6,384,256]{2,1,0:T(8,128)(2,1)S(1)} %get-tuple-element.72.after), channel_id=1, source_target_pairs={{1,2},{3,4},{5,6},{2,1},{4,3},{6,5},{9,10},{11,12},{13,14},{10,9},... | collective-permute-start | bytes 3538952 | tf_op jit(solution)/shard_map/ppermute | solution.py:449
  18.8 1.7 %collective-permute-done.5.refs_0_.far = bf16[128,1536]{1,0:T(8,128)(2,1)S(1)} collective-permute-done((bf16[128,1536]{1,0:T(8,128)(2,1)S(1)}, bf16[128,1536]{1,0:T(8,128)(2,1)S(1)}, u32[]{:S(2)}, u32[]{:S(2)}) %collective-permute-start.5) | collective-permute-done | bytes 393248 | tf_op jit(solution)/shard_map/ppermute | solution.py:445
  20.6 2.2 %collective-permute-start.6 = (bf16[128,768]{1,0:T(8,128)(2,1)S(1)}, bf16[128,768]{1,0:T(8,128)(2,1)S(1)}, u32[]{:S(2)}, u32[]{:S(2)}) collective-permute-start(bf16[128,768]{1,0:T(8,128)(2,1)S(1)} %get-tuple-element.74.refs_0_), channel_id=1, source_target_pairs={{0,8},{1,9},{2,10},{3,11},{4,12},{5,13},{6,14},{7,15},{8,0},{9,1},... | collective-permute-start | bytes 589832 | tf_op jit(solution)/shard_map/ppermute | solution.py:455
  23.0 2.9 %collective-permute-done.6.xa_ref.xa = bf16[128,768]{1,0:T(8,128)(2,1)S(1)} collective-permute-done((bf16[128,768]{1,0:T(8,128)(2,1)S(1)}, bf16[128,768]{1,0:T(8,128)(2,1)S(1)}, u32[]{:S(2)}, u32[]{:S(2)}) %collective-permute-start.6) | collective-permute-done | bytes 196640 | tf_op jit(solution)/shard_map/ppermute | solution.py:455
  25.9 3.8 %collective-permute-start.8 = (bf16[128,768]{1,0:T(8,128)(2,1)S(1)}, bf16[128,768]{1,0:T(8,128)(2,1)S(1)}, u32[]{:S(2)}, u32[]{:S(2)}) collective-permute-start(bf16[128,768]{1,0:T(8,128)(2,1)S(1)} %get-tuple-element.76), channel_id=1, source_target_pairs={{0,16},{1,2},{2,1},{3,4},{4,3},{5,6},{6,5},{7,23},{8,24},{9,10},{1... | collective-permute-start | bytes 589832 | tf_op jit(solution)/shard_map/ppermute | solution.py:445
  29.6 4.0 %collective-permute-start.9 = (bf16[128,768]{1,0:T(8,128)(2,1)S(1)}, bf16[128,768]{1,0:T(8,128)(2,1)S(1)}, u32[]{:S(2)}, u32[]{:S(2)}) collective-permute-start(bf16[128,768]{1,0:T(8,128)(2,1)S(1)} %get-tuple-element.76), channel_id=1, source_target_pairs={{0,1},{1,0},{2,3},{3,2},{4,5},{5,4},{6,7},{7,6},{8,9},{9,8},{10,11... | collective-permute-start | bytes 589832 | tf_op jit(solution)/shard_map/ppermute | solution.py:428
  33.8 2.1 %collective-permute-done.8.refs_0_.xfa = bf16[128,768]{1,0:T(8,128)(2,1)S(1)} collective-permute-done((bf16[128,768]{1,0:T(8,128)(2,1)S(1)}, bf16[128,768]{1,0:T(8,128)(2,1)S(1)}, u32[]{:S(2)}, u32[]{:S(2)}) %collective-permute-start.8) | collective-permute-done | bytes 196640 | tf_op jit(solution)/shard_map/ppermute | solution.py:445
  36.0 3.1 %collective-permute-done.12.xb = bf16[128,768]{1,0:T(8,128)(2,1)S(1)} collective-permute-done((bf16[128,768]{1,0:T(8,128)(2,1)S(1)}, bf16[128,768]{1,0:T(8,128)(2,1)S(1)}, u32[]{:S(2)}, u32[]{:S(2)}) %collective-permute-start.12) | collective-permute-done | bytes 196640 | tf_op jit(solution)/shard_map/ppermute | solution.py:445
  39.1 3.6 %collective-permute-start.14 = (bf16[128,768]{1,0:T(8,128)(2,1)S(1)}, bf16[128,768]{1,0:T(8,128)(2,1)S(1)}, u32[]{:S(2)}, u32[]{:S(2)}) collective-permute-start(bf16[128,768]{1,0:T(8,128)(2,1)S(1)} %get-tuple-element.85.refs_2_), channel_id=1, source_target_pairs={{0,24},{1,25},{2,26},{3,27},{4,28},{5,29},{6,30},{7,31},{8,16},{9,... | collective-permute-start | bytes 589832 | tf_op jit(solution)/shard_map/ppermute | solution.py:455
  42.7 4.9 %collective-permute-done.14.xa_ref.xa = bf16[128,768]{1,0:T(8,128)(2,1)S(1)} collective-permute-done((bf16[128,768]{1,0:T(8,128)(2,1)S(1)}, bf16[128,768]{1,0:T(8,128)(2,1)S(1)}, u32[]{:S(2)}, u32[]{:S(2)}) %collective-permute-start.14) | collective-permute-done | bytes 196640 | tf_op jit(solution)/shard_map/ppermute | solution.py:455
  47.6 1.6 %collective-permute-start.15 = (bf16[128,768]{1,0:T(8,128)(2,1)S(1)}, bf16[128,768]{1,0:T(8,128)(2,1)S(1)}, u32[]{:S(2)}, u32[]{:S(2)}) collective-permute-start(bf16[128,768]{1,0:T(8,128)(2,1)S(1)} %get-tuple-element.86), channel_id=1, source_target_pairs={{0,16},{1,2},{2,1},{3,4},{4,3},{5,6},{6,5},{7,23},{8,24},{9,10},{1... | collective-permute-start | bytes 589832 | tf_op jit(solution)/shard_map/ppermute | solution.py:445
  49.3 3.3 %collective-permute-start.16 = (bf16[128,768]{1,0:T(8,128)(2,1)S(1)}, bf16[128,768]{1,0:T(8,128)(2,1)S(1)}, u32[]{:S(2)}, u32[]{:S(2)}) collective-permute-start(bf16[128,768]{1,0:T(8,128)(2,1)S(1)} %get-tuple-element.86), channel_id=1, source_target_pairs={{0,1},{1,0},{2,3},{3,2},{4,5},{5,4},{6,7},{7,6},{8,9},{9,8},{10,11... | collective-permute-start | bytes 589832 | tf_op jit(solution)/shard_map/ppermute | solution.py:428
  54.0 4.1 %collective-permute-done.19.xb = bf16[128,768]{1,0:T(8,128)(2,1)S(1)} collective-permute-done((bf16[128,768]{1,0:T(8,128)(2,1)S(1)}, bf16[128,768]{1,0:T(8,128)(2,1)S(1)}, u32[]{:S(2)}, u32[]{:S(2)}) %collective-permute-start.19) | collective-permute-done | bytes 196640 | tf_op jit(solution)/shard_map/ppermute | solution.py:445
  58.2 3.4 %collective-permute-start.20 = (bf16[128,768]{1,0:T(8,128)(2,1)S(1)}, bf16[128,768]{1,0:T(8,128)(2,1)S(1)}, u32[]{:S(2)}, u32[]{:S(2)}) collective-permute-start(bf16[128,768]{1,0:T(8,128)(2,1)S(1)} %get-tuple-element.97.refs_4_), channel_id=1, source_target_pairs={{0,8},{1,9},{2,10},{3,11},{4,12},{5,13},{6,14},{7,15},{8,0},{9,1},... | collective-permute-start | bytes 589832 | tf_op jit(solution)/shard_map/ppermute | solution.py:455
  62.7 3.8 %collective-permute-done.20.xa_ref.xa = bf16[128,768]{1,0:T(8,128)(2,1)S(1)} collective-permute-done((bf16[128,768]{1,0:T(8,128)(2,1)S(1)}, bf16[128,768]{1,0:T(8,128)(2,1)S(1)}, u32[]{:S(2)}, u32[]{:S(2)}) %collective-permute-start.20) | collective-permute-done | bytes 196640 | tf_op jit(solution)/shard_map/ppermute | solution.py:455
  67.0 1.9 %collective-permute-start.21 = (bf16[128,768]{1,0:T(8,128)(2,1)S(1)}, bf16[128,768]{1,0:T(8,128)(2,1)S(1)}, u32[]{:S(2)}, u32[]{:S(2)}) collective-permute-start(bf16[128,768]{1,0:T(8,128)(2,1)S(1)} %get-tuple-element.98), channel_id=1, source_target_pairs={{0,16},{1,2},{2,1},{3,4},{4,3},{5,6},{6,5},{7,23},{8,24},{9,10},{1... | collective-permute-start | bytes 589832 | tf_op jit(solution)/shard_map/ppermute | solution.py:445
  69.4 1.3 %collective-permute-done.23.xb.own_x = bf16[128,768]{1,0:T(8,128)(2,1)S(1)} collective-permute-done((bf16[128,768]{1,0:T(8,128)(2,1)S(1)}, bf16[128,768]{1,0:T(8,128)(2,1)S(1)}, u32[]{:S(2)}, u32[]{:S(2)}) %collective-permute-start.23) | collective-permute-done | bytes 196640 | tf_op jit(solution)/shard_map/ppermute | solution.py:455
  72.4 2.4 %own.5 = (bf16[128,1536]{1,0:T(8,128)(2,1)S(1)}, f32[128,1536]{1,0:T(8,128)S(1)}, f32[128,1536]{1,0:T(8,128)S(1)}, f32[128,768]{1,0:T(8,128)S(1)}) custom-call(f32[128,1536]{1,0:T(8,128)S(1)} %get-tuple-element.102.acc, bf16[128,768]{1,0:T(8,128)(2,1)S(1)} %collective-permute-done.20.xa_ref.xa, bf16[128,768]{1,0:T(8,128)(2,1)S(1)} %collective-permute-done.23.xb.own_x, ...), custom_call_target="tpu_custom_call" | custom-call | tf_op jit(solution)/shard_map/own/pallas_call | solution.py:596
  74.8 1.6 %near.5 = (f32[128,1536]{1,0:T(8,128)S(1)}, f32[128,1536]{1,0:T(8,128)S(1)}, f32[128,1536]{1,0:T(8,128)S(1)}) custom-call(bf16[128,768]{1,0:T(8,128)(2,1)S(1)} %collective-permute-done.21.refs_0_.xfa, bf16[128,768]{1,0:T(8,128)(2,1)S(1)} %collective-permute-done.22.refs_1_.xa, bf16[128,768]{1,0:T(8,128)(2,1)S(1)} %collective-permute-done.24.xb, ...), custom_call_target="tpu_custom_call" | custom-call | tf_op jit(solution)/shard_map/near/pallas_call | solution.py:608
  76.9 1.7 %far.5 = (bf16[128,768]{1,0:T(8,128)(2,1)S(1)}, bf16[128,1536]{1,0:T(8,128)(2,1)S(1)}, bf16[128,1536]{1,0:T(8,128)(2,1)S(1)}) custom-call(f32[128,1536]{1,0:T(8,128)S(1)} %get-tuple-element.105.acc, bf16[128,768]{1,0:T(8,128)(2,1)S(1)} %collective-permute-done.25.xb, bf16[1536,1536]{1,0:T(8,128)(2,1)S(1)} %get-tuple-element.60.wot, ...), custom_call_target="tpu_custom_call" | custom-call | tf_op jit(solution)/shard_map/far/pallas_call | solution.py:615
  78.6 1.9 %finish.1 = bf16[128,1536]{1,0:T(8,128)(2,1)} custom-call(bf16[128,1536]{1,0:T(8,128)(2,1)S(1)} %get-tuple-element.109.dk, bf16[128,1536]{1,0:T(8,128)(2,1)S(1)} %get-tuple-element.110.dv, bf16[128,1536]{1,0:T(8,128)(2,1)S(1)} %get-tuple-element.111.dq, bf16[128,768]{1,0:T(8,128)(2,1)S(1)} %collective-permute-done.23.xb.own_x, ...), custom_call_target="tpu_custom_call" | custom-call | tf_op jit(solution)/shard_map/finish/pallas_call | solution.py:628
  (59 shorter events, 10.3 us)
Async XLA Ops:
  0.0 10.9 %collective-permute-start = (bf16[128,1536]{1,0:T(8,128)(2,1)}, bf16[128,1536]{1,0:T(8,128)(2,1)S(1)}, u32[]{:S(2)}, u32[]{:S(2)}) collective-permute-start(bf16[128,1536]{1,0:T(8,128)(2,1)} %bitcast.14), channel_id=1, source_target_pairs={{0,1},{1,0},{2,3},{3,2},{4,5},{5,4},{6,7},{7,6},{8,9},{9,8},{10,11... | collective-permute-start | bytes 1179656 | tf_op jit(solution)/shard_map/ppermute | solution.py:428
  0.1 10.9 %collective-permute-start.1 = (bf16[128,1536]{1,0:T(8,128)(2,1)}, bf16[128,1536]{1,0:T(8,128)(2,1)S(1)}, u32[]{:S(2)}, u32[]{:S(2)}) collective-permute-start(bf16[128,1536]{1,0:T(8,128)(2,1)} %bitcast.15), channel_id=1, source_target_pairs={{0,16},{1,2},{2,1},{3,4},{4,3},{5,6},{6,5},{7,23},{8,24},{9,10},{1... | collective-permute-start | bytes 1179656 | tf_op jit(solution)/shard_map/ppermute | solution.py:445
  2.7 10.1 %collective-permute-start.3 = (bf16[128,1536]{1,0:T(8,128)(2,1)}, bf16[128,1536]{1,0:T(8,128)(2,1)S(1)}, u32[]{:S(2)}, u32[]{:S(2)}) collective-permute-start(bf16[128,1536]{1,0:T(8,128)(2,1)} %bitcast.17), channel_id=1, source_target_pairs={{0,16},{1,2},{2,1},{3,4},{4,3},{5,6},{6,5},{7,23},{8,24},{9,10},{1... | collective-permute-start | bytes 1179656 | tf_op jit(solution)/shard_map/ppermute | solution.py:445
  10.5 2.4 %collective-permute-start.2 = (bf16[128,1536]{1,0:T(8,128)(2,1)S(1)}, bf16[128,1536]{1,0:T(8,128)(2,1)S(1)}, u32[]{:S(2)}, u32[]{:S(2)}) collective-permute-start(bf16[128,1536]{1,0:T(8,128)(2,1)S(1)} %get-tuple-element.65.v0.v), channel_id=1, source_target_pairs={{0,1},{1,0},{2,3},{3,2},{4,5},{5,4},{6,7},{7,6},{8,9},{9,8},{10,11... | collective-permute-start | bytes 1179656 | tf_op jit(solution)/shard_map/ppermute | solution.py:428
  12.9 7.6 %collective-permute-start.5 = (bf16[128,1536]{1,0:T(8,128)(2,1)S(1)}, bf16[128,1536]{1,0:T(8,128)(2,1)S(1)}, u32[]{:S(2)}, u32[]{:S(2)}) collective-permute-start(bf16[128,1536]{1,0:T(8,128)(2,1)S(1)} %get-tuple-element.73), channel_id=1, source_target_pairs={{0,16},{1,2},{2,1},{3,4},{4,3},{5,6},{6,5},{7,23},{8,24},{9,10},{1... | collective-permute-start | bytes 1179656 | tf_op jit(solution)/shard_map/ppermute | solution.py:445
  15.0 7.9 %collective-permute-start.7 = (bf16[6,384,256]{2,1,0:T(8,128)(2,1)S(1)}, bf16[6,384,256]{2,1,0:T(8,128)(2,1)S(1)}, u32[]{:S(2)}, u32[]{:S(2)}) collective-permute-start(bf16[6,384,256]{2,1,0:T(8,128)(2,1)S(1)} %get-tuple-element.75), channel_id=1, source_target_pairs={{0,1},{1,0},{2,3},{3,2},{4,5},{5,4},{6,7},{7,6},{8,9},{9,8},{10,11... | collective-permute-start | bytes 3538952 | tf_op jit(solution)/shard_map/ppermute | solution.py:428
  16.0 4.5 %collective-permute-start.4 = (bf16[128,1536]{1,0:T(8,128)(2,1)S(1)}, bf16[128,1536]{1,0:T(8,128)(2,1)S(1)}, u32[]{:S(2)}, u32[]{:S(2)}) collective-permute-start(bf16[128,1536]{1,0:T(8,128)(2,1)S(1)} %first_near.1.after), channel_id=1, source_target_pairs={{0,1},{1,0},{2,3},{3,2},{4,5},{5,4},{6,7},{7,6},{8,9},{9,8},{10,11... | collective-permute-start | bytes 1179656 | tf_op jit(solution)/shard_map/ppermute | solution.py:428
  16.1 17.7 %collective-permute-start.13 = (bf16[6,384,256]{2,1,0:T(8,128)(2,1)S(1)}, bf16[6,384,256]{2,1,0:T(8,128)(2,1)S(1)}, u32[]{:S(2)}, u32[]{:S(2)}) collective-permute-start(bf16[6,384,256]{2,1,0:T(8,128)(2,1)S(1)} %get-tuple-element.72.after), channel_id=1, source_target_pairs={{1,2},{3,4},{5,6},{2,1},{4,3},{6,5},{9,10},{11,12},{13,14},{10,9},... | collective-permute-start | bytes 3538952 | tf_op jit(solution)/shard_map/ppermute | solution.py:449
  20.6 5.3 %collective-permute-start.6 = (bf16[128,768]{1,0:T(8,128)(2,1)S(1)}, bf16[128,768]{1,0:T(8,128)(2,1)S(1)}, u32[]{:S(2)}, u32[]{:S(2)}) collective-permute-start(bf16[128,768]{1,0:T(8,128)(2,1)S(1)} %get-tuple-element.74.refs_0_), channel_id=1, source_target_pairs={{0,8},{1,9},{2,10},{3,11},{4,12},{5,13},{6,14},{7,15},{8,0},{9,1},... | collective-permute-start | bytes 589832 | tf_op jit(solution)/shard_map/ppermute | solution.py:455
  22.8 10.9 %collective-permute-start.10 = (bf16[128,768]{1,0:T(8,128)(2,1)S(1)}, bf16[128,768]{1,0:T(8,128)(2,1)S(1)}, u32[]{:S(2)}, u32[]{:S(2)}) collective-permute-start(bf16[128,768]{1,0:T(8,128)(2,1)S(1)} %get-tuple-element.77.refs_1_), channel_id=1, source_target_pairs={{0,8},{1,9},{2,10},{3,11},{4,12},{5,13},{6,14},{7,15},{8,0},{9,1},... | collective-permute-start | bytes 589832 | tf_op jit(solution)/shard_map/ppermute | solution.py:455
  25.9 10.1 %collective-permute-start.8 = (bf16[128,768]{1,0:T(8,128)(2,1)S(1)}, bf16[128,768]{1,0:T(8,128)(2,1)S(1)}, u32[]{:S(2)}, u32[]{:S(2)}) collective-permute-start(bf16[128,768]{1,0:T(8,128)(2,1)S(1)} %get-tuple-element.76), channel_id=1, source_target_pairs={{0,16},{1,2},{2,1},{3,4},{4,3},{5,6},{6,5},{7,23},{8,24},{9,10},{1... | collective-permute-start | bytes 589832 | tf_op jit(solution)/shard_map/ppermute | solution.py:445
  29.6 6.3 %collective-permute-start.9 = (bf16[128,768]{1,0:T(8,128)(2,1)S(1)}, bf16[128,768]{1,0:T(8,128)(2,1)S(1)}, u32[]{:S(2)}, u32[]{:S(2)}) collective-permute-start(bf16[128,768]{1,0:T(8,128)(2,1)S(1)} %get-tuple-element.76), channel_id=1, source_target_pairs={{0,1},{1,0},{2,3},{3,2},{4,5},{5,4},{6,7},{7,6},{8,9},{9,8},{10,11... | collective-permute-start | bytes 589832 | tf_op jit(solution)/shard_map/ppermute | solution.py:428
  33.7 5.4 %collective-permute-start.12 = (bf16[128,768]{1,0:T(8,128)(2,1)S(1)}, bf16[128,768]{1,0:T(8,128)(2,1)S(1)}, u32[]{:S(2)}, u32[]{:S(2)}) collective-permute-start(bf16[128,768]{1,0:T(8,128)(2,1)S(1)} %collective-permute-done.10.xb.own_x), channel_id=1, source_target_pairs={{0,16},{1,2},{2,1},{3,4},{4,3},{5,6},{6,5},{7,23},{8,24},{9,10},{1... | collective-permute-start | bytes 589832 | tf_op jit(solution)/shard_map/ppermute | solution.py:445
  39.1 8.6 %collective-permute-start.14 = (bf16[128,768]{1,0:T(8,128)(2,1)S(1)}, bf16[128,768]{1,0:T(8,128)(2,1)S(1)}, u32[]{:S(2)}, u32[]{:S(2)}) collective-permute-start(bf16[128,768]{1,0:T(8,128)(2,1)S(1)} %get-tuple-element.85.refs_2_), channel_id=1, source_target_pairs={{0,24},{1,25},{2,26},{3,27},{4,28},{5,29},{6,30},{7,31},{8,16},{9,... | collective-permute-start | bytes 589832 | tf_op jit(solution)/shard_map/ppermute | solution.py:455
  42.7 9.9 %collective-permute-start.17 = (bf16[128,768]{1,0:T(8,128)(2,1)S(1)}, bf16[128,768]{1,0:T(8,128)(2,1)S(1)}, u32[]{:S(2)}, u32[]{:S(2)}) collective-permute-start(bf16[128,768]{1,0:T(8,128)(2,1)S(1)} %rest.2.refs_3_), channel_id=1, source_target_pairs={{0,24},{1,25},{2,26},{3,27},{4,28},{5,29},{6,30},{7,31},{8,16},{9,... | collective-permute-start | bytes 589832 | tf_op jit(solution)/shard_map/ppermute | solution.py:455
  47.6 5.7 %collective-permute-start.15 = (bf16[128,768]{1,0:T(8,128)(2,1)S(1)}, bf16[128,768]{1,0:T(8,128)(2,1)S(1)}, u32[]{:S(2)}, u32[]{:S(2)}) collective-permute-start(bf16[128,768]{1,0:T(8,128)(2,1)S(1)} %get-tuple-element.86), channel_id=1, source_target_pairs={{0,16},{1,2},{2,1},{3,4},{4,3},{5,6},{6,5},{7,23},{8,24},{9,10},{1... | collective-permute-start | bytes 589832 | tf_op jit(solution)/shard_map/ppermute | solution.py:445
  49.3 4.4 %collective-permute-start.16 = (bf16[128,768]{1,0:T(8,128)(2,1)S(1)}, bf16[128,768]{1,0:T(8,128)(2,1)S(1)}, u32[]{:S(2)}, u32[]{:S(2)}) collective-permute-start(bf16[128,768]{1,0:T(8,128)(2,1)S(1)} %get-tuple-element.86), channel_id=1, source_target_pairs={{0,1},{1,0},{2,3},{3,2},{4,5},{5,4},{6,7},{7,6},{8,9},{9,8},{10,11... | collective-permute-start | bytes 589832 | tf_op jit(solution)/shard_map/ppermute | solution.py:428
  52.8 5.4 %collective-permute-start.19 = (bf16[128,768]{1,0:T(8,128)(2,1)S(1)}, bf16[128,768]{1,0:T(8,128)(2,1)S(1)}, u32[]{:S(2)}, u32[]{:S(2)}) collective-permute-start(bf16[128,768]{1,0:T(8,128)(2,1)S(1)} %collective-permute-done.17.xb.own_x), channel_id=1, source_target_pairs={{0,16},{1,2},{2,1},{3,4},{4,3},{5,6},{6,5},{7,23},{8,24},{9,10},{1... | collective-permute-start | bytes 589832 | tf_op jit(solution)/shard_map/ppermute | solution.py:445
  58.2 8.4 %collective-permute-start.20 = (bf16[128,768]{1,0:T(8,128)(2,1)S(1)}, bf16[128,768]{1,0:T(8,128)(2,1)S(1)}, u32[]{:S(2)}, u32[]{:S(2)}) collective-permute-start(bf16[128,768]{1,0:T(8,128)(2,1)S(1)} %get-tuple-element.97.refs_4_), channel_id=1, source_target_pairs={{0,8},{1,9},{2,10},{3,11},{4,12},{5,13},{6,14},{7,15},{8,0},{9,1},... | collective-permute-start | bytes 589832 | tf_op jit(solution)/shard_map/ppermute | solution.py:455
  61.6 9.2 %collective-permute-start.23 = (bf16[128,768]{1,0:T(8,128)(2,1)S(1)}, bf16[128,768]{1,0:T(8,128)(2,1)S(1)}, u32[]{:S(2)}, u32[]{:S(2)}) collective-permute-start(bf16[128,768]{1,0:T(8,128)(2,1)S(1)} %rest.3.refs_5_), channel_id=1, source_target_pairs={{0,8},{1,9},{2,10},{3,11},{4,12},{5,13},{6,14},{7,15},{8,0},{9,1},... | collective-permute-start | bytes 589832 | tf_op jit(solution)/shard_map/ppermute | solution.py:455
  67.0 7.8 %collective-permute-start.21 = (bf16[128,768]{1,0:T(8,128)(2,1)S(1)}, bf16[128,768]{1,0:T(8,128)(2,1)S(1)}, u32[]{:S(2)}, u32[]{:S(2)}) collective-permute-start(bf16[128,768]{1,0:T(8,128)(2,1)S(1)} %get-tuple-element.98), channel_id=1, source_target_pairs={{0,16},{1,2},{2,1},{3,4},{4,3},{5,6},{6,5},{7,23},{8,24},{9,10},{1... | collective-permute-start | bytes 589832 | tf_op jit(solution)/shard_map/ppermute | solution.py:445
  68.9 5.9 %collective-permute-start.22 = (bf16[128,768]{1,0:T(8,128)(2,1)S(1)}, bf16[128,768]{1,0:T(8,128)(2,1)S(1)}, u32[]{:S(2)}, u32[]{:S(2)}) collective-permute-start(bf16[128,768]{1,0:T(8,128)(2,1)S(1)} %get-tuple-element.98), channel_id=1, source_target_pairs={{0,1},{1,0},{2,3},{3,2},{4,5},{5,4},{6,7},{7,6},{8,9},{9,8},{10,11... | collective-permute-start | bytes 589832 | tf_op jit(solution)/shard_map/ppermute | solution.py:428
  70.7 4.1 %collective-permute-start.24 = (bf16[128,768]{1,0:T(8,128)(2,1)S(1)}, bf16[128,768]{1,0:T(8,128)(2,1)S(1)}, u32[]{:S(2)}, u32[]{:S(2)}) collective-permute-start(bf16[128,768]{1,0:T(8,128)(2,1)S(1)} %collective-permute-done.23.xb.own_x), channel_id=1, source_target_pairs={{0,1},{1,0},{2,3},{3,2},{4,5},{5,4},{6,7},{7,6},{8,9},{9,8},{10,11... | collective-permute-start | bytes 589832 | tf_op jit(solution)/shard_map/ppermute | solution.py:428
  71.6 5.3 %collective-permute-start.25 = (bf16[128,768]{1,0:T(8,128)(2,1)S(1)}, bf16[128,768]{1,0:T(8,128)(2,1)S(1)}, u32[]{:S(2)}, u32[]{:S(2)}) collective-permute-start(bf16[128,768]{1,0:T(8,128)(2,1)S(1)} %collective-permute-done.23.xb.own_x), channel_id=1, source_target_pairs={{0,16},{1,2},{2,1},{3,4},{4,3},{5,6},{6,5},{7,23},{8,24},{9,10},{1... | collective-permute-start | bytes 589832 | tf_op jit(solution)/shard_map/ppermute | solution.py:445
  (2 other events, 3.8 us)

commit v3 on v2

--- a/solution.py
+++ b/solution.py
@@ -30,6 +30,7 @@
 
 
 def prep_kernel(
+    last,
     wo_hbm,
     wk_hbm,
     wv_hbm,
@@ -49,6 +50,7 @@
     x,
     qbd,
     keep,
+    bd,
     raw,
     flags,
     sems,
@@ -88,6 +90,12 @@
             for r in range(0, rows, TILE):
                 part = pl.ds(start + r, TILE)
                 dst[:, part] = raw[n, part, :].T
+
+        if n == 0:
+
+            @pl.when(lax.axis_index("pipe") == last)
+            def _():
+                fill_diagonal(bd, wot, x[...], None)
     window_copy.wait()
     tile = lax.axis_index("seq")
     odd = lax.rem(tile, 2)
@@ -205,12 +213,6 @@
     return dot_nn(dk[...], wkt[:, part]) + dot_nn(dv[...], wvt[:, part])
 
 
-def first_out_kernel(last, x, wot, bd):
-    @pl.when(lax.axis_index("pipe") == last)
-    def _():
-        fill_diagonal(bd, wot, x[...], None)
-
-
 def first_far_kernel(
     last, scaling, bd, qbd, pt, v0, v1, v2, wkt, wvt, far_ref, ds_ref, dk, dv, dp
 ):
@@ -387,18 +389,32 @@
 
 
 def finish_kernel(dk, dv, dq, own_x, wqt, wkt, wvt, *refs):
-    done_refs, out_ref = refs[:-1], refs[-1]
+    done_refs, (out_ref, tail, sems) = refs[:-3], refs[-3:]
     position = lax.axis_index("pipe")
     split = done_refs[0].shape[1]
-    out_ref[:, :split] = done_refs[-1][...]
-    out_ref[:, split:] = last_columns(dk, dv, dq, own_x, wqt, wkt, wvt)
     count = len(done_refs) // 2
+
+    def write(n, value):
+        part = pl.ds(n * split, value.shape[1])
+        return pltpu.make_async_copy(value, out_ref.at[:, part], sems.at[n])
+
+    @pl.when(position == 0)
+    def _():
+        write(0, done_refs[-1]).start()
+        tail[...] = last_columns(dk, dv, dq, own_x, wqt, wkt, wvt)
+        write(1, tail).start()
+        write(0, done_refs[-1]).wait()
+        write(1, tail).wait()
+
     for step in range(count):
 
         @pl.when(position == count - step)
         def _():
-            out_ref[:, :split] = done_refs[2 * step][...]
-            out_ref[:, split:] = done_refs[2 * step + 1][...]
+            copies = [write(0, done_refs[2 * step]), write(1, done_refs[2 * step + 1])]
+            for copy in copies:
+                copy.start()
+            for copy in copies:
+                copy.wait()
 
 
 def body(
@@ -473,13 +489,13 @@
     ]
     diagonal = pltpu.VMEM(block, bf16)
 
-    def call(kernel, name, ins, outs, scratch=(), limit=12, cost=0):
+    def call(kernel, name, ins, outs, scratch=(), limit=12, cost=0, place=vmem):
         single = not isinstance(outs, list)
         estimate = pl.CostEstimate(flops=cost, bytes_accessed=0, transcendentals=0)
         return pl.pallas_call(
             kernel,
             in_specs=ins,
-            out_specs=vmem if single else [vmem] * len(outs),
+            out_specs=place if single else [vmem] * len(outs),
             out_shape=outs,
             scratch_shapes=list(scratch),
             compiler_params=pltpu.CompilerParams(vmem_limit_bytes=limit * MIB),
@@ -494,8 +510,8 @@
     k2 = far(key_rows[0])
     v2 = far(value_rows[0])
     k1 = near(key_rows[0])
-    wot, wkt, wvt, wqt, q, k, v, x, qbd, keep = call(
-        prep_kernel,
+    wot, wkt, wvt, wqt, q, k, v, x, qbd, keep, bd = call(
+        functools.partial(prep_kernel, sections - 1),
         "prep",
         [anywhere] * 9,
         [
@@ -509,6 +525,7 @@
             tile,
             diagonal,
             pltpu.VMEM((2, pairs, 8, 2 * TILE), jnp.int32),
+            diagonal,
         ],
         [
             pltpu.VMEM((4, model, width), bf16),
@@ -544,10 +561,7 @@
         [dp_scratch],
     )(keep, qbd, k, k1, clean(k2, k1))
 
-    bd = call(
-        functools.partial(first_out_kernel, sections - 1), "first_out", [vmem] * 2, diagonal
-    )(x, wot)
-    v2 = clean(v2, pt, bd)
+    v2 = clean(v2, pt)
     to_far, ds = call(
         functools.partial(first_far_kernel, sections - 1, scaling),
         "first_far",
@@ -630,6 +644,8 @@
         "finish",
         [vmem] * (8 + len(done)),
         jax.ShapeDtypeStruct((rows, model), bf16),
+        [pltpu.VMEM((rows, model - split), bf16), pltpu.SemaphoreType.DMA((2,))],
+        place=anywhere,
     )(*rest_in, *done, done_a)
     return out[None]
 

time: 81 us -> 81.1 us (level)
    pallas_call x2 -> x1, Pallas kernels: 7.73 us -> 7.73 us  [body(): call(functools.partial(prep_kernel, sections - 1), 'prep', [anywhere] * 9...]
where the time goes in v3:
time: 81.1 us; the launch traced here: 80.6 us
  starting transfers between devices  36.9 us (45%)
  waiting for transfers between devices  25.3 us (31%)
  Pallas kernels  18 us (22%)
    ppermute x9, starting transfers between devices, far(): return lax.ppermute(value, ('pipe', 'seq'), spread(pairs_of))  13.4 us
    ppermute x6, waiting for transfers between devices, hop(): return lax.ppermute(value, ('pipe', 'seq'), spread(pairs_of))  12.9 us
    ppermute x9, waiting for transfers between devices, far(): return lax.ppermute(value, ('pipe', 'seq'), spread(pairs_of))  11.8 us
    ppermute x6, starting transfers between devices, hop(): return lax.ppermute(value, ('pipe', 'seq'), spread(pairs_of))  10.5 us
    ppermute x10, starting transfers between devices, near(): return lax.ppermute(value, 'seq', near_pairs)  10.3 us
    pallas_call x1, Pallas kernels, body(): call(functools.partial(prep_kernel, sections - 1), 'prep', [anywhere] * 9...  7.73 us
    ppermute x1, starting transfers between devices, far_within(): return lax.ppermute(value, ('pipe', 'seq'), moves)  2.67 us
    pallas_call x3, Pallas kernels, body(): call(functools.partial(own_kernel, source - 1, scaling), 'own', [vmem] *...  2.4 us
  transfers between devices with their start and end apart: 26, of which 12 were waited for; matrix products, arithmetic and copies ran while one was open for 0% of the time, Pallas kernels for 18%

profile of v3, /device:TPU:1, one launch (start us, length us, event | category | flops | bytes accessed | tf_op | source)
XLA Modules:
  0.0 80.6 jit_solution(13651605175132535990)
XLA Ops:
  0.1 2.6 %collective-permute-start.1 = (bf16[128,1536]{1,0:T(8,128)(2,1)}, bf16[128,1536]{1,0:T(8,128)(2,1)S(1)}, u32[]{:S(2)}, u32[]{:S(2)}) collective-permute-start(bf16[128,1536]{1,0:T(8,128)(2,1)} %bitcast.15), channel_id=1, source_target_pairs={{0,16},{1,2},{2,1},{3,4},{4,3},{5,6},{6,5},{7,23},{8,24},{9,10},{1... | collective-permute-start | bytes 1179656 | tf_op jit(solution)/shard_map/ppermute | solution.py:461
  2.8 7.7 %prep.1 = (bf16[1536,1536]{1,0:T(8,128)(2,1)S(1)}, bf16[1536,1536]{1,0:T(8,128)(2,1)S(1)}, bf16[1536,1536]{1,0:T(8,128)(2,1)S(1)}, bf16[1536,1536]{1,0:T(8,128)(...) custom-call(bf16[1536,1536]{1,0:T(8,128)(2,1)} %bitcast.9, ...), custom_call_target="tpu_custom_call" | custom-call | tf_op jit(solution)/shard_map/prep/pallas_call | solution.py:513
  12.9 1.6 %collective-permute-start.5 = (bf16[128,1536]{1,0:T(8,128)(2,1)S(1)}, bf16[128,1536]{1,0:T(8,128)(2,1)S(1)}, u32[]{:S(2)}, u32[]{:S(2)}) collective-permute-start(bf16[128,1536]{1,0:T(8,128)(2,1)S(1)} %get-tuple-element.74), channel_id=1, source_target_pairs={{0,16},{1,2},{2,1},{3,4},{4,3},{5,6},{6,5},{7,23},{8,24},{9,10},{1... | collective-permute-start | bytes 1179656 | tf_op jit(solution)/shard_map/ppermute | solution.py:461
  16.1 2.7 %collective-permute-start.13 = (bf16[6,384,256]{2,1,0:T(8,128)(2,1)S(1)}, bf16[6,384,256]{2,1,0:T(8,128)(2,1)S(1)}, u32[]{:S(2)}, u32[]{:S(2)}) collective-permute-start(bf16[6,384,256]{2,1,0:T(8,128)(2,1)S(1)} %get-tuple-element.73.after), channel_id=1, source_target_pairs={{1,2},{3,4},{5,6},{2,1},{4,3},{6,5},{9,10},{11,12},{13,14},{10,9},... | collective-permute-start | bytes 3538952 | tf_op jit(solution)/shard_map/ppermute | solution.py:465
  18.8 1.7 %collective-permute-done.5.refs_0_.far = bf16[128,1536]{1,0:T(8,128)(2,1)S(1)} collective-permute-done((bf16[128,1536]{1,0:T(8,128)(2,1)S(1)}, bf16[128,1536]{1,0:T(8,128)(2,1)S(1)}, u32[]{:S(2)}, u32[]{:S(2)}) %collective-permute-start.5) | collective-permute-done | bytes 393248 | tf_op jit(solution)/shard_map/ppermute | solution.py:461
  20.6 2.3 %collective-permute-start.6 = (bf16[128,768]{1,0:T(8,128)(2,1)S(1)}, bf16[128,768]{1,0:T(8,128)(2,1)S(1)}, u32[]{:S(2)}, u32[]{:S(2)}) collective-permute-start(bf16[128,768]{1,0:T(8,128)(2,1)S(1)} %get-tuple-element.75.refs_0_), channel_id=1, source_target_pairs={{0,8},{1,9},{2,10},{3,11},{4,12},{5,13},{6,14},{7,15},{8,0},{9,1},... | collective-permute-start | bytes 589832 | tf_op jit(solution)/shard_map/ppermute | solution.py:471
  23.0 2.9 %collective-permute-done.6.xa_ref.xa = bf16[128,768]{1,0:T(8,128)(2,1)S(1)} collective-permute-done((bf16[128,768]{1,0:T(8,128)(2,1)S(1)}, bf16[128,768]{1,0:T(8,128)(2,1)S(1)}, u32[]{:S(2)}, u32[]{:S(2)}) %collective-permute-start.6) | collective-permute-done | bytes 196640 | tf_op jit(solution)/shard_map/ppermute | solution.py:471
  25.9 3.7 %collective-permute-start.8 = (bf16[128,768]{1,0:T(8,128)(2,1)S(1)}, bf16[128,768]{1,0:T(8,128)(2,1)S(1)}, u32[]{:S(2)}, u32[]{:S(2)}) collective-permute-start(bf16[128,768]{1,0:T(8,128)(2,1)S(1)} %get-tuple-element.78), channel_id=1, source_target_pairs={{0,16},{1,2},{2,1},{3,4},{4,3},{5,6},{6,5},{7,23},{8,24},{9,10},{1... | collective-permute-start | bytes 589832 | tf_op jit(solution)/shard_map/ppermute | solution.py:461
  29.6 4.1 %collective-permute-start.9 = (bf16[128,768]{1,0:T(8,128)(2,1)S(1)}, bf16[128,768]{1,0:T(8,128)(2,1)S(1)}, u32[]{:S(2)}, u32[]{:S(2)}) collective-permute-start(bf16[128,768]{1,0:T(8,128)(2,1)S(1)} %get-tuple-element.78), channel_id=1, source_target_pairs={{0,1},{1,0},{2,3},{3,2},{4,5},{5,4},{6,7},{7,6},{8,9},{9,8},{10,11... | collective-permute-start | bytes 589832 | tf_op jit(solution)/shard_map/ppermute | solution.py:444
  33.9 2.1 %collective-permute-done.8.refs_0_.xfa = bf16[128,768]{1,0:T(8,128)(2,1)S(1)} collective-permute-done((bf16[128,768]{1,0:T(8,128)(2,1)S(1)}, bf16[128,768]{1,0:T(8,128)(2,1)S(1)}, u32[]{:S(2)}, u32[]{:S(2)}) %collective-permute-start.8) | collective-permute-done | bytes 196640 | tf_op jit(solution)/shard_map/ppermute | solution.py:461
  36.0 3.1 %collective-permute-done.12.xb = bf16[128,768]{1,0:T(8,128)(2,1)S(1)} collective-permute-done((bf16[128,768]{1,0:T(8,128)(2,1)S(1)}, bf16[128,768]{1,0:T(8,128)(2,1)S(1)}, u32[]{:S(2)}, u32[]{:S(2)}) %collective-permute-start.12) | collective-permute-done | bytes 196640 | tf_op jit(solution)/shard_map/ppermute | solution.py:461
  39.1 3.6 %collective-permute-start.14 = (bf16[128,768]{1,0:T(8,128)(2,1)S(1)}, bf16[128,768]{1,0:T(8,128)(2,1)S(1)}, u32[]{:S(2)}, u32[]{:S(2)}) collective-permute-start(bf16[128,768]{1,0:T(8,128)(2,1)S(1)} %get-tuple-element.87.refs_2_), channel_id=1, source_target_pairs={{0,24},{1,25},{2,26},{3,27},{4,28},{5,29},{6,30},{7,31},{8,16},{9,... | collective-permute-start | bytes 589832 | tf_op jit(solution)/shard_map/ppermute | solution.py:471
  42.7 4.9 %collective-permute-done.14.xa_ref.xa = bf16[128,768]{1,0:T(8,128)(2,1)S(1)} collective-permute-done((bf16[128,768]{1,0:T(8,128)(2,1)S(1)}, bf16[128,768]{1,0:T(8,128)(2,1)S(1)}, u32[]{:S(2)}, u32[]{:S(2)}) %collective-permute-start.14) | collective-permute-done | bytes 196640 | tf_op jit(solution)/shard_map/ppermute | solution.py:471
  47.6 1.8 %collective-permute-start.15 = (bf16[128,768]{1,0:T(8,128)(2,1)S(1)}, bf16[128,768]{1,0:T(8,128)(2,1)S(1)}, u32[]{:S(2)}, u32[]{:S(2)}) collective-permute-start(bf16[128,768]{1,0:T(8,128)(2,1)S(1)} %get-tuple-element.88), channel_id=1, source_target_pairs={{0,16},{1,2},{2,1},{3,4},{4,3},{5,6},{6,5},{7,23},{8,24},{9,10},{1... | collective-permute-start | bytes 589832 | tf_op jit(solution)/shard_map/ppermute | solution.py:461
  49.4 3.2 %collective-permute-start.16 = (bf16[128,768]{1,0:T(8,128)(2,1)S(1)}, bf16[128,768]{1,0:T(8,128)(2,1)S(1)}, u32[]{:S(2)}, u32[]{:S(2)}) collective-permute-start(bf16[128,768]{1,0:T(8,128)(2,1)S(1)} %get-tuple-element.88), channel_id=1, source_target_pairs={{0,1},{1,0},{2,3},{3,2},{4,5},{5,4},{6,7},{7,6},{8,9},{9,8},{10,11... | collective-permute-start | bytes 589832 | tf_op jit(solution)/shard_map/ppermute | solution.py:444
  54.0 4.1 %collective-permute-done.19.xb = bf16[128,768]{1,0:T(8,128)(2,1)S(1)} collective-permute-done((bf16[128,768]{1,0:T(8,128)(2,1)S(1)}, bf16[128,768]{1,0:T(8,128)(2,1)S(1)}, u32[]{:S(2)}, u32[]{:S(2)}) %collective-permute-start.19) | collective-permute-done | bytes 196640 | tf_op jit(solution)/shard_map/ppermute | solution.py:461
  58.2 3.4 %collective-permute-start.20 = (bf16[128,768]{1,0:T(8,128)(2,1)S(1)}, bf16[128,768]{1,0:T(8,128)(2,1)S(1)}, u32[]{:S(2)}, u32[]{:S(2)}) collective-permute-start(bf16[128,768]{1,0:T(8,128)(2,1)S(1)} %get-tuple-element.99.refs_4_), channel_id=1, source_target_pairs={{0,8},{1,9},{2,10},{3,11},{4,12},{5,13},{6,14},{7,15},{8,0},{9,1},... | collective-permute-start | bytes 589832 | tf_op jit(solution)/shard_map/ppermute | solution.py:471
  62.7 3.8 %collective-permute-done.20.xa_ref.xa = bf16[128,768]{1,0:T(8,128)(2,1)S(1)} collective-permute-done((bf16[128,768]{1,0:T(8,128)(2,1)S(1)}, bf16[128,768]{1,0:T(8,128)(2,1)S(1)}, u32[]{:S(2)}, u32[]{:S(2)}) %collective-permute-start.20) | collective-permute-done | bytes 196640 | tf_op jit(solution)/shard_map/ppermute | solution.py:471
  67.0 1.9 %collective-permute-start.21 = (bf16[128,768]{1,0:T(8,128)(2,1)S(1)}, bf16[128,768]{1,0:T(8,128)(2,1)S(1)}, u32[]{:S(2)}, u32[]{:S(2)}) collective-permute-start(bf16[128,768]{1,0:T(8,128)(2,1)S(1)} %get-tuple-element.100), channel_id=1, source_target_pairs={{0,16},{1,2},{2,1},{3,4},{4,3},{5,6},{6,5},{7,23},{8,24},{9,10},{1... | collective-permute-start | bytes 589832 | tf_op jit(solution)/shard_map/ppermute | solution.py:461
  69.4 1.3 %collective-permute-done.23.xb.own_x = bf16[128,768]{1,0:T(8,128)(2,1)S(1)} collective-permute-done((bf16[128,768]{1,0:T(8,128)(2,1)S(1)}, bf16[128,768]{1,0:T(8,128)(2,1)S(1)}, u32[]{:S(2)}, u32[]{:S(2)}) %collective-permute-start.23) | collective-permute-done | bytes 196640 | tf_op jit(solution)/shard_map/ppermute | solution.py:471
  72.6 2.4 %own.5 = (bf16[128,1536]{1,0:T(8,128)(2,1)S(1)}, f32[128,1536]{1,0:T(8,128)S(1)}, f32[128,1536]{1,0:T(8,128)S(1)}, f32[128,768]{1,0:T(8,128)S(1)}) custom-call(f32[128,1536]{1,0:T(8,128)S(1)} %get-tuple-element.104.acc, bf16[128,768]{1,0:T(8,128)(2,1)S(1)} %collective-permute-done.20.xa_ref.xa, bf16[128,768]{1,0:T(8,128)(2,1)S(1)} %collective-permute-done.23.xb.own_x, ...), custom_call_target="tpu_custom_call" | custom-call | tf_op jit(solution)/shard_map/own/pallas_call | solution.py:610
  75.0 1.6 %near.5 = (f32[128,1536]{1,0:T(8,128)S(1)}, f32[128,1536]{1,0:T(8,128)S(1)}, f32[128,1536]{1,0:T(8,128)S(1)}) custom-call(bf16[128,768]{1,0:T(8,128)(2,1)S(1)} %collective-permute-done.21.refs_0_.xfa, bf16[128,768]{1,0:T(8,128)(2,1)S(1)} %collective-permute-done.22.refs_1_.xa, bf16[128,768]{1,0:T(8,128)(2,1)S(1)} %collective-permute-done.24.xb, ...), custom_call_target="tpu_custom_call" | custom-call | tf_op jit(solution)/shard_map/near/pallas_call | solution.py:622
  76.9 1.7 %far.5 = (bf16[128,768]{1,0:T(8,128)(2,1)S(1)}, bf16[128,1536]{1,0:T(8,128)(2,1)S(1)}, bf16[128,1536]{1,0:T(8,128)(2,1)S(1)}) custom-call(f32[128,1536]{1,0:T(8,128)S(1)} %get-tuple-element.107.acc, bf16[128,768]{1,0:T(8,128)(2,1)S(1)} %collective-permute-done.25.xb, bf16[1536,1536]{1,0:T(8,128)(2,1)S(1)} %get-tuple-element.76.wot, ...), custom_call_target="tpu_custom_call" | custom-call | tf_op jit(solution)/shard_map/far/pallas_call | solution.py:629
  78.6 1.8 %finish.1 = bf16[128,1536]{1,0:T(8,128)(2,1)} custom-call(bf16[128,1536]{1,0:T(8,128)(2,1)S(1)} %get-tuple-element.111.dk, bf16[128,1536]{1,0:T(8,128)(2,1)S(1)} %get-tuple-element.112.dv, bf16[128,1536]{1,0:T(8,128)(2,1)S(1)} %get-tuple-element.113.dq, bf16[128,768]{1,0:T(8,128)(2,1)S(1)} %collective-permute-done.23.xb.own_x, ...), custom_call_target="tpu_custom_call" | custom-call | tf_op jit(solution)/shard_map/finish/pallas_call | solution.py:642
  (58 shorter events, 10.3 us)
Async XLA Ops:
  0.0 10.9 %collective-permute-start = (bf16[128,1536]{1,0:T(8,128)(2,1)}, bf16[128,1536]{1,0:T(8,128)(2,1)S(1)}, u32[]{:S(2)}, u32[]{:S(2)}) collective-permute-start(bf16[128,1536]{1,0:T(8,128)(2,1)} %bitcast.14), channel_id=1, source_target_pairs={{0,1},{1,0},{2,3},{3,2},{4,5},{5,4},{6,7},{7,6},{8,9},{9,8},{10,11... | collective-permute-start | bytes 1179656 | tf_op jit(solution)/shard_map/ppermute | solution.py:444
  0.1 10.8 %collective-permute-start.1 = (bf16[128,1536]{1,0:T(8,128)(2,1)}, bf16[128,1536]{1,0:T(8,128)(2,1)S(1)}, u32[]{:S(2)}, u32[]{:S(2)}) collective-permute-start(bf16[128,1536]{1,0:T(8,128)(2,1)} %bitcast.15), channel_id=1, source_target_pairs={{0,16},{1,2},{2,1},{3,4},{4,3},{5,6},{6,5},{7,23},{8,24},{9,10},{1... | collective-permute-start | bytes 1179656 | tf_op jit(solution)/shard_map/ppermute | solution.py:461
  2.7 10.1 %collective-permute-start.3 = (bf16[128,1536]{1,0:T(8,128)(2,1)}, bf16[128,1536]{1,0:T(8,128)(2,1)S(1)}, u32[]{:S(2)}, u32[]{:S(2)}) collective-permute-start(bf16[128,1536]{1,0:T(8,128)(2,1)} %bitcast.17), channel_id=1, source_target_pairs={{0,16},{1,2},{2,1},{3,4},{4,3},{5,6},{6,5},{7,23},{8,24},{9,10},{1... | collective-permute-start | bytes 1179656 | tf_op jit(solution)/shard_map/ppermute | solution.py:461
  10.5 2.4 %collective-permute-start.2 = (bf16[128,1536]{1,0:T(8,128)(2,1)S(1)}, bf16[128,1536]{1,0:T(8,128)(2,1)S(1)}, u32[]{:S(2)}, u32[]{:S(2)}) collective-permute-start(bf16[128,1536]{1,0:T(8,128)(2,1)S(1)} %get-tuple-element.66.v0.v), channel_id=1, source_target_pairs={{0,1},{1,0},{2,3},{3,2},{4,5},{5,4},{6,7},{7,6},{8,9},{9,8},{10,11... | collective-permute-start | bytes 1179656 | tf_op jit(solution)/shard_map/ppermute | solution.py:444
  12.9 7.6 %collective-permute-start.5 = (bf16[128,1536]{1,0:T(8,128)(2,1)S(1)}, bf16[128,1536]{1,0:T(8,128)(2,1)S(1)}, u32[]{:S(2)}, u32[]{:S(2)}) collective-permute-start(bf16[128,1536]{1,0:T(8,128)(2,1)S(1)} %get-tuple-element.74), channel_id=1, source_target_pairs={{0,16},{1,2},{2,1},{3,4},{4,3},{5,6},{6,5},{7,23},{8,24},{9,10},{1... | collective-permute-start | bytes 1179656 | tf_op jit(solution)/shard_map/ppermute | solution.py:461
  15.0 7.9 %collective-permute-start.7 = (bf16[6,384,256]{2,1,0:T(8,128)(2,1)S(1)}, bf16[6,384,256]{2,1,0:T(8,128)(2,1)S(1)}, u32[]{:S(2)}, u32[]{:S(2)}) collective-permute-start(bf16[6,384,256]{2,1,0:T(8,128)(2,1)S(1)} %get-tuple-element.77), channel_id=1, source_target_pairs={{0,1},{1,0},{2,3},{3,2},{4,5},{5,4},{6,7},{7,6},{8,9},{9,8},{10,11... | collective-permute-start | bytes 3538952 | tf_op jit(solution)/shard_map/ppermute | solution.py:444
  16.0 4.5 %collective-permute-start.4 = (bf16[128,1536]{1,0:T(8,128)(2,1)S(1)}, bf16[128,1536]{1,0:T(8,128)(2,1)S(1)}, u32[]{:S(2)}, u32[]{:S(2)}) collective-permute-start(bf16[128,1536]{1,0:T(8,128)(2,1)S(1)} %first_near.1.after), channel_id=1, source_target_pairs={{0,1},{1,0},{2,3},{3,2},{4,5},{5,4},{6,7},{7,6},{8,9},{9,8},{10,11... | collective-permute-start | bytes 1179656 | tf_op jit(solution)/shard_map/ppermute | solution.py:444
  16.1 17.7 %collective-permute-start.13 = (bf16[6,384,256]{2,1,0:T(8,128)(2,1)S(1)}, bf16[6,384,256]{2,1,0:T(8,128)(2,1)S(1)}, u32[]{:S(2)}, u32[]{:S(2)}) collective-permute-start(bf16[6,384,256]{2,1,0:T(8,128)(2,1)S(1)} %get-tuple-element.73.after), channel_id=1, source_target_pairs={{1,2},{3,4},{5,6},{2,1},{4,3},{6,5},{9,10},{11,12},{13,14},{10,9},... | collective-permute-start | bytes 3538952 | tf_op jit(solution)/shard_map/ppermute | solution.py:465
  20.6 5.3 %collective-permute-start.6 = (bf16[128,768]{1,0:T(8,128)(2,1)S(1)}, bf16[128,768]{1,0:T(8,128)(2,1)S(1)}, u32[]{:S(2)}, u32[]{:S(2)}) collective-permute-start(bf16[128,768]{1,0:T(8,128)(2,1)S(1)} %get-tuple-element.75.refs_0_), channel_id=1, source_target_pairs={{0,8},{1,9},{2,10},{3,11},{4,12},{5,13},{6,14},{7,15},{8,0},{9,1},... | collective-permute-start | bytes 589832 | tf_op jit(solution)/shard_map/ppermute | solution.py:471
  22.8 10.9 %collective-permute-start.10 = (bf16[128,768]{1,0:T(8,128)(2,1)S(1)}, bf16[128,768]{1,0:T(8,128)(2,1)S(1)}, u32[]{:S(2)}, u32[]{:S(2)}) collective-permute-start(bf16[128,768]{1,0:T(8,128)(2,1)S(1)} %get-tuple-element.79.refs_1_), channel_id=1, source_target_pairs={{0,8},{1,9},{2,10},{3,11},{4,12},{5,13},{6,14},{7,15},{8,0},{9,1},... | collective-permute-start | bytes 589832 | tf_op jit(solution)/shard_map/ppermute | solution.py:471
  25.9 10.1 %collective-permute-start.8 = (bf16[128,768]{1,0:T(8,128)(2,1)S(1)}, bf16[128,768]{1,0:T(8,128)(2,1)S(1)}, u32[]{:S(2)}, u32[]{:S(2)}) collective-permute-start(bf16[128,768]{1,0:T(8,128)(2,1)S(1)} %get-tuple-element.78), channel_id=1, source_target_pairs={{0,16},{1,2},{2,1},{3,4},{4,3},{5,6},{6,5},{7,23},{8,24},{9,10},{1... | collective-permute-start | bytes 589832 | tf_op jit(solution)/shard_map/ppermute | solution.py:461
  29.6 6.3 %collective-permute-start.9 = (bf16[128,768]{1,0:T(8,128)(2,1)S(1)}, bf16[128,768]{1,0:T(8,128)(2,1)S(1)}, u32[]{:S(2)}, u32[]{:S(2)}) collective-permute-start(bf16[128,768]{1,0:T(8,128)(2,1)S(1)} %get-tuple-element.78), channel_id=1, source_target_pairs={{0,1},{1,0},{2,3},{3,2},{4,5},{5,4},{6,7},{7,6},{8,9},{9,8},{10,11... | collective-permute-start | bytes 589832 | tf_op jit(solution)/shard_map/ppermute | solution.py:444
  33.7 5.4 %collective-permute-start.12 = (bf16[128,768]{1,0:T(8,128)(2,1)S(1)}, bf16[128,768]{1,0:T(8,128)(2,1)S(1)}, u32[]{:S(2)}, u32[]{:S(2)}) collective-permute-start(bf16[128,768]{1,0:T(8,128)(2,1)S(1)} %collective-permute-done.10.xb.own_x), channel_id=1, source_target_pairs={{0,16},{1,2},{2,1},{3,4},{4,3},{5,6},{6,5},{7,23},{8,24},{9,10},{1... | collective-permute-start | bytes 589832 | tf_op jit(solution)/shard_map/ppermute | solution.py:461
  39.1 8.5 %collective-permute-start.14 = (bf16[128,768]{1,0:T(8,128)(2,1)S(1)}, bf16[128,768]{1,0:T(8,128)(2,1)S(1)}, u32[]{:S(2)}, u32[]{:S(2)}) collective-permute-start(bf16[128,768]{1,0:T(8,128)(2,1)S(1)} %get-tuple-element.87.refs_2_), channel_id=1, source_target_pairs={{0,24},{1,25},{2,26},{3,27},{4,28},{5,29},{6,30},{7,31},{8,16},{9,... | collective-permute-start | bytes 589832 | tf_op jit(solution)/shard_map/ppermute | solution.py:471
  42.7 9.9 %collective-permute-start.17 = (bf16[128,768]{1,0:T(8,128)(2,1)S(1)}, bf16[128,768]{1,0:T(8,128)(2,1)S(1)}, u32[]{:S(2)}, u32[]{:S(2)}) collective-permute-start(bf16[128,768]{1,0:T(8,128)(2,1)S(1)} %rest.2.refs_3_), channel_id=1, source_target_pairs={{0,24},{1,25},{2,26},{3,27},{4,28},{5,29},{6,30},{7,31},{8,16},{9,... | collective-permute-start | bytes 589832 | tf_op jit(solution)/shard_map/ppermute | solution.py:471
  47.6 5.8 %collective-permute-start.15 = (bf16[128,768]{1,0:T(8,128)(2,1)S(1)}, bf16[128,768]{1,0:T(8,128)(2,1)S(1)}, u32[]{:S(2)}, u32[]{:S(2)}) collective-permute-start(bf16[128,768]{1,0:T(8,128)(2,1)S(1)} %get-tuple-element.88), channel_id=1, source_target_pairs={{0,16},{1,2},{2,1},{3,4},{4,3},{5,6},{6,5},{7,23},{8,24},{9,10},{1... | collective-permute-start | bytes 589832 | tf_op jit(solution)/shard_map/ppermute | solution.py:461
  49.4 4.2 %collective-permute-start.16 = (bf16[128,768]{1,0:T(8,128)(2,1)S(1)}, bf16[128,768]{1,0:T(8,128)(2,1)S(1)}, u32[]{:S(2)}, u32[]{:S(2)}) collective-permute-start(bf16[128,768]{1,0:T(8,128)(2,1)S(1)} %get-tuple-element.88), channel_id=1, source_target_pairs={{0,1},{1,0},{2,3},{3,2},{4,5},{5,4},{6,7},{7,6},{8,9},{9,8},{10,11... | collective-permute-start | bytes 589832 | tf_op jit(solution)/shard_map/ppermute | solution.py:444
  52.8 5.4 %collective-permute-start.19 = (bf16[128,768]{1,0:T(8,128)(2,1)S(1)}, bf16[128,768]{1,0:T(8,128)(2,1)S(1)}, u32[]{:S(2)}, u32[]{:S(2)}) collective-permute-start(bf16[128,768]{1,0:T(8,128)(2,1)S(1)} %collective-permute-done.17.xb.own_x), channel_id=1, source_target_pairs={{0,16},{1,2},{2,1},{3,4},{4,3},{5,6},{6,5},{7,23},{8,24},{9,10},{1... | collective-permute-start | bytes 589832 | tf_op jit(solution)/shard_map/ppermute | solution.py:461
  58.2 8.4 %collective-permute-start.20 = (bf16[128,768]{1,0:T(8,128)(2,1)S(1)}, bf16[128,768]{1,0:T(8,128)(2,1)S(1)}, u32[]{:S(2)}, u32[]{:S(2)}) collective-permute-start(bf16[128,768]{1,0:T(8,128)(2,1)S(1)} %get-tuple-element.99.refs_4_), channel_id=1, source_target_pairs={{0,8},{1,9},{2,10},{3,11},{4,12},{5,13},{6,14},{7,15},{8,0},{9,1},... | collective-permute-start | bytes 589832 | tf_op jit(solution)/shard_map/ppermute | solution.py:471
  61.6 9.2 %collective-permute-start.23 = (bf16[128,768]{1,0:T(8,128)(2,1)S(1)}, bf16[128,768]{1,0:T(8,128)(2,1)S(1)}, u32[]{:S(2)}, u32[]{:S(2)}) collective-permute-start(bf16[128,768]{1,0:T(8,128)(2,1)S(1)} %rest.3.refs_5_), channel_id=1, source_target_pairs={{0,8},{1,9},{2,10},{3,11},{4,12},{5,13},{6,14},{7,15},{8,0},{9,1},... | collective-permute-start | bytes 589832 | tf_op jit(solution)/shard_map/ppermute | solution.py:471
  67.0 8.0 %collective-permute-start.21 = (bf16[128,768]{1,0:T(8,128)(2,1)S(1)}, bf16[128,768]{1,0:T(8,128)(2,1)S(1)}, u32[]{:S(2)}, u32[]{:S(2)}) collective-permute-start(bf16[128,768]{1,0:T(8,128)(2,1)S(1)} %get-tuple-element.100), channel_id=1, source_target_pairs={{0,16},{1,2},{2,1},{3,4},{4,3},{5,6},{6,5},{7,23},{8,24},{9,10},{1... | collective-permute-start | bytes 589832 | tf_op jit(solution)/shard_map/ppermute | solution.py:461
  68.9 6.1 %collective-permute-start.22 = (bf16[128,768]{1,0:T(8,128)(2,1)S(1)}, bf16[128,768]{1,0:T(8,128)(2,1)S(1)}, u32[]{:S(2)}, u32[]{:S(2)}) collective-permute-start(bf16[128,768]{1,0:T(8,128)(2,1)S(1)} %get-tuple-element.100), channel_id=1, source_target_pairs={{0,1},{1,0},{2,3},{3,2},{4,5},{5,4},{6,7},{7,6},{8,9},{9,8},{10,11... | collective-permute-start | bytes 589832 | tf_op jit(solution)/shard_map/ppermute | solution.py:444
  70.7 4.3 %collective-permute-start.24 = (bf16[128,768]{1,0:T(8,128)(2,1)S(1)}, bf16[128,768]{1,0:T(8,128)(2,1)S(1)}, u32[]{:S(2)}, u32[]{:S(2)}) collective-permute-start(bf16[128,768]{1,0:T(8,128)(2,1)S(1)} %collective-permute-done.23.xb.own_x), channel_id=1, source_target_pairs={{0,1},{1,0},{2,3},{3,2},{4,5},{5,4},{6,7},{7,6},{8,9},{9,8},{10,11... | collective-permute-start | bytes 589832 | tf_op jit(solution)/shard_map/ppermute | solution.py:444
  71.6 5.3 %collective-permute-start.25 = (bf16[128,768]{1,0:T(8,128)(2,1)S(1)}, bf16[128,768]{1,0:T(8,128)(2,1)S(1)}, u32[]{:S(2)}, u32[]{:S(2)}) collective-permute-start(bf16[128,768]{1,0:T(8,128)(2,1)S(1)} %collective-permute-done.23.xb.own_x), channel_id=1, source_target_pairs={{0,16},{1,2},{2,1},{3,4},{4,3},{5,6},{6,5},{7,23},{8,24},{9,10},{1... | collective-permute-start | bytes 589832 | tf_op jit(solution)/shard_map/ppermute | solution.py:461
  (2 other events, 3.7 us)

commit v4 on v2

--- a/solution.py
+++ b/solution.py
@@ -30,6 +30,7 @@
 
 
 def prep_kernel(
+    last,
     wo_hbm,
     wk_hbm,
     wv_hbm,
@@ -49,6 +50,7 @@
     x,
     qbd,
     keep,
+    bd,
     raw,
     flags,
     sems,
@@ -88,6 +90,12 @@
             for r in range(0, rows, TILE):
                 part = pl.ds(start + r, TILE)
                 dst[:, part] = raw[n, part, :].T
+
+        if n == 0:
+
+            @pl.when(lax.axis_index("pipe") == last)
+            def _():
+                fill_diagonal(bd, wot, x[...], None)
     window_copy.wait()
     tile = lax.axis_index("seq")
     odd = lax.rem(tile, 2)
@@ -205,12 +213,6 @@
     return dot_nn(dk[...], wkt[:, part]) + dot_nn(dv[...], wvt[:, part])
 
 
-def first_out_kernel(last, x, wot, bd):
-    @pl.when(lax.axis_index("pipe") == last)
-    def _():
-        fill_diagonal(bd, wot, x[...], None)
-
-
 def first_far_kernel(
     last, scaling, bd, qbd, pt, v0, v1, v2, wkt, wvt, far_ref, ds_ref, dk, dv, dp
 ):
@@ -494,8 +496,8 @@
     k2 = far(key_rows[0])
     v2 = far(value_rows[0])
     k1 = near(key_rows[0])
-    wot, wkt, wvt, wqt, q, k, v, x, qbd, keep = call(
-        prep_kernel,
+    wot, wkt, wvt, wqt, q, k, v, x, qbd, keep, bd = call(
+        functools.partial(prep_kernel, sections - 1),
         "prep",
         [anywhere] * 9,
         [
@@ -509,6 +511,7 @@
             tile,
             diagonal,
             pltpu.VMEM((2, pairs, 8, 2 * TILE), jnp.int32),
+            diagonal,
         ],
         [
             pltpu.VMEM((4, model, width), bf16),
@@ -544,10 +547,7 @@
         [dp_scratch],
     )(keep, qbd, k, k1, clean(k2, k1))
 
-    bd = call(
-        functools.partial(first_out_kernel, sections - 1), "first_out", [vmem] * 2, diagonal
-    )(x, wot)
-    v2 = clean(v2, pt, bd)
+    v2 = clean(v2, pt)
     to_far, ds = call(
         functools.partial(first_far_kernel, sections - 1, scaling),
         "first_far",

time: 81 us -> 81 us (level)
    pallas_call x2 -> x1, Pallas kernels: 7.73 us -> 7.73 us  [body(): call(functools.partial(prep_kernel, sections - 1), 'prep', [anywhere] * 9...]
where the time goes in v4:
time: 81 us; the launch traced here: 80.5 us
  starting transfers between devices  36.9 us (46%)
  waiting for transfers between devices  25.3 us (31%)
  Pallas kernels  18 us (22%)
    ppermute x9, starting transfers between devices, far(): return lax.ppermute(value, ('pipe', 'seq'), spread(pairs_of))  13.4 us
    ppermute x6, waiting for transfers between devices, hop(): return lax.ppermute(value, ('pipe', 'seq'), spread(pairs_of))  12.9 us
    ppermute x9, waiting for transfers between devices, far(): return lax.ppermute(value, ('pipe', 'seq'), spread(pairs_of))  11.8 us
    ppermute x6, starting transfers between devices, hop(): return lax.ppermute(value, ('pipe', 'seq'), spread(pairs_of))  10.5 us
    ppermute x10, starting transfers between devices, near(): return lax.ppermute(value, 'seq', near_pairs)  10.3 us
    pallas_call x1, Pallas kernels, body(): call(functools.partial(prep_kernel, sections - 1), 'prep', [anywhere] * 9...  7.73 us
    ppermute x1, starting transfers between devices, far_within(): return lax.ppermute(value, ('pipe', 'seq'), moves)  2.67 us
    pallas_call x3, Pallas kernels, body(): call(functools.partial(own_kernel, source - 1, scaling), 'own', [vmem] *...  2.4 us
  transfers between devices with their start and end apart: 26, of which 12 were waited for; matrix products, arithmetic and copies ran while one was open for 0% of the time, Pallas kernels for 18%

profile of v4, /device:TPU:1, one launch (start us, length us, event | category | flops | bytes accessed | tf_op | source)
XLA Modules:
  0.0 80.5 jit_solution(16032009292671322896)
XLA Ops:
  0.1 2.6 %collective-permute-start.1 = (bf16[128,1536]{1,0:T(8,128)(2,1)}, bf16[128,1536]{1,0:T(8,128)(2,1)S(1)}, u32[]{:S(2)}, u32[]{:S(2)}) collective-permute-start(bf16[128,1536]{1,0:T(8,128)(2,1)} %bitcast.15), channel_id=1, source_target_pairs={{0,16},{1,2},{2,1},{3,4},{4,3},{5,6},{6,5},{7,23},{8,24},{9,10},{1... | collective-permute-start | bytes 1179656 | tf_op jit(solution)/shard_map/ppermute | solution.py:447
  2.8 7.7 %prep.1 = (bf16[1536,1536]{1,0:T(8,128)(2,1)S(1)}, bf16[1536,1536]{1,0:T(8,128)(2,1)S(1)}, bf16[1536,1536]{1,0:T(8,128)(2,1)S(1)}, bf16[1536,1536]{1,0:T(8,128)(...) custom-call(bf16[1536,1536]{1,0:T(8,128)(2,1)} %bitcast.9, ...), custom_call_target="tpu_custom_call" | custom-call | tf_op jit(solution)/shard_map/prep/pallas_call | solution.py:499
  12.9 1.6 %collective-permute-start.5 = (bf16[128,1536]{1,0:T(8,128)(2,1)S(1)}, bf16[128,1536]{1,0:T(8,128)(2,1)S(1)}, u32[]{:S(2)}, u32[]{:S(2)}) collective-permute-start(bf16[128,1536]{1,0:T(8,128)(2,1)S(1)} %get-tuple-element.74), channel_id=1, source_target_pairs={{0,16},{1,2},{2,1},{3,4},{4,3},{5,6},{6,5},{7,23},{8,24},{9,10},{1... | collective-permute-start | bytes 1179656 | tf_op jit(solution)/shard_map/ppermute | solution.py:447
  16.1 2.7 %collective-permute-start.13 = (bf16[6,384,256]{2,1,0:T(8,128)(2,1)S(1)}, bf16[6,384,256]{2,1,0:T(8,128)(2,1)S(1)}, u32[]{:S(2)}, u32[]{:S(2)}) collective-permute-start(bf16[6,384,256]{2,1,0:T(8,128)(2,1)S(1)} %get-tuple-element.73.after), channel_id=1, source_target_pairs={{1,2},{3,4},{5,6},{2,1},{4,3},{6,5},{9,10},{11,12},{13,14},{10,9},... | collective-permute-start | bytes 3538952 | tf_op jit(solution)/shard_map/ppermute | solution.py:451
  18.8 1.7 %collective-permute-done.5.refs_0_.far = bf16[128,1536]{1,0:T(8,128)(2,1)S(1)} collective-permute-done((bf16[128,1536]{1,0:T(8,128)(2,1)S(1)}, bf16[128,1536]{1,0:T(8,128)(2,1)S(1)}, u32[]{:S(2)}, u32[]{:S(2)}) %collective-permute-start.5) | collective-permute-done | bytes 393248 | tf_op jit(solution)/shard_map/ppermute | solution.py:447
  20.6 2.3 %collective-permute-start.6 = (bf16[128,768]{1,0:T(8,128)(2,1)S(1)}, bf16[128,768]{1,0:T(8,128)(2,1)S(1)}, u32[]{:S(2)}, u32[]{:S(2)}) collective-permute-start(bf16[128,768]{1,0:T(8,128)(2,1)S(1)} %get-tuple-element.75.refs_0_), channel_id=1, source_target_pairs={{0,8},{1,9},{2,10},{3,11},{4,12},{5,13},{6,14},{7,15},{8,0},{9,1},... | collective-permute-start | bytes 589832 | tf_op jit(solution)/shard_map/ppermute | solution.py:457
  23.0 2.9 %collective-permute-done.6.xa_ref.xa = bf16[128,768]{1,0:T(8,128)(2,1)S(1)} collective-permute-done((bf16[128,768]{1,0:T(8,128)(2,1)S(1)}, bf16[128,768]{1,0:T(8,128)(2,1)S(1)}, u32[]{:S(2)}, u32[]{:S(2)}) %collective-permute-start.6) | collective-permute-done | bytes 196640 | tf_op jit(solution)/shard_map/ppermute | solution.py:457
  25.9 3.7 %collective-permute-start.8 = (bf16[128,768]{1,0:T(8,128)(2,1)S(1)}, bf16[128,768]{1,0:T(8,128)(2,1)S(1)}, u32[]{:S(2)}, u32[]{:S(2)}) collective-permute-start(bf16[128,768]{1,0:T(8,128)(2,1)S(1)} %get-tuple-element.78), channel_id=1, source_target_pairs={{0,16},{1,2},{2,1},{3,4},{4,3},{5,6},{6,5},{7,23},{8,24},{9,10},{1... | collective-permute-start | bytes 589832 | tf_op jit(solution)/shard_map/ppermute | solution.py:447
  29.6 4.1 %collective-permute-start.9 = (bf16[128,768]{1,0:T(8,128)(2,1)S(1)}, bf16[128,768]{1,0:T(8,128)(2,1)S(1)}, u32[]{:S(2)}, u32[]{:S(2)}) collective-permute-start(bf16[128,768]{1,0:T(8,128)(2,1)S(1)} %get-tuple-element.78), channel_id=1, source_target_pairs={{0,1},{1,0},{2,3},{3,2},{4,5},{5,4},{6,7},{7,6},{8,9},{9,8},{10,11... | collective-permute-start | bytes 589832 | tf_op jit(solution)/shard_map/ppermute | solution.py:430
  33.9 2.1 %collective-permute-done.8.refs_0_.xfa = bf16[128,768]{1,0:T(8,128)(2,1)S(1)} collective-permute-done((bf16[128,768]{1,0:T(8,128)(2,1)S(1)}, bf16[128,768]{1,0:T(8,128)(2,1)S(1)}, u32[]{:S(2)}, u32[]{:S(2)}) %collective-permute-start.8) | collective-permute-done | bytes 196640 | tf_op jit(solution)/shard_map/ppermute | solution.py:447
  36.0 3.1 %collective-permute-done.12.xb = bf16[128,768]{1,0:T(8,128)(2,1)S(1)} collective-permute-done((bf16[128,768]{1,0:T(8,128)(2,1)S(1)}, bf16[128,768]{1,0:T(8,128)(2,1)S(1)}, u32[]{:S(2)}, u32[]{:S(2)}) %collective-permute-start.12) | collective-permute-done | bytes 196640 | tf_op jit(solution)/shard_map/ppermute | solution.py:447
  39.1 3.6 %collective-permute-start.14 = (bf16[128,768]{1,0:T(8,128)(2,1)S(1)}, bf16[128,768]{1,0:T(8,128)(2,1)S(1)}, u32[]{:S(2)}, u32[]{:S(2)}) collective-permute-start(bf16[128,768]{1,0:T(8,128)(2,1)S(1)} %get-tuple-element.87.refs_2_), channel_id=1, source_target_pairs={{0,24},{1,25},{2,26},{3,27},{4,28},{5,29},{6,30},{7,31},{8,16},{9,... | collective-permute-start | bytes 589832 | tf_op jit(solution)/shard_map/ppermute | solution.py:457
  42.7 4.9 %collective-permute-done.14.xa_ref.xa = bf16[128,768]{1,0:T(8,128)(2,1)S(1)} collective-permute-done((bf16[128,768]{1,0:T(8,128)(2,1)S(1)}, bf16[128,768]{1,0:T(8,128)(2,1)S(1)}, u32[]{:S(2)}, u32[]{:S(2)}) %collective-permute-start.14) | collective-permute-done | bytes 196640 | tf_op jit(solution)/shard_map/ppermute | solution.py:457
  47.6 1.8 %collective-permute-start.15 = (bf16[128,768]{1,0:T(8,128)(2,1)S(1)}, bf16[128,768]{1,0:T(8,128)(2,1)S(1)}, u32[]{:S(2)}, u32[]{:S(2)}) collective-permute-start(bf16[128,768]{1,0:T(8,128)(2,1)S(1)} %get-tuple-element.88), channel_id=1, source_target_pairs={{0,16},{1,2},{2,1},{3,4},{4,3},{5,6},{6,5},{7,23},{8,24},{9,10},{1... | collective-permute-start | bytes 589832 | tf_op jit(solution)/shard_map/ppermute | solution.py:447
  49.4 3.2 %collective-permute-start.16 = (bf16[128,768]{1,0:T(8,128)(2,1)S(1)}, bf16[128,768]{1,0:T(8,128)(2,1)S(1)}, u32[]{:S(2)}, u32[]{:S(2)}) collective-permute-start(bf16[128,768]{1,0:T(8,128)(2,1)S(1)} %get-tuple-element.88), channel_id=1, source_target_pairs={{0,1},{1,0},{2,3},{3,2},{4,5},{5,4},{6,7},{7,6},{8,9},{9,8},{10,11... | collective-permute-start | bytes 589832 | tf_op jit(solution)/shard_map/ppermute | solution.py:430
  54.0 4.1 %collective-permute-done.19.xb = bf16[128,768]{1,0:T(8,128)(2,1)S(1)} collective-permute-done((bf16[128,768]{1,0:T(8,128)(2,1)S(1)}, bf16[128,768]{1,0:T(8,128)(2,1)S(1)}, u32[]{:S(2)}, u32[]{:S(2)}) %collective-permute-start.19) | collective-permute-done | bytes 196640 | tf_op jit(solution)/shard_map/ppermute | solution.py:447
  58.2 3.4 %collective-permute-start.20 = (bf16[128,768]{1,0:T(8,128)(2,1)S(1)}, bf16[128,768]{1,0:T(8,128)(2,1)S(1)}, u32[]{:S(2)}, u32[]{:S(2)}) collective-permute-start(bf16[128,768]{1,0:T(8,128)(2,1)S(1)} %get-tuple-element.99.refs_4_), channel_id=1, source_target_pairs={{0,8},{1,9},{2,10},{3,11},{4,12},{5,13},{6,14},{7,15},{8,0},{9,1},... | collective-permute-start | bytes 589832 | tf_op jit(solution)/shard_map/ppermute | solution.py:457
  62.7 3.8 %collective-permute-done.20.xa_ref.xa = bf16[128,768]{1,0:T(8,128)(2,1)S(1)} collective-permute-done((bf16[128,768]{1,0:T(8,128)(2,1)S(1)}, bf16[128,768]{1,0:T(8,128)(2,1)S(1)}, u32[]{:S(2)}, u32[]{:S(2)}) %collective-permute-start.20) | collective-permute-done | bytes 196640 | tf_op jit(solution)/shard_map/ppermute | solution.py:457
  67.0 1.9 %collective-permute-start.21 = (bf16[128,768]{1,0:T(8,128)(2,1)S(1)}, bf16[128,768]{1,0:T(8,128)(2,1)S(1)}, u32[]{:S(2)}, u32[]{:S(2)}) collective-permute-start(bf16[128,768]{1,0:T(8,128)(2,1)S(1)} %get-tuple-element.100), channel_id=1, source_target_pairs={{0,16},{1,2},{2,1},{3,4},{4,3},{5,6},{6,5},{7,23},{8,24},{9,10},{1... | collective-permute-start | bytes 589832 | tf_op jit(solution)/shard_map/ppermute | solution.py:447
  69.4 1.3 %collective-permute-done.23.xb.own_x = bf16[128,768]{1,0:T(8,128)(2,1)S(1)} collective-permute-done((bf16[128,768]{1,0:T(8,128)(2,1)S(1)}, bf16[128,768]{1,0:T(8,128)(2,1)S(1)}, u32[]{:S(2)}, u32[]{:S(2)}) %collective-permute-start.23) | collective-permute-done | bytes 196640 | tf_op jit(solution)/shard_map/ppermute | solution.py:457
  72.6 2.4 %own.5 = (bf16[128,1536]{1,0:T(8,128)(2,1)S(1)}, f32[128,1536]{1,0:T(8,128)S(1)}, f32[128,1536]{1,0:T(8,128)S(1)}, f32[128,768]{1,0:T(8,128)S(1)}) custom-call(f32[128,1536]{1,0:T(8,128)S(1)} %get-tuple-element.104.acc, bf16[128,768]{1,0:T(8,128)(2,1)S(1)} %collective-permute-done.20.xa_ref.xa, bf16[128,768]{1,0:T(8,128)(2,1)S(1)} %collective-permute-done.23.xb.own_x, ...), custom_call_target="tpu_custom_call" | custom-call | tf_op jit(solution)/shard_map/own/pallas_call | solution.py:596
  75.0 1.6 %near.5 = (f32[128,1536]{1,0:T(8,128)S(1)}, f32[128,1536]{1,0:T(8,128)S(1)}, f32[128,1536]{1,0:T(8,128)S(1)}) custom-call(bf16[128,768]{1,0:T(8,128)(2,1)S(1)} %collective-permute-done.21.refs_0_.xfa, bf16[128,768]{1,0:T(8,128)(2,1)S(1)} %collective-permute-done.22.refs_1_.xa, bf16[128,768]{1,0:T(8,128)(2,1)S(1)} %collective-permute-done.24.xb, ...), custom_call_target="tpu_custom_call" | custom-call | tf_op jit(solution)/shard_map/near/pallas_call | solution.py:608
  76.9 1.7 %far.5 = (bf16[128,768]{1,0:T(8,128)(2,1)S(1)}, bf16[128,1536]{1,0:T(8,128)(2,1)S(1)}, bf16[128,1536]{1,0:T(8,128)(2,1)S(1)}) custom-call(f32[128,1536]{1,0:T(8,128)S(1)} %get-tuple-element.107.acc, bf16[128,768]{1,0:T(8,128)(2,1)S(1)} %collective-permute-done.25.xb, bf16[1536,1536]{1,0:T(8,128)(2,1)S(1)} %get-tuple-element.76.wot, ...), custom_call_target="tpu_custom_call" | custom-call | tf_op jit(solution)/shard_map/far/pallas_call | solution.py:615
  78.6 1.9 %finish.1 = bf16[128,1536]{1,0:T(8,128)(2,1)} custom-call(bf16[128,1536]{1,0:T(8,128)(2,1)S(1)} %get-tuple-element.111.dk, bf16[128,1536]{1,0:T(8,128)(2,1)S(1)} %get-tuple-element.112.dv, bf16[128,1536]{1,0:T(8,128)(2,1)S(1)} %get-tuple-element.113.dq, bf16[128,768]{1,0:T(8,128)(2,1)S(1)} %collective-permute-done.23.xb.own_x, ...), custom_call_target="tpu_custom_call" | custom-call | tf_op jit(solution)/shard_map/finish/pallas_call | solution.py:628
  (58 shorter events, 10.3 us)
Async XLA Ops:
  0.0 10.9 %collective-permute-start = (bf16[128,1536]{1,0:T(8,128)(2,1)}, bf16[128,1536]{1,0:T(8,128)(2,1)S(1)}, u32[]{:S(2)}, u32[]{:S(2)}) collective-permute-start(bf16[128,1536]{1,0:T(8,128)(2,1)} %bitcast.14), channel_id=1, source_target_pairs={{0,1},{1,0},{2,3},{3,2},{4,5},{5,4},{6,7},{7,6},{8,9},{9,8},{10,11... | collective-permute-start | bytes 1179656 | tf_op jit(solution)/shard_map/ppermute | solution.py:430
  0.1 10.8 %collective-permute-start.1 = (bf16[128,1536]{1,0:T(8,128)(2,1)}, bf16[128,1536]{1,0:T(8,128)(2,1)S(1)}, u32[]{:S(2)}, u32[]{:S(2)}) collective-permute-start(bf16[128,1536]{1,0:T(8,128)(2,1)} %bitcast.15), channel_id=1, source_target_pairs={{0,16},{1,2},{2,1},{3,4},{4,3},{5,6},{6,5},{7,23},{8,24},{9,10},{1... | collective-permute-start | bytes 1179656 | tf_op jit(solution)/shard_map/ppermute | solution.py:447
  2.7 10.1 %collective-permute-start.3 = (bf16[128,1536]{1,0:T(8,128)(2,1)}, bf16[128,1536]{1,0:T(8,128)(2,1)S(1)}, u32[]{:S(2)}, u32[]{:S(2)}) collective-permute-start(bf16[128,1536]{1,0:T(8,128)(2,1)} %bitcast.17), channel_id=1, source_target_pairs={{0,16},{1,2},{2,1},{3,4},{4,3},{5,6},{6,5},{7,23},{8,24},{9,10},{1... | collective-permute-start | bytes 1179656 | tf_op jit(solution)/shard_map/ppermute | solution.py:447
  10.5 2.4 %collective-permute-start.2 = (bf16[128,1536]{1,0:T(8,128)(2,1)S(1)}, bf16[128,1536]{1,0:T(8,128)(2,1)S(1)}, u32[]{:S(2)}, u32[]{:S(2)}) collective-permute-start(bf16[128,1536]{1,0:T(8,128)(2,1)S(1)} %get-tuple-element.66.v0.v), channel_id=1, source_target_pairs={{0,1},{1,0},{2,3},{3,2},{4,5},{5,4},{6,7},{7,6},{8,9},{9,8},{10,11... | collective-permute-start | bytes 1179656 | tf_op jit(solution)/shard_map/ppermute | solution.py:430
  12.9 7.6 %collective-permute-start.5 = (bf16[128,1536]{1,0:T(8,128)(2,1)S(1)}, bf16[128,1536]{1,0:T(8,128)(2,1)S(1)}, u32[]{:S(2)}, u32[]{:S(2)}) collective-permute-start(bf16[128,1536]{1,0:T(8,128)(2,1)S(1)} %get-tuple-element.74), channel_id=1, source_target_pairs={{0,16},{1,2},{2,1},{3,4},{4,3},{5,6},{6,5},{7,23},{8,24},{9,10},{1... | collective-permute-start | bytes 1179656 | tf_op jit(solution)/shard_map/ppermute | solution.py:447
  15.0 7.9 %collective-permute-start.7 = (bf16[6,384,256]{2,1,0:T(8,128)(2,1)S(1)}, bf16[6,384,256]{2,1,0:T(8,128)(2,1)S(1)}, u32[]{:S(2)}, u32[]{:S(2)}) collective-permute-start(bf16[6,384,256]{2,1,0:T(8,128)(2,1)S(1)} %get-tuple-element.77), channel_id=1, source_target_pairs={{0,1},{1,0},{2,3},{3,2},{4,5},{5,4},{6,7},{7,6},{8,9},{9,8},{10,11... | collective-permute-start | bytes 3538952 | tf_op jit(solution)/shard_map/ppermute | solution.py:430
  16.0 4.5 %collective-permute-start.4 = (bf16[128,1536]{1,0:T(8,128)(2,1)S(1)}, bf16[128,1536]{1,0:T(8,128)(2,1)S(1)}, u32[]{:S(2)}, u32[]{:S(2)}) collective-permute-start(bf16[128,1536]{1,0:T(8,128)(2,1)S(1)} %first_near.1.after), channel_id=1, source_target_pairs={{0,1},{1,0},{2,3},{3,2},{4,5},{5,4},{6,7},{7,6},{8,9},{9,8},{10,11... | collective-permute-start | bytes 1179656 | tf_op jit(solution)/shard_map/ppermute | solution.py:430
  16.1 17.7 %collective-permute-start.13 = (bf16[6,384,256]{2,1,0:T(8,128)(2,1)S(1)}, bf16[6,384,256]{2,1,0:T(8,128)(2,1)S(1)}, u32[]{:S(2)}, u32[]{:S(2)}) collective-permute-start(bf16[6,384,256]{2,1,0:T(8,128)(2,1)S(1)} %get-tuple-element.73.after), channel_id=1, source_target_pairs={{1,2},{3,4},{5,6},{2,1},{4,3},{6,5},{9,10},{11,12},{13,14},{10,9},... | collective-permute-start | bytes 3538952 | tf_op jit(solution)/shard_map/ppermute | solution.py:451
  20.6 5.3 %collective-permute-start.6 = (bf16[128,768]{1,0:T(8,128)(2,1)S(1)}, bf16[128,768]{1,0:T(8,128)(2,1)S(1)}, u32[]{:S(2)}, u32[]{:S(2)}) collective-permute-start(bf16[128,768]{1,0:T(8,128)(2,1)S(1)} %get-tuple-element.75.refs_0_), channel_id=1, source_target_pairs={{0,8},{1,9},{2,10},{3,11},{4,12},{5,13},{6,14},{7,15},{8,0},{9,1},... | collective-permute-start | bytes 589832 | tf_op jit(solution)/shard_map/ppermute | solution.py:457
  22.8 10.9 %collective-permute-start.10 = (bf16[128,768]{1,0:T(8,128)(2,1)S(1)}, bf16[128,768]{1,0:T(8,128)(2,1)S(1)}, u32[]{:S(2)}, u32[]{:S(2)}) collective-permute-start(bf16[128,768]{1,0:T(8,128)(2,1)S(1)} %get-tuple-element.79.refs_1_), channel_id=1, source_target_pairs={{0,8},{1,9},{2,10},{3,11},{4,12},{5,13},{6,14},{7,15},{8,0},{9,1},... | collective-permute-start | bytes 589832 | tf_op jit(solution)/shard_map/ppermute | solution.py:457
  25.9 10.1 %collective-permute-start.8 = (bf16[128,768]{1,0:T(8,128)(2,1)S(1)}, bf16[128,768]{1,0:T(8,128)(2,1)S(1)}, u32[]{:S(2)}, u32[]{:S(2)}) collective-permute-start(bf16[128,768]{1,0:T(8,128)(2,1)S(1)} %get-tuple-element.78), channel_id=1, source_target_pairs={{0,16},{1,2},{2,1},{3,4},{4,3},{5,6},{6,5},{7,23},{8,24},{9,10},{1... | collective-permute-start | bytes 589832 | tf_op jit(solution)/shard_map/ppermute | solution.py:447
  29.6 6.3 %collective-permute-start.9 = (bf16[128,768]{1,0:T(8,128)(2,1)S(1)}, bf16[128,768]{1,0:T(8,128)(2,1)S(1)}, u32[]{:S(2)}, u32[]{:S(2)}) collective-permute-start(bf16[128,768]{1,0:T(8,128)(2,1)S(1)} %get-tuple-element.78), channel_id=1, source_target_pairs={{0,1},{1,0},{2,3},{3,2},{4,5},{5,4},{6,7},{7,6},{8,9},{9,8},{10,11... | collective-permute-start | bytes 589832 | tf_op jit(solution)/shard_map/ppermute | solution.py:430
  33.7 5.4 %collective-permute-start.12 = (bf16[128,768]{1,0:T(8,128)(2,1)S(1)}, bf16[128,768]{1,0:T(8,128)(2,1)S(1)}, u32[]{:S(2)}, u32[]{:S(2)}) collective-permute-start(bf16[128,768]{1,0:T(8,128)(2,1)S(1)} %collective-permute-done.10.xb.own_x), channel_id=1, source_target_pairs={{0,16},{1,2},{2,1},{3,4},{4,3},{5,6},{6,5},{7,23},{8,24},{9,10},{1... | collective-permute-start | bytes 589832 | tf_op jit(solution)/shard_map/ppermute | solution.py:447
  39.1 8.5 %collective-permute-start.14 = (bf16[128,768]{1,0:T(8,128)(2,1)S(1)}, bf16[128,768]{1,0:T(8,128)(2,1)S(1)}, u32[]{:S(2)}, u32[]{:S(2)}) collective-permute-start(bf16[128,768]{1,0:T(8,128)(2,1)S(1)} %get-tuple-element.87.refs_2_), channel_id=1, source_target_pairs={{0,24},{1,25},{2,26},{3,27},{4,28},{5,29},{6,30},{7,31},{8,16},{9,... | collective-permute-start | bytes 589832 | tf_op jit(solution)/shard_map/ppermute | solution.py:457
  42.7 9.9 %collective-permute-start.17 = (bf16[128,768]{1,0:T(8,128)(2,1)S(1)}, bf16[128,768]{1,0:T(8,128)(2,1)S(1)}, u32[]{:S(2)}, u32[]{:S(2)}) collective-permute-start(bf16[128,768]{1,0:T(8,128)(2,1)S(1)} %rest.2.refs_3_), channel_id=1, source_target_pairs={{0,24},{1,25},{2,26},{3,27},{4,28},{5,29},{6,30},{7,31},{8,16},{9,... | collective-permute-start | bytes 589832 | tf_op jit(solution)/shard_map/ppermute | solution.py:457
  47.6 5.8 %collective-permute-start.15 = (bf16[128,768]{1,0:T(8,128)(2,1)S(1)}, bf16[128,768]{1,0:T(8,128)(2,1)S(1)}, u32[]{:S(2)}, u32[]{:S(2)}) collective-permute-start(bf16[128,768]{1,0:T(8,128)(2,1)S(1)} %get-tuple-element.88), channel_id=1, source_target_pairs={{0,16},{1,2},{2,1},{3,4},{4,3},{5,6},{6,5},{7,23},{8,24},{9,10},{1... | collective-permute-start | bytes 589832 | tf_op jit(solution)/shard_map/ppermute | solution.py:447
  49.4 4.2 %collective-permute-start.16 = (bf16[128,768]{1,0:T(8,128)(2,1)S(1)}, bf16[128,768]{1,0:T(8,128)(2,1)S(1)}, u32[]{:S(2)}, u32[]{:S(2)}) collective-permute-start(bf16[128,768]{1,0:T(8,128)(2,1)S(1)} %get-tuple-element.88), channel_id=1, source_target_pairs={{0,1},{1,0},{2,3},{3,2},{4,5},{5,4},{6,7},{7,6},{8,9},{9,8},{10,11... | collective-permute-start | bytes 589832 | tf_op jit(solution)/shard_map/ppermute | solution.py:430
  52.8 5.4 %collective-permute-start.19 = (bf16[128,768]{1,0:T(8,128)(2,1)S(1)}, bf16[128,768]{1,0:T(8,128)(2,1)S(1)}, u32[]{:S(2)}, u32[]{:S(2)}) collective-permute-start(bf16[128,768]{1,0:T(8,128)(2,1)S(1)} %collective-permute-done.17.xb.own_x), channel_id=1, source_target_pairs={{0,16},{1,2},{2,1},{3,4},{4,3},{5,6},{6,5},{7,23},{8,24},{9,10},{1... | collective-permute-start | bytes 589832 | tf_op jit(solution)/shard_map/ppermute | solution.py:447
  58.2 8.4 %collective-permute-start.20 = (bf16[128,768]{1,0:T(8,128)(2,1)S(1)}, bf16[128,768]{1,0:T(8,128)(2,1)S(1)}, u32[]{:S(2)}, u32[]{:S(2)}) collective-permute-start(bf16[128,768]{1,0:T(8,128)(2,1)S(1)} %get-tuple-element.99.refs_4_), channel_id=1, source_target_pairs={{0,8},{1,9},{2,10},{3,11},{4,12},{5,13},{6,14},{7,15},{8,0},{9,1},... | collective-permute-start | bytes 589832 | tf_op jit(solution)/shard_map/ppermute | solution.py:457
  61.6 9.2 %collective-permute-start.23 = (bf16[128,768]{1,0:T(8,128)(2,1)S(1)}, bf16[128,768]{1,0:T(8,128)(2,1)S(1)}, u32[]{:S(2)}, u32[]{:S(2)}) collective-permute-start(bf16[128,768]{1,0:T(8,128)(2,1)S(1)} %rest.3.refs_5_), channel_id=1, source_target_pairs={{0,8},{1,9},{2,10},{3,11},{4,12},{5,13},{6,14},{7,15},{8,0},{9,1},... | collective-permute-start | bytes 589832 | tf_op jit(solution)/shard_map/ppermute | solution.py:457
  67.0 8.0 %collective-permute-start.21 = (bf16[128,768]{1,0:T(8,128)(2,1)S(1)}, bf16[128,768]{1,0:T(8,128)(2,1)S(1)}, u32[]{:S(2)}, u32[]{:S(2)}) collective-permute-start(bf16[128,768]{1,0:T(8,128)(2,1)S(1)} %get-tuple-element.100), channel_id=1, source_target_pairs={{0,16},{1,2},{2,1},{3,4},{4,3},{5,6},{6,5},{7,23},{8,24},{9,10},{1... | collective-permute-start | bytes 589832 | tf_op jit(solution)/shard_map/ppermute | solution.py:447
  68.9 6.1 %collective-permute-start.22 = (bf16[128,768]{1,0:T(8,128)(2,1)S(1)}, bf16[128,768]{1,0:T(8,128)(2,1)S(1)}, u32[]{:S(2)}, u32[]{:S(2)}) collective-permute-start(bf16[128,768]{1,0:T(8,128)(2,1)S(1)} %get-tuple-element.100), channel_id=1, source_target_pairs={{0,1},{1,0},{2,3},{3,2},{4,5},{5,4},{6,7},{7,6},{8,9},{9,8},{10,11... | collective-permute-start | bytes 589832 | tf_op jit(solution)/shard_map/ppermute | solution.py:430
  70.7 4.3 %collective-permute-start.24 = (bf16[128,768]{1,0:T(8,128)(2,1)S(1)}, bf16[128,768]{1,0:T(8,128)(2,1)S(1)}, u32[]{:S(2)}, u32[]{:S(2)}) collective-permute-start(bf16[128,768]{1,0:T(8,128)(2,1)S(1)} %collective-permute-done.23.xb.own_x), channel_id=1, source_target_pairs={{0,1},{1,0},{2,3},{3,2},{4,5},{5,4},{6,7},{7,6},{8,9},{9,8},{10,11... | collective-permute-start | bytes 589832 | tf_op jit(solution)/shard_map/ppermute | solution.py:430
  71.6 5.3 %collective-permute-start.25 = (bf16[128,768]{1,0:T(8,128)(2,1)S(1)}, bf16[128,768]{1,0:T(8,128)(2,1)S(1)}, u32[]{:S(2)}, u32[]{:S(2)}) collective-permute-start(bf16[128,768]{1,0:T(8,128)(2,1)S(1)} %collective-permute-done.23.xb.own_x), channel_id=1, source_target_pairs={{0,16},{1,2},{2,1},{3,4},{4,3},{5,6},{6,5},{7,23},{8,24},{9,10},{1... | collective-permute-start | bytes 589832 | tf_op jit(solution)/shard_map/ppermute | solution.py:447
  (2 other events, 3.7 us)
